TPU v7x, 512 devices: a whole 4x4x16 slice. The times are simulated.
512 devices in a mesh: row: 32 (over y, x, core), col: 16 (over z).
Axes of the slice: x: 4, y: 4, z: 16, core: 2. Of those that a mesh axis runs over, the one named last changes fastest.
Arguments:
- covariance: float32 [8192, 8192], P('row', 'col'), may hold values from -4 to 60, as said below
- observations: float32 [64, 8192], P(None, 'row'), may hold values from -6 to 6
Outputs:
- factored: float32 [8192, 8192], P('row', 'col')
- solved: float32 [64, 8192], P(None, 'row')
- site_terms: float32 [64], replicated
Inputs may be any that keep to these rules, and one draw needn't show every extreme that they name: `covariance`: symmetric and positive definite.
All inputs are finite; a program needn't handle non-finite values.
Results may differ from a plain program's by a relative error of at most 0.0001.
Values sent between devices are 32-bit elements; how exact they have to be, the bound alone decides.
No kernel may reach another device: no remote copies, remote signals or barrier semaphores. Data moves between devices by JAX's collectives and lax.ppermute only.
A program may use at most 64 MiB of HBM per device.

v0:
```python
import jax
import jax.numpy as jnp
from jax import lax
from jax.sharding import PartitionSpec as P


def spread(value, axis, source):
    kept = jnp.where(lax.axis_index(axis) == source, value, 0).astype(value.dtype)
    return lax.psum(kept, axis)


def pack_pair(first_arr, second_arr):
    return jnp.concatenate([first_arr.reshape(-1), second_arr.reshape(-1)])


def split_pair(packed, first_shape, second_shape):
    first_len = first_shape[0] * first_shape[1]
    return (packed[:first_len].reshape(first_shape), packed[first_len:].reshape(second_shape))


def factor_block(diag_block, column_block, target_block, row_tile, first_tile, tile_count):
    chol_factor = jnp.linalg.cholesky(diag_block)
    below_rows = jax.scipy.linalg.solve_triangular(chol_factor, column_block.T, lower=True).T
    solved_obs = jax.scipy.linalg.solve_triangular(chol_factor, target_block.T, lower=True)
    beyond = row_tile >= first_tile + tile_count
    inside = row_tile >= first_tile
    factor_rows = jnp.where(
        beyond, below_rows, jnp.where(inside, chol_factor, jnp.zeros_like(below_rows))
    )
    return (chol_factor, factor_rows, solved_obs)


def advance_targets(targets, factor_rows, solved_obs, row_tile, first_tile, tile_count):
    reduced = targets - jnp.dot(factor_rows, solved_obs, precision=lax.Precision.HIGHEST).T
    own_rows = solved_obs.T
    beyond = row_tile >= first_tile + tile_count
    inside = row_tile >= first_tile
    return jnp.where(beyond, reduced, jnp.where(inside, own_rows, targets))


def apply_update(
    region, product, factor_rows, row_tile, col_tiles, col_start, first_tile, tile_count
):
    tile_width = factor_rows.shape[0]
    place_at = first_tile * tile_width - col_start
    placed = lax.dynamic_update_slice(jnp.zeros_like(region), factor_rows, (jnp.int32(0), place_at))
    trailing = col_tiles >= first_tile + tile_count
    panel_here = (col_tiles >= first_tile) & jnp.logical_not(trailing)
    row_beyond = row_tile >= first_tile + tile_count
    row_inside = row_tile >= first_tile
    updated = region - product
    trail_value = jnp.where(
        row_beyond, updated, jnp.where(row_inside, jnp.zeros_like(region), region)
    )
    return jnp.where(trailing[None, :], trail_value, jnp.where(panel_here[None, :], placed, region))


def section_totals(chol_factor, solved_obs):
    return (
        2.0 * jnp.sum(jnp.log(jnp.diagonal(chol_factor))),
        jnp.sum(solved_obs * solved_obs, axis=0),
    )


def shards(covariance, observations):
    tile_width = covariance.shape[0]
    local_cols = covariance.shape[1]
    tiles_here = local_cols // tile_width
    row_tile = lax.axis_index("row")
    col_index = lax.axis_index("col")
    col_start = col_index * local_cols
    col_tiles = (col_start + jnp.arange(local_cols, dtype=jnp.int32)) // tile_width
    matrix = covariance
    targets = observations
    target_shape = (observations.shape[0], tile_width)
    log_total = jnp.zeros((), jnp.float32)
    quadratic = jnp.zeros((observations.shape[0],), jnp.float32)
    source = matrix[:, 0:tile_width]
    for section in range(2):
        column_block = spread(source, "col", 0)
        packed = spread(pack_pair(column_block, targets), "row", section)
        diag_block, target_block = split_pair(packed, (tile_width, tile_width), target_shape)
        chol_factor, factor_rows, solved_obs = factor_block(
            diag_block, column_block, target_block, row_tile, section, 1
        )
        targets = advance_targets(targets, factor_rows, solved_obs, row_tile, section, 1)
        log_part, quad_part = section_totals(chol_factor, solved_obs)
        log_total = log_total + log_part
        quadratic = quadratic + quad_part
        copies = []
        for holder in range(tiles_here):
            copies.append(spread(factor_rows, "row", col_index * tiles_here + holder))
        ahead = section + 1
        product = jnp.dot(
            factor_rows, jnp.concatenate(copies, axis=0).T, precision=lax.Precision.HIGHEST
        )
        matrix = apply_update(
            matrix, product, factor_rows, row_tile, col_tiles, col_start, section, 1
        )
        if section == 0:
            source = matrix[:, ahead * tile_width : (ahead + 1) * tile_width]
    site_terms = -(quadratic + log_total) / (4.0 * tile_width)
    return (matrix, targets, site_terms)


def solution(mesh):
    in_specs = (P("row", "col"), P(None, "row"))
    out_specs = (P("row", "col"), P(None, "row"), P())
    return jax.shard_map(shards, mesh=mesh, in_specs=in_specs, out_specs=out_specs, check_vma=False)
```

profile of v0, /device:TPU:1, one launch (start us, length us, event | category | flops | bytes accessed | tf_op | source)
XLA Modules:
  0.0 967.2 jit_solution(398394385858111955)
XLA Ops:
  7.2 1.7 slice_select_fusion.1
  9.0 0.8 copy-done.3
  9.8 132.7 %all-reduce.10.cloned.1.call-done = f32[256,256]{1,0:T(8,128)} async-done(((f32[256,256]{1,0:T(8,128)}), f32[256,256]{1,0:T(8,128)}) %all-reduce.10.cloned.1.call-update) | async-done | bytes 262160 | tf_op jit(solution)/shard_map/psum | solution.py:9
  142.5 1.1 copy.19
  143.6 0.7 maximum_select_fusion
  144.4 141.1 %all-reduce.12.cloned.1.call-done = f32[81920]{0:T(1024)} async-done(((f32[81920]{0:T(1024)}), f32[81920]{0:T(1024)}) %all-reduce.12.cloned.1.call-update) | async-done | bytes 327696 | tf_op jit(solution)/shard_map/psum | solution.py:9
  285.5 0.9 slice-done
  286.8 11.7 %cholesky.130 = f32[128,128]{1,0:T(8,128)S(1)} custom-call(f32[128,128]{1,0:T(8,128)S(1)} %cholesky.194), custom_call_target="Cholesky" | custom-call | tf_op jit(solution)/shard_map/jit(cholesky)/cholesky | solution.py:22
  298.5 9.8 %custom-call.21 = f32[1,128,128]{1,2,0:T(8,128)S(1)} custom-call(f32[1,128,128]{2,1,0:T(8,128)S(1)} %get-tuple-element.81), custom_call_target="InvertDiagBlocksLowerTriangular" | custom-call | tf_op jit(solution)/shard_map/jit(cholesky)/cholesky | solution.py:22
  308.8 11.7 %cholesky.147 = f32[128,128]{1,0:T(8,128)S(1)} custom-call(f32[128,128]{1,0:T(8,128)S(1)} %convolution_subtract_fusion.5), custom_call_target="Cholesky" | custom-call | tf_op jit(solution)/shard_map/jit(cholesky)/cholesky | solution.py:22
  320.6 0.6 compare_reduce_fusion.2
  322.7 4.2 while.8
  322.9 0.6 fusion.71
  323.5 1.4 bitcast_dynamic-update-slice_fusion.4
  324.9 0.6 fusion.71
  325.5 1.4 bitcast_dynamic-update-slice_fusion.4
  326.9 19.7 %custom-call.22 = f32[2,128,128]{1,2,0:T(8,128)S(1)} custom-call(f32[2,128,128]{2,1,0:T(8,128)S(1)} %get-tuple-element.34), custom_call_target="InvertDiagBlocksLowerTriangular" | custom-call | tf_op jit(solution)/shard_map/jit(_solve_triangular)/triangular_solve | solution.py:23
  347.4 0.8 slice-done.1
  348.6 0.8 broadcast_select_fusion.3
  350.0 133.1 %all-reduce.20.cloned.1.call-done = (f32[256,256]{1,0:T(8,128)}, f32[256,256]{1,0:T(8,128)}) async-done(((f32[256,256]{1,0:T(8,128)}, f32[256,256]{1,0:T(8,128)}), (f32[256,256]{1,0:T(8,128)}, f32[256,256]{1,0:T(8,128)})) %all-reduce.20.cloned.1.call-update) | async-done | bytes 524304 | tf_op jit(solution)/shard_map/psum | solution.py:9
  483.1 1.8 fusion.3
  484.9 0.7 slice_select_fusion
  486.3 125.5 %all-reduce.14.cloned.1.call-done = f32[256,256]{1,0:T(8,128)} async-done(((f32[256,256]{1,0:T(8,128)}), f32[256,256]{1,0:T(8,128)}) %all-reduce.14.cloned.1.call-update) | async-done | bytes 262160 | tf_op jit(solution)/shard_map/psum | solution.py:9
  611.8 1.1 copy.21
  612.8 0.7 maximum_select_fusion.1
  613.7 2.3 gather_fusion
  616.2 0.6 log_reduce_fusion.1
  616.8 137.9 %all-reduce.16.cloned.1.call-done = f32[81920]{0:T(1024)} async-done(((f32[81920]{0:T(1024)}), f32[81920]{0:T(1024)}) %all-reduce.16.cloned.1.call-update) | async-done | bytes 327696 | tf_op jit(solution)/shard_map/psum | solution.py:9
  754.7 0.9 slice-done.2
  755.9 11.7 %cholesky.164 = f32[128,128]{1,0:T(8,128)S(1)} custom-call(f32[128,128]{1,0:T(8,128)S(1)} %cholesky.197), custom_call_target="Cholesky" | custom-call | tf_op jit(solution)/shard_map/jit(cholesky)/cholesky | solution.py:22
  767.7 9.8 %custom-call.24 = f32[1,128,128]{1,2,0:T(8,128)S(1)} custom-call(f32[1,128,128]{2,1,0:T(8,128)S(1)} %get-tuple-element.77), custom_call_target="InvertDiagBlocksLowerTriangular" | custom-call | tf_op jit(solution)/shard_map/jit(cholesky)/cholesky | solution.py:22
  778.0 11.7 %cholesky.181 = f32[128,128]{1,0:T(8,128)S(1)} custom-call(f32[128,128]{1,0:T(8,128)S(1)} %convolution_subtract_fusion.4), custom_call_target="Cholesky" | custom-call | tf_op jit(solution)/shard_map/jit(cholesky)/cholesky | solution.py:22
  789.7 0.6 compare_reduce_fusion
  790.4 0.6 compare_reduce_fusion.1
  792.4 4.0 while.9
  792.4 0.6 fusion.72
  793.0 1.4 bitcast_dynamic-update-slice_fusion.5
  794.4 0.6 fusion.72
  795.0 1.4 bitcast_dynamic-update-slice_fusion.5
  796.4 19.9 %custom-call.25 = f32[2,128,128]{1,2,0:T(8,128)S(1)} custom-call(f32[2,128,128]{2,1,0:T(8,128)S(1)} %get-tuple-element.36), custom_call_target="InvertDiagBlocksLowerTriangular" | custom-call | tf_op jit(solution)/shard_map/jit(_solve_triangular)/triangular_solve | solution.py:23
  817.1 2.3 gather_fusion.1
  819.5 0.6 log_reduce_fusion
  820.1 0.8 slice-done.3
  822.1 0.8 broadcast_select_fusion.1
  824.1 0.5 negate_multiply_fusion
  824.6 1.0 fusion.4
  825.6 132.1 %all-reduce.18.cloned.1.call-done = (f32[256,256]{1,0:T(8,128)}, f32[256,256]{1,0:T(8,128)}) async-done(((f32[256,256]{1,0:T(8,128)}, f32[256,256]{1,0:T(8,128)}), (f32[256,256]{1,0:T(8,128)}, f32[256,256]{1,0:T(8,128)})) %all-reduce.18.cloned.1.call-update) | async-done | bytes 524304 | tf_op jit(solution)/shard_map/psum | solution.py:9
  957.8 2.6 fusion.1
  (79 shorter events, 6.4 us)
Async XLA Ops:
  7.2 135.3 %all-reduce.10.cloned.1.call-start = ((), (), s32[]{:S(2)}) async-start(), calls=%async_computation | async-start | bytes 524288 | tf_op jit(solution)/shard_map/psum | solution.py:9
  8.9 0.8 copy-start.3
  8.9 276.6 %all-reduce.12.cloned.1.call-start = ((), (), s32[]{:S(2)}) async-start(), calls=%async_computation.1 | async-start | bytes 655360 | tf_op jit(solution)/shard_map/psum | solution.py:9
  144.3 338.8 %all-reduce.20.cloned.1.call-start = ((), (), s32[]{:S(2)}) async-start(), calls=%async_computation.5 | async-start | bytes 1048576 | tf_op jit(solution)/shard_map/psum | solution.py:9
  285.5 0.9 slice-start
  322.6 23.9 %copy-start.1 = (f32[256,256]{1,0:T(8,128)S(1)}, f32[256,256]{1,0:T(8,128)}, u32[]{:S(2)}) copy-start(f32[256,256]{1,0:T(8,128)} %all-reduce.10.cloned.1.call-done) | copy-start | bytes 786436
  347.4 0.8 slice-start.1
  349.4 133.6 %copy-start = (f32[256,512]{1,0:T(8,128)S(1)}, f32[256,512]{1,0:T(8,128)}, u32[]{:S(2)}) copy-start(f32[256,512]{1,0:T(8,128)} %param.7) | copy-start | bytes 1572868
  349.5 262.3 %all-reduce.14.cloned.1.call-start = ((), (), s32[]{:S(2)}) async-start(), calls=%async_computation.2 | async-start | bytes 524288 | tf_op jit(solution)/shard_map/psum | solution.py:9
  485.6 269.1 %all-reduce.16.cloned.1.call-start = ((), (), s32[]{:S(2)}) async-start(), calls=%async_computation.3 | async-start | bytes 655360 | tf_op jit(solution)/shard_map/psum | solution.py:9
  613.6 344.1 %all-reduce.18.cloned.1.call-start = ((), (), s32[]{:S(2)}) async-start(), calls=%async_computation.4 | async-start | bytes 1048576 | tf_op jit(solution)/shard_map/psum | solution.py:9
  754.7 0.9 slice-start.2
  792.3 23.9 %copy-start.2 = (f32[256,256]{1,0:T(8,128)S(1)}, f32[256,256]{1,0:T(8,128)}, u32[]{:S(2)}) copy-start(f32[256,256]{1,0:T(8,128)} %all-reduce.14.cloned.1.call-done) | copy-start | bytes 786436
  820.1 0.8 slice-start.3
Sparse Core Ops, SparseCore 0:
  10.9 131.5 all-reduce.9
  146.7 138.8 all-reduce.11
  349.6 133.4 all-reduce.19
  485.8 125.8 all-reduce.13
  615.8 138.8 all-reduce.15
  824.2 133.4 all-reduce.17
where the time goes:
time: 968 us; the launch traced here: 967 us
  waiting for transfers between devices  803 us (83%)
  other arithmetic  116 us (12%)
  local copies, waits for them, and re-layouts  20 us (2%)
  between operations  18.4 us (2%)
  matrix products  9.83 us (1%)
    psum x6, waiting for transfers between devices, spread(): return lax.psum(kept, axis)  802 us
    another operation x13, other arithmetic, factor_block(): chol_factor = jnp.linalg.cholesky(diag_block)  68.5 us
    another operation x5, other arithmetic, factor_block(): jax.scipy.linalg.solve_triangular(chol_factor, column_block.T, lower=True)  39.6 us
  transfers between devices with their start and end apart: 6, of which 6 were waited for; matrix products, arithmetic and copies ran while one was open for 1% of the time, Pallas kernels for 0%

commit v1 on v0

v1 whole, which is shorter than its diff:
```python
import jax
import jax.numpy as jnp
from jax import lax
from jax.sharding import PartitionSpec as P

HI = lax.Precision.HIGHEST


def dot(a, b):
    return jnp.dot(a, b, precision=HI)


def tree_step(value, hop, extent, position):
    pairs = [(z, z + hop) for z in range(0, extent, 2 * hop)]
    moved = lax.ppermute(value, "col", pairs)
    return jnp.where(position % (2 * hop) == hop, moved, value)


def factor(block):
    chol = jnp.linalg.cholesky(block)
    inv = jax.scipy.linalg.solve_triangular(
        chol, jnp.eye(block.shape[0], dtype=block.dtype), lower=True
    )
    return chol, inv


def shards(covariance, observations):
    tile, wide = covariance.shape
    nrhs = observations.shape[0]
    rows = lax.axis_size("row")
    cols = lax.axis_size("col")
    row = lax.axis_index("row")
    col = lax.axis_index("col")
    part = tile // rows

    with jax.named_scope("scatter"):
        obs_parts = observations.reshape(rows, part // 2, -1)
        lanes = obs_parts.shape[2]
        obs_parts = jnp.pad(obs_parts, ((0, 0), (0, part - part // 2), (0, 0)))
        sent = jnp.concatenate([covariance.reshape(rows, part, wide), obs_parts], axis=2)
        got = lax.all_to_all(sent, "row", split_axis=0, concat_axis=0, tiled=True)
        first, second = got[0], got[1]

    with jax.named_scope("columns"):
        col_piece = jnp.concatenate([first[:, :wide], second[:, :wide]], axis=0)
        col_all = lax.all_gather(col_piece, "row", axis=0, tiled=False)
        col0 = col_all[:, :part].reshape(tile, wide)
        col1 = col_all[:, part:].reshape(tile, wide)

    hops = []
    hop = cols // 2
    while hop >= 1:
        hops.append(hop)
        hop //= 2

    with jax.named_scope("diag"):
        diag_piece = jnp.concatenate([first[:, :tile], second[:, :wide]], axis=1)
        for hop in hops:
            diag_piece = tree_step(diag_piece, hop, cols, col)
        obs_piece = jnp.concatenate([first[: part // 2, wide:], second[: part // 2, wide:]], axis=0)
        piece = jnp.concatenate([diag_piece, obs_piece], axis=1)
        spread = jnp.broadcast_to(piece[None], (rows,) + piece.shape)
        whole = lax.all_to_all(spread, "row", split_axis=0, concat_axis=0, tiled=True)
        diag00 = whole[:, :, :tile].reshape(tile, tile)
        diag10 = whole[:, :, tile : 2 * tile].reshape(tile, tile)
        diag11 = whole[:, :, 2 * tile : 3 * tile].reshape(tile, tile)
        obs0 = whole[:, : part // 2, 3 * tile :].reshape(nrhs, tile)
        obs1 = whole[:, part // 2 :, 3 * tile :].reshape(nrhs, tile)

    with jax.named_scope("rowpanel"):
        panel = covariance
        for hop in hops:
            panel = tree_step(panel, hop, cols, col)
        row0, row1 = panel[:, :tile], panel[:, tile:]

    chol0, inv0 = factor(diag00)
    low = dot(diag10, inv0.T)
    chol1, inv1 = factor(diag11 - dot(low, low.T))

    with jax.named_scope("solve"):
        x0 = dot(row0, inv0.T)
        x1 = dot(row1 - dot(x0, low.T), inv1.T)
        y0 = dot(inv0, col0)
        y1 = dot(inv1, col1 - dot(low, y0))
        z0 = dot(obs0, inv0.T)
        z1 = dot(obs1 - dot(z0, low.T), inv1.T)

    with jax.named_scope("update"):
        trail = covariance - dot(x0, y0) - dot(x1, y1)
        is0, is1 = row == 0, row == 1
        left = jnp.where(is0, chol0, jnp.where(is1, low, x0))
        right = jnp.where(is0, 0.0, jnp.where(is1, chol1, x1))
        other = jnp.where(row <= 1, 0.0, trail)
        factored = jnp.where(col == 0, jnp.concatenate([left, right], axis=1), other)
        reduced = observations - dot(z0, x0.T) - dot(z1, x1.T)
        solved = jnp.where(is0, z0, jnp.where(is1, z1, reduced))

    with jax.named_scope("terms"):
        logdet = 2.0 * (jnp.sum(jnp.log(jnp.diagonal(chol0))) + jnp.sum(jnp.log(jnp.diagonal(chol1))))
        quad = jnp.sum(z0 * z0, axis=1) + jnp.sum(z1 * z1, axis=1)
        site_terms = -(quad + logdet) / (4.0 * tile)
    return factored, solved, site_terms


def solution(mesh):
    in_specs = (P("row", "col"), P(None, "row"))
    out_specs = (P("row", "col"), P(None, "row"), P())
    return jax.shard_map(shards, mesh=mesh, in_specs=in_specs, out_specs=out_specs, check_vma=False)
```

time: 968 us -> 256 us (0.26)
  waiting for transfers between devices: 803 us -> 19.5 us
  starting transfers between devices: 0.25 us -> 60.1 us
    psum x6 -> x0, waiting for transfers between devices: 802 us -> none  [spread(): return lax.psum(kept, axis)]
    ppermute x0 -> x8, starting transfers between devices: none -> 41.7 us  [tree_step(): moved = lax.ppermute(value, 'col', pairs)]
    ppermute x0 -> x8, waiting for transfers between devices: none -> 19.1 us  [tree_step(): moved = lax.ppermute(value, 'col', pairs)]
    all_to_all x0 -> x2, starting transfers between devices: none -> 18.4 us  [the longest x1 10.6 us: shards(): got = lax.all_to_all(sent, 'row', split_axis=0, concat_axis=0, tiled=True)]
  transfers between devices with their start and end apart: 6 -> 11, of which waited for: 6 -> 5; matrix products, arithmetic and copies ran while one was open for 1% -> 56% of each run, Pallas kernels for 0% -> 0%
where the time goes in v1:
time: 256 us; the launch traced here: 251 us
  other arithmetic  115 us (45%)
  starting transfers between devices  60.1 us (23%)
  local copies, waits for them, and re-layouts  23.5 us (9%)
  waiting for transfers between devices  19.5 us (8%)
  between operations  19 us (7%)
  matrix products  14.5 us (6%)
    another operation x13, other arithmetic, factor(): chol = jnp.linalg.cholesky(block)  68.7 us
    ppermute x8, starting transfers between devices, tree_step(): moved = lax.ppermute(value, 'col', pairs)  41.7 us
    another operation x5, other arithmetic, factor(): jax.scipy.linalg.solve_triangular(chol, jnp.eye(block.shape[0], dtype=blo...  40.6 us
    ppermute x8, waiting for transfers between devices, tree_step(): moved = lax.ppermute(value, 'col', pairs)  19.1 us
    all_to_all x1, starting transfers between devices, shards(): got = lax.all_to_all(sent, 'row', split_axis=0, concat_axis=0, tiled=True)  10.6 us
    dot_general x15, matrix products, dot(): return jnp.dot(a, b, precision=HI)  9.87 us
    another operation x15, local copies, waits for them, and re-layouts, factor(): jax.scipy.linalg.solve_triangular(chol, jnp.eye(block.shape[0], dtype=blo...  7.99 us
    all_to_all x1, starting transfers between devices, shards(): lax.all_to_all(spread, 'row', split_axis=0, concat_axis=0, tiled=True)  7.79 us
  transfers between devices with their start and end apart: 11, of which 5 were waited for; matrix products, arithmetic and copies ran while one was open for 56% of the time, Pallas kernels for 0%

profile of v1, /device:TPU:1, one launch (start us, length us, event | category | flops | bytes accessed | tf_op | source)
XLA Modules:
  0.0 251.5 jit_solution(2971150187470025305)
XLA Ops:
  7.2 0.9 reshape.50
  8.0 1.9 select_maximum_fusion
  10.0 10.6 %all-to-all-start = ((f32[32,8,640]{2,1,0:T(8,128)}), f32[32,8,640]{2,1,0:T(8,128)S(1)}, u32[]{:S(2)}, u32[]{:S(2)}) async-start(f32[32,8,640]{2,1,0:T(8,128)} %select_maximum_fusion), calls=%async_computation | async-start | bytes 1310720 | tf_op jit(solution)/shard_map/scatter/all_to_all | solution.py:41
  20.6 13.6 %collective-permute-start.4 = (f32[256,512]{1,0:T(8,128)S(1)}, f32[256,512]{1,0:T(8,128)S(1)}, u32[]{:S(2)}, u32[]{:S(2)}) collective-permute-start(f32[256,512]{1,0:T(8,128)S(1)} %copy-done), channel_id=1, source_target_pairs={{0,8},{16,24},{32,40},{48,56},{64,72},{80,88},{96,104},{112,120},{... | collective-permute-start | bytes 1572872 | tf_op jit(solution)/shard_map/rowpanel/ppermute | solution.py:15
  34.3 12.8 %collective-permute-start = (f32[8,768]{1,0:T(8,128)S(1)}, f32[8,768]{1,0:T(8,128)S(1)}, u32[]{:S(2)}, u32[]{:S(2)}) collective-permute-start(f32[8,768]{1,0:T(8,128)S(1)} %pad_maximum_fusion.10), channel_id=1, source_target_pairs={{0,8},{16,24},{32,40},{48,56},{64,72},{80,88},{96,104},{112,120},{... | collective-permute-start | bytes 73736 | tf_op jit(solution)/shard_map/diag/ppermute | solution.py:15
  47.1 0.9 collective-permute-done
  48.0 1.3 collective-permute-start.1
  49.4 0.9 collective-permute-done.1
  50.3 1.3 collective-permute-start.2
  51.6 7.6 %collective-permute-start.5 = (f32[256,512]{1,0:T(8,128)S(1)}, f32[256,512]{1,0:T(8,128)S(1)}, u32[]{:S(2)}, u32[]{:S(2)}) collective-permute-start(f32[256,512]{1,0:T(8,128)S(1)} %broadcast_select_fusion), channel_id=1, source_target_pairs={{0,4},{8,12},{16,20},{24,28},{32,36},{40,44},{48,52},{56,60},{64,6... | collective-permute-start | bytes 1572872 | tf_op jit(solution)/shard_map/rowpanel/ppermute | solution.py:15
  59.3 1.3 collective-permute-start.3
  60.6 8.1 %collective-permute-done.3 = f32[8,768]{1,0:T(8,128)S(1)} collective-permute-done((f32[8,768]{1,0:T(8,128)S(1)}, f32[8,768]{1,0:T(8,128)S(1)}, u32[]{:S(2)}, u32[]{:S(2)}) %collective-permute-start.3) | collective-permute-done | bytes 24608 | tf_op jit(solution)/shard_map/diag/ppermute | solution.py:15
  68.7 1.1 broadcast_in_dim.21
  69.7 7.8 %all-to-all-start.1 = ((f32[32,8,896]{2,1,0:T(8,128)}), f32[32,8,896]{2,1,0:T(8,128)S(1)}, u32[]{:S(2)}, u32[]{:S(2)}) async-start(f32[32,8,896]{2,1,0:T(8,128)} %broadcast_in_dim.21), calls=%async_computation.1 | async-start | bytes 1835008 | tf_op jit(solution)/shard_map/diag/all_to_all | solution.py:63
  77.7 1.3 collective-permute-start.6
  79.1 0.7 copy-done.12
  79.8 0.7 copy-done.9
  81.1 9.2 %collective-permute-done.6 = f32[256,512]{1,0:T(8,128)S(1)} collective-permute-done((f32[256,512]{1,0:T(8,128)S(1)}, f32[256,512]{1,0:T(8,128)S(1)}, u32[]{:S(2)}, u32[]{:S(2)}) %collective-permute-start.6) | collective-permute-done | bytes 524320 | tf_op jit(solution)/shard_map/rowpanel/ppermute | solution.py:15
  90.4 2.5 %collective-permute-start.7 = (f32[256,512]{1,0:T(8,128)S(1)}, f32[256,512]{1,0:T(8,128)}, u32[]{:S(2)}, u32[]{:S(2)}) collective-permute-start(f32[256,512]{1,0:T(8,128)S(1)} %broadcast_select_fusion.2), channel_id=1, source_target_pairs={{0,1},{2,3},{4,5},{6,7},{8,9},{10,11},{12,13},{14,15},{16,17},{18,... | collective-permute-start | bytes 1572872 | tf_op jit(solution)/shard_map/rowpanel/ppermute | solution.py:15
  93.5 11.7 %cholesky.130 = f32[128,128]{1,0:T(8,128)S(1)} custom-call(f32[128,128]{1,0:T(8,128)S(1)} %cholesky.194), custom_call_target="Cholesky" | custom-call | tf_op jit(solution)/shard_map/jit(cholesky)/cholesky | solution.py:20
  105.3 9.8 %custom-call.17 = f32[1,128,128]{1,2,0:T(8,128)S(1)} custom-call(f32[1,128,128]{2,1,0:T(8,128)S(1)} %get-tuple-element.58), custom_call_target="InvertDiagBlocksLowerTriangular" | custom-call | tf_op jit(solution)/shard_map/jit(cholesky)/cholesky | solution.py:20
  115.8 11.7 %cholesky.147 = f32[128,128]{1,0:T(8,128)S(1)} custom-call(f32[128,128]{1,0:T(8,128)S(1)} %convolution_subtract_fusion.7), custom_call_target="Cholesky" | custom-call | tf_op jit(solution)/shard_map/jit(cholesky)/cholesky | solution.py:20
  129.6 4.0 %while.4 = (s32[]{:T(128)}, f32[256,256]{1,0:T(8,128)S(1)}, s32[2,2]{1,0:T(2,128)S(1)}, f32[2,128,128]{2,1,0:T(8,128)S(1)}, s32[]{:T(128)}) while((s32[]{:T(128)}, f32[256,256]{1,0:T(8,128)S(1)}, s32[2,2]{1,0:T(2,128)S(1)}, f32[2,128,128]{2,1,0:T(8,128)S(1)}, s32[]{:T(128)}) %tuple.52), condition=%wide.while_cond, body=%wide.while_body.sunk | while | flops 2 | bytes 131181 | solution.py:21
  130.3 1.4 bitcast_dynamic-update-slice_fusion.4
  132.3 1.4 bitcast_dynamic-update-slice_fusion.4
  133.7 19.8 %custom-call.18 = f32[2,128,128]{1,2,0:T(8,128)S(1)} custom-call(f32[2,128,128]{2,1,0:T(8,128)S(1)} %get-tuple-element.19), custom_call_target="InvertDiagBlocksLowerTriangular" | custom-call | tf_op jit(solution)/shard_map/jit(_solve_triangular)/triangular_solve | solution.py:21
  154.4 0.8 copy.18
  156.9 0.7 fusion.9
  157.7 0.8 cholesky.197
  158.5 11.7 %cholesky.164 = f32[128,128]{1,0:T(8,128)S(1)} custom-call(f32[128,128]{1,0:T(8,128)S(1)} %cholesky.197), custom_call_target="Cholesky" | custom-call | tf_op jit(solution)/shard_map/jit(cholesky)/cholesky | solution.py:20
  170.3 9.8 %custom-call.19 = f32[1,128,128]{1,2,0:T(8,128)S(1)} custom-call(f32[1,128,128]{2,1,0:T(8,128)S(1)} %get-tuple-element.54), custom_call_target="InvertDiagBlocksLowerTriangular" | custom-call | tf_op jit(solution)/shard_map/jit(cholesky)/cholesky | solution.py:20
  180.1 1.1 fusion.23
  181.3 1.1 convolution_subtract_fusion.6
  182.5 11.7 %cholesky.181 = f32[128,128]{1,0:T(8,128)S(1)} custom-call(f32[128,128]{1,0:T(8,128)S(1)} %convolution_subtract_fusion.6), custom_call_target="Cholesky" | custom-call | tf_op jit(solution)/shard_map/jit(cholesky)/cholesky | solution.py:20
  194.3 0.8 compare_reduce_fusion
  197.0 1.0 fusion.11
  198.0 2.3 gather_fusion.1
  201.0 2.3 gather_fusion
  204.1 0.9 reshape.56
  205.8 4.0 %while.5 = (s32[]{:T(128)}, f32[256,256]{1,0:T(8,128)S(1)}, s32[2,2]{1,0:T(2,128)S(1)}, f32[2,128,128]{2,1,0:T(8,128)S(1)}, s32[]{:T(128)}) while((s32[]{:T(128)}, f32[256,256]{1,0:T(8,128)S(1)}, s32[2,2]{1,0:T(2,128)S(1)}, f32[2,128,128]{2,1,0:T(8,128)S(1)}, s32[]{:T(128)}) %tuple.60), condition=%wide.while_cond.clone, body=%wide.while_body.clone.sunk | while | flops 2 | bytes 131181 | solution.py:21
  206.5 1.4 bitcast_dynamic-update-slice_fusion.5
  208.5 1.4 bitcast_dynamic-update-slice_fusion.5
  209.9 19.7 %custom-call.20 = f32[2,128,128]{1,2,0:T(8,128)S(1)} custom-call(f32[2,128,128]{2,1,0:T(8,128)S(1)} %get-tuple-element.20), custom_call_target="InvertDiagBlocksLowerTriangular" | custom-call | tf_op jit(solution)/shard_map/jit(_solve_triangular)/triangular_solve | solution.py:21
  234.3 0.8 copy.17
  237.3 0.9 fusion.3
  238.2 0.9 copy-done.2
  239.2 1.7 fusion.4
  242.9 1.5 fusion.1
  (110 shorter events, 18.5 us)
Async XLA Ops:
  10.0 10.6 %copy-start = (f32[256,512]{1,0:T(8,128)S(1)}, f32[256,512]{1,0:T(8,128)}, u32[]{:S(2)}) copy-start(f32[256,512]{1,0:T(8,128)} %param.5) | copy-start | bytes 1572868
  10.0 24.2 %all-to-all-start = ((f32[32,8,640]{2,1,0:T(8,128)}), f32[32,8,640]{2,1,0:T(8,128)S(1)}, u32[]{:S(2)}, u32[]{:S(2)}) async-start(f32[32,8,640]{2,1,0:T(8,128)} %select_maximum_fusion), calls=%async_computation | async-start | bytes 1310720 | tf_op jit(solution)/shard_map/scatter/all_to_all | solution.py:41
  20.6 31.0 %collective-permute-start.4 = (f32[256,512]{1,0:T(8,128)S(1)}, f32[256,512]{1,0:T(8,128)S(1)}, u32[]{:S(2)}, u32[]{:S(2)}) collective-permute-start(f32[256,512]{1,0:T(8,128)S(1)} %copy-done), channel_id=1, source_target_pairs={{0,8},{16,24},{32,40},{48,56},{64,72},{80,88},{96,104},{112,120},{... | collective-permute-start | bytes 1572872 | tf_op jit(solution)/shard_map/rowpanel/ppermute | solution.py:15
  34.2 26.4 %copy-start.11 = (f32[8,640]{1,0:T(8,128)}, f32[8,640]{1,0:T(8,128)S(1)}, u32[]{:S(2)}) copy-start(f32[8,640]{1,0:T(8,128)S(1)} %get-tuple-element.49) | copy-start | bytes 61444
  34.2 13.8 %copy-start.8 = (f32[8,512]{1,0:T(8,128)}, f32[8,512]{1,0:T(8,128)S(1)}, u32[]{:S(2)}) copy-start(f32[8,512]{1,0:T(8,128)S(1)} %slice.118) | copy-start | bytes 49156
  34.3 13.8 %collective-permute-start = (f32[8,768]{1,0:T(8,128)S(1)}, f32[8,768]{1,0:T(8,128)S(1)}, u32[]{:S(2)}, u32[]{:S(2)}) collective-permute-start(f32[8,768]{1,0:T(8,128)S(1)} %pad_maximum_fusion.10), channel_id=1, source_target_pairs={{0,8},{16,24},{32,40},{48,56},{64,72},{80,88},{96,104},{112,120},{... | collective-permute-start | bytes 73736 | tf_op jit(solution)/shard_map/diag/ppermute | solution.py:15
  48.0 2.2 collective-permute-start.1
  50.3 9.0 %collective-permute-start.2 = (f32[8,768]{1,0:T(8,128)S(1)}, f32[8,768]{1,0:T(8,128)S(1)}, u32[]{:S(2)}, u32[]{:S(2)}) collective-permute-start(f32[8,768]{1,0:T(8,128)S(1)} %broadcast_select_fusion.5), channel_id=1, source_target_pairs={{0,2},{4,6},{8,10},{12,14},{16,18},{20,22},{24,26},{28,30},{32,34}... | collective-permute-start | bytes 73736 | tf_op jit(solution)/shard_map/diag/ppermute | solution.py:15
  51.6 25.9 %collective-permute-start.5 = (f32[256,512]{1,0:T(8,128)S(1)}, f32[256,512]{1,0:T(8,128)S(1)}, u32[]{:S(2)}, u32[]{:S(2)}) collective-permute-start(f32[256,512]{1,0:T(8,128)S(1)} %broadcast_select_fusion), channel_id=1, source_target_pairs={{0,4},{8,12},{16,20},{24,28},{32,36},{40,44},{48,52},{56,60},{64,6... | collective-permute-start | bytes 1572872 | tf_op jit(solution)/shard_map/rowpanel/ppermute | solution.py:15
  59.3 9.4 %collective-permute-start.3 = (f32[8,768]{1,0:T(8,128)S(1)}, f32[8,768]{1,0:T(8,128)S(1)}, u32[]{:S(2)}, u32[]{:S(2)}) collective-permute-start(f32[8,768]{1,0:T(8,128)S(1)} %broadcast_select_fusion.6), channel_id=1, source_target_pairs={{0,1},{2,3},{4,5},{6,7},{8,9},{10,11},{12,13},{14,15},{16,17},{18,... | collective-permute-start | bytes 73736 | tf_op jit(solution)/shard_map/diag/ppermute | solution.py:15
  69.7 23.6 %all-to-all-start.1 = ((f32[32,8,896]{2,1,0:T(8,128)}), f32[32,8,896]{2,1,0:T(8,128)S(1)}, u32[]{:S(2)}, u32[]{:S(2)}) async-start(f32[32,8,896]{2,1,0:T(8,128)} %broadcast_in_dim.21), calls=%async_computation.1 | async-start | bytes 1835008 | tf_op jit(solution)/shard_map/diag/all_to_all | solution.py:63
  77.5 161.7 %all-gather.3.cloned.1.call-start = ((), (), s32[]{:S(2)}) async-start(), calls=%async_computation.2 | async-start | bytes 1081344 | tf_op jit(solution)/shard_map/columns/all_gather | solution.py:46
  77.7 12.7 %collective-permute-start.6 = (f32[256,512]{1,0:T(8,128)S(1)}, f32[256,512]{1,0:T(8,128)S(1)}, u32[]{:S(2)}, u32[]{:S(2)}) collective-permute-start(f32[256,512]{1,0:T(8,128)S(1)} %broadcast_select_fusion.1), channel_id=1, source_target_pairs={{0,2},{4,6},{8,10},{12,14},{16,18},{20,22},{24,26},{28,30},{32,34}... | collective-permute-start | bytes 1572872 | tf_op jit(solution)/shard_map/rowpanel/ppermute | solution.py:15
  79.0 0.7 copy-start.12
  79.8 0.7 copy-start.9
  90.4 143.3 %collective-permute-start.7 = (f32[256,512]{1,0:T(8,128)S(1)}, f32[256,512]{1,0:T(8,128)}, u32[]{:S(2)}, u32[]{:S(2)}) collective-permute-start(f32[256,512]{1,0:T(8,128)S(1)} %broadcast_select_fusion.2), channel_id=1, source_target_pairs={{0,1},{2,3},{4,5},{6,7},{8,9},{10,11},{12,13},{14,15},{16,17},{18,... | collective-permute-start | bytes 1572872 | tf_op jit(solution)/shard_map/rowpanel/ppermute | solution.py:15
  155.3 0.9 copy-start.4
  194.2 2.8 %copy-start.3 = (f32[256,256]{1,0:T(8,128)}, f32[256,256]{1,0:T(8,128)S(1)}, u32[]{:S(2)}) copy-start(f32[256,256]{1,0:T(8,128)S(1)} %get-tuple-element.52) | copy-start | bytes 786436
  204.9 0.8 copy-start.10
  205.4 25.0 %copy-start.5 = (f32[64,256]{1,0:T(8,128)}, f32[64,256]{1,0:T(8,128)S(1)}, u32[]{:S(2)}) copy-start(f32[64,256]{1,0:T(8,128)S(1)} %get-tuple-element.60) | copy-start | bytes 196612
  236.2 0.8 copy-start.6
  236.2 0.9 copy-start.7
  238.2 0.9 copy-start.2
  239.2 1.8 copy-start.1
Sparse Core Ops, SparseCore 0:
  81.5 61.3 all-gather.2

commit v2 on v1

v2 whole, which is shorter than its diff:
```python
import jax
import jax.numpy as jnp
from jax import lax
from jax.experimental import pallas as pl
from jax.experimental.pallas import tpu as pltpu
from jax.sharding import PartitionSpec as P

HI = lax.Precision.HIGHEST


def dot(a, b):
    return jnp.dot(a, b, precision=HI)


def tree_step(value, hop, extent, position):
    pairs = [(z, z + hop) for z in range(0, extent, 2 * hop)]
    moved = lax.ppermute(value, "col", pairs)
    return jnp.where(position % (2 * hop) == hop, moved, value)


SUB = 8
LANES = 128


def factor_tile(blocks):
    shape = (SUB, LANES)
    lane = lax.broadcasted_iota(jnp.int32, shape, 1)
    sub = lax.broadcasted_iota(jnp.int32, shape, 0)
    count = len(blocks)
    blocks = list(blocks)
    upper, inverse = [], []
    for b in range(count):
        base = b * SUB
        here = blocks[b]
        across = [jnp.broadcast_to(here[:, base + k : base + k + 1], shape) for k in range(SUB)]
        rows = [jnp.broadcast_to(here[k : k + 1, :], shape) for k in range(SUB)]
        s = {}
        for k in range(SUB):
            for i in range(k, SUB):
                s[i, k] = jnp.broadcast_to(across[k][i : i + 1, :], shape)
        rinv, low, u, w = [], {}, [], []
        for k in range(SUB):
            rinv.append(lax.rsqrt(s[k, k]))
            for i in range(k + 1, SUB):
                low[i, k] = s[i, k] * rinv[k]
            for j in range(k + 1, SUB):
                for i in range(j, SUB):
                    s[i, j] = s[i, j] - low[i, k] * low[j, k]
            uk = rows[k]
            wk = jnp.where(lane < base, rows[k], jnp.where(lane == base + k, 1.0, 0.0))
            for m in range(k):
                uk = uk - low[k, m] * u[m]
                wk = wk - low[k, m] * w[m]
            u.append(uk * rinv[k])
            w.append(wk * rinv[k])
        u_block, w_block = u[0], w[0]
        for k in range(1, SUB):
            u_block = jnp.where(sub == k, u[k], u_block)
            w_block = jnp.where(sub == k, w[k], w_block)
        upper.append(jnp.where(lane >= sub + base, u_block, 0.0))
        inverse.append(w_block)
        if b + 1 == count:
            break
        q = [None] * SUB
        for k in reversed(range(SUB)):
            v = jnp.where(lane < base + SUB, w[k], u[k])
            for m in range(k + 1, SUB):
                v = v - low[m, k] * q[m]
            q[k] = v * rinv[k]
        keep = (lane < base) | (lane >= base + SUB)
        for i in range(b + 1, count):
            old = blocks[i]
            terms = [
                jnp.broadcast_to(old[:, base + k : base + k + 1], shape) * q[k] for k in range(SUB)
            ]
            while len(terms) > 1:
                terms = [terms[t] + terms[t + 1] for t in range(0, len(terms), 2)]
            blocks[i] = jnp.where(keep, old, 0.0) - terms[0]
    return upper, inverse


def factor_kernel(d00_ref, d1_ref, low_ref, inv_ref, work):
    tile = d00_ref.shape[0]
    size = 2 * tile
    work[:tile, :tile] = d00_ref[...]
    work[tile:, :] = d1_ref[...]
    work[:tile, tile:] = d1_ref[:, :tile].T
    row_id = lax.broadcasted_iota(jnp.int32, (size, LANES), 0)
    col_id = lax.broadcasted_iota(jnp.int32, (LANES, size), 1)

    def step(t, carry):
        base = pl.multiple_of(t * LANES, LANES)
        tile_rows = pl.ds(base, LANES)
        here = [work[pl.ds(base + SUB * i, SUB), tile_rows] for i in range(LANES // SUB)]
        up, inv = factor_tile(here)
        up = jnp.concatenate(up, axis=0)
        inv = jnp.concatenate(inv, axis=0)
        across = jnp.dot(inv, work[tile_rows, :], precision=HI, preferred_element_type=jnp.float32)
        below = lax.dot_general(
            work[:, tile_rows], inv, (((1,), (1,)), ((), ())), precision=HI,
            preferred_element_type=jnp.float32,
        )
        below = jnp.where(row_id >= base + LANES, below, 0.0)
        low_ref[:, tile_rows] = below
        low_ref[tile_rows, tile_rows] = up.T
        inv_ref[tile_rows, :] = jnp.where(col_id < base, across, 0.0)
        inv_ref[tile_rows, tile_rows] = inv
        work[tile_rows, :] = across
        work[tile_rows, tile_rows] = inv
        across = work[tile_rows, :]
        work[:, tile_rows] = jnp.zeros((size, LANES), jnp.float32)
        work[...] = work[...] - jnp.dot(
            below, across, precision=HI, preferred_element_type=jnp.float32
        )
        return carry

    lax.fori_loop(0, size // LANES, step, 0)


def factor(d00, d1):
    tile = d00.shape[0]
    size = 2 * tile
    return pl.pallas_call(
        factor_kernel,
        out_shape=[jax.ShapeDtypeStruct((size, size), jnp.float32)] * 2,
        in_specs=[pl.BlockSpec(memory_space=pltpu.VMEM)] * 2,
        out_specs=[pl.BlockSpec(memory_space=pltpu.VMEM)] * 2,
        scratch_shapes=[pltpu.VMEM((size, size), jnp.float32)],
        compiler_params=pltpu.CompilerParams(vmem_limit_bytes=32 * 1024 * 1024),
        cost_estimate=pl.CostEstimate(flops=2 * size**3, bytes_accessed=16 * size * size, transcendentals=size),
        name="factor",
    )(d00, d1)


def shards(covariance, observations):
    tile, wide = covariance.shape
    nrhs = observations.shape[0]
    rows = lax.axis_size("row")
    cols = lax.axis_size("col")
    row = lax.axis_index("row")
    col = lax.axis_index("col")
    part = tile // rows

    with jax.named_scope("scatter"):
        obs_parts = observations.reshape(rows, part // 2, -1)
        lanes = obs_parts.shape[2]
        obs_parts = jnp.pad(obs_parts, ((0, 0), (0, part - part // 2), (0, 0)))
        sent = jnp.concatenate([covariance.reshape(rows, part, wide), obs_parts], axis=2)
        got = lax.all_to_all(sent, "row", split_axis=0, concat_axis=0, tiled=True)
        first, second = got[0], got[1]

    with jax.named_scope("columns"):
        col_piece = jnp.concatenate([first[:, :wide], second[:, :wide]], axis=0)
        col_all = lax.all_gather(col_piece, "row", axis=0, tiled=False)
        columns = jnp.concatenate(
            [col_all[:, :part].reshape(tile, wide), col_all[:, part:].reshape(tile, wide)], axis=0
        )

    hops = []
    hop = cols // 2
    while hop >= 1:
        hops.append(hop)
        hop //= 2

    with jax.named_scope("diag"):
        diag_piece = jnp.concatenate([first[:, :tile], second[:, :wide]], axis=1)
        for hop in hops:
            diag_piece = tree_step(diag_piece, hop, cols, col)
        obs_piece = jnp.concatenate([first[: part // 2, wide:], second[: part // 2, wide:]], axis=0)
        piece = jnp.concatenate([diag_piece, obs_piece], axis=1)
        spread = jnp.broadcast_to(piece[None], (rows,) + piece.shape)
        whole = lax.all_to_all(spread, "row", split_axis=0, concat_axis=0, tiled=True)
        diag0 = whole[:, :, :tile].reshape(tile, tile)
        diag1 = whole[:, :, tile : 3 * tile].reshape(tile, wide)
        obs0 = whole[:, : part // 2, 3 * tile :].reshape(nrhs, tile)
        obs1 = whole[:, part // 2 :, 3 * tile :].reshape(nrhs, tile)
        obs_both = jnp.concatenate([obs0, obs1], axis=1)

    with jax.named_scope("rowpanel"):
        panel = covariance
        for hop in hops:
            panel = tree_step(panel, hop, cols, col)

    low, inv = factor(diag0, diag1)

    with jax.named_scope("solve"):
        x = dot(panel, inv.T)
        y = dot(inv, columns)
        z = dot(obs_both, inv.T)

    with jax.named_scope("update"):
        trail = covariance - dot(x, y)
        first_rows = jnp.where(row == 0, low[:tile], low[tile:])
        edge = jnp.where(row <= 1, first_rows, x)
        other = jnp.where(row <= 1, 0.0, trail)
        factored = jnp.where(col == 0, edge, other)
        reduced = observations - dot(z, x.T)
        solved = jnp.where(row == 0, z[:, :tile], jnp.where(row == 1, z[:, tile:], reduced))

    with jax.named_scope("terms"):
        logdet = 2.0 * jnp.sum(jnp.log(jnp.diagonal(low)))
        quad = jnp.sum(z * z, axis=1)
        site_terms = -(quad + logdet) / (4.0 * tile)
    return factored, solved, site_terms


def solution(mesh):
    in_specs = (P("row", "col"), P(None, "row"))
    out_specs = (P("row", "col"), P(None, "row"), P())
    return jax.shard_map(shards, mesh=mesh, in_specs=in_specs, out_specs=out_specs, check_vma=False)
```

time: 256 us -> 155 us (0.61); the launches traced: 251 us -> 154 us
  other arithmetic: 115 us -> 4.75 us
  Pallas kernels: 0 us -> 30.9 us
  local copies, waits for them, and re-layouts: 23.5 us -> 9.39 us
  waiting for transfers between devices: 19.5 us -> 26.3 us
  matrix products: 14.5 us -> 8.32 us
  between operations: 19 us -> 15 us
    another operation x18 -> x0, other arithmetic: 109 us -> none  [the longest x13 68.7 us: factor(): chol = jnp.linalg.cholesky(block)]
    pallas_call x0 -> x1, Pallas kernels: none -> 30.9 us  [factor(): pl.pallas_call(factor_kernel, out_shape=[jax.ShapeDtypeStruct((size, size...]
    another operation x23 -> x0, local copies, waits for them, and re-layouts: 9.07 us -> none  [the longest x15 7.99 us: factor(): jax.scipy.linalg.solve_triangular(chol, jnp.eye(block.shape[0], dtype=blo...]
    all_gather x1, waiting for transfers between devices: 0.02 us -> 5.73 us  [shards(): col_all = lax.all_gather(col_piece, 'row', axis=0, tiled=False)]
    another operation x10 -> x0, matrix products: 4.59 us -> none  [the longest x4 2.84 us: factor(): chol = jnp.linalg.cholesky(block)]
    unnamed x26 -> x6, local copies, waits for them, and re-layouts: 3.96 us -> 0.01 us
    dot_general x15 -> x5, matrix products: 9.87 us -> 8.32 us  [dot(): return jnp.dot(a, b, precision=HI)]
  transfers between devices with their start and end apart: 11 -> 11, of which waited for: 5 -> 5; matrix products, arithmetic and copies ran while one was open for 56% -> 10% of each run, Pallas kernels for 0% -> 20%
where the time goes in v2:
time: 155 us; the launch traced here: 154 us
  starting transfers between devices  59.7 us (39%)
  Pallas kernels  30.9 us (20%)
  waiting for transfers between devices  26.3 us (17%)
  between operations  15 us (10%)
  local copies, waits for them, and re-layouts  9.39 us (6%)
  matrix products  8.32 us (5%)
  other arithmetic  4.75 us (3%)
    ppermute x8, starting transfers between devices, tree_step(): moved = lax.ppermute(value, 'col', pairs)  41.3 us
    pallas_call x1, Pallas kernels, factor(): pl.pallas_call(factor_kernel, out_shape=[jax.ShapeDtypeStruct((size, size...  30.9 us
    ppermute x8, waiting for transfers between devices, tree_step(): moved = lax.ppermute(value, 'col', pairs)  20.6 us
    all_to_all x1, starting transfers between devices, shards(): got = lax.all_to_all(sent, 'row', split_axis=0, concat_axis=0, tiled=True)  10.6 us
    dot_general x5, matrix products, dot(): return jnp.dot(a, b, precision=HI)  8.32 us
    all_to_all x1, starting transfers between devices, shards(): lax.all_to_all(spread, 'row', split_axis=0, concat_axis=0, tiled=True)  7.81 us
    all_gather x1, waiting for transfers between devices, shards(): col_all = lax.all_gather(col_piece, 'row', axis=0, tiled=False)  5.73 us
    gather x1, local copies, waits for them, and re-layouts, shards(): logdet = 2.0 * jnp.sum(jnp.log(jnp.diagonal(low)))  4.52 us
  transfers between devices with their start and end apart: 11, of which 5 were waited for; matrix products, arithmetic and copies ran while one was open for 10% of the time, Pallas kernels for 20%

profile of v2, /device:TPU:1, one launch (start us, length us, event | category | flops | bytes accessed | tf_op | source)
XLA Modules:
  0.0 154.4 jit_solution(1391077654191191364)
XLA Ops:
  7.2 0.9 reshape.32
  8.0 1.9 %select_maximum_fusion = f32[32,8,640]{2,1,0:T(8,128)} fusion(f32[32,4,128]{2,1,0:T(4,128)S(1)} %reshape.32, f32[32,8,512]{2,1,0:T(8,128)} %bitcast.23), kind=kLoop, calls=%fused_computation.10 | loop fusion | flops 491520 | bytes 1245184 | tf_op jit(solution)/shard_map/scatter/concatenate | solution.py:148
  10.0 0.0 copy-start
  10.0 10.6 %all-to-all-start = ((f32[32,8,640]{2,1,0:T(8,128)}), f32[32,8,640]{2,1,0:T(8,128)S(1)}, u32[]{:S(2)}, u32[]{:S(2)}) async-start(f32[32,8,640]{2,1,0:T(8,128)} %select_maximum_fusion), calls=%async_computation | async-start | bytes 1310720 | tf_op jit(solution)/shard_map/scatter/all_to_all | solution.py:149
  20.5 0.0 copy-done
  20.6 13.6 %collective-permute-start.4 = (f32[256,512]{1,0:T(8,128)S(1)}, f32[256,512]{1,0:T(8,128)S(1)}, u32[]{:S(2)}, u32[]{:S(2)}) collective-permute-start(f32[256,512]{1,0:T(8,128)S(1)} %copy-done), channel_id=1, source_target_pairs={{0,8},{16,24},{32,40},{48,56},{64,72},{80,88},{96,104},{112,120},{... | collective-permute-start | bytes 1572872 | tf_op jit(solution)/shard_map/rowpanel/ppermute | solution.py:17
  34.2 0.0 all-to-all-done
  34.2 12.8 %collective-permute-start = (f32[8,768]{1,0:T(8,128)S(1)}, f32[8,768]{1,0:T(8,128)S(1)}, u32[]{:S(2)}, u32[]{:S(2)}) collective-permute-start(f32[8,768]{1,0:T(8,128)S(1)} %pad_maximum_fusion.1), channel_id=1, source_target_pairs={{0,8},{16,24},{32,40},{48,56},{64,72},{80,88},{96,104},{112,120},{... | collective-permute-start | bytes 73736 | tf_op jit(solution)/shard_map/diag/ppermute | solution.py:17
  47.1 0.9 collective-permute-done
  48.0 1.3 collective-permute-start.1
  49.3 0.9 collective-permute-done.1
  50.2 1.3 collective-permute-start.2
  51.5 0.0 collective-permute-done.4
  51.5 0.1 broadcast_select_fusion
  51.6 7.6 %collective-permute-start.5 = (f32[256,512]{1,0:T(8,128)S(1)}, f32[256,512]{1,0:T(8,128)S(1)}, u32[]{:S(2)}, u32[]{:S(2)}) collective-permute-start(f32[256,512]{1,0:T(8,128)S(1)} %broadcast_select_fusion), channel_id=1, source_target_pairs={{0,4},{8,12},{16,20},{24,28},{32,36},{40,44},{48,52},{56,60},{64,6... | collective-permute-start | bytes 1572872 | tf_op jit(solution)/shard_map/rowpanel/ppermute | solution.py:17
  59.2 0.0 collective-permute-done.2
  59.2 1.3 collective-permute-start.3
  60.6 8.1 %collective-permute-done.3 = f32[8,768]{1,0:T(8,128)S(1)} collective-permute-done((f32[8,768]{1,0:T(8,128)S(1)}, f32[8,768]{1,0:T(8,128)S(1)}, u32[]{:S(2)}, u32[]{:S(2)}) %collective-permute-start.3) | collective-permute-done | bytes 24608 | tf_op jit(solution)/shard_map/diag/ppermute | solution.py:17
  68.7 1.0 broadcast_in_dim.14
  69.7 7.8 %all-to-all-start.1 = ((f32[32,8,896]{2,1,0:T(8,128)}), f32[32,8,896]{2,1,0:T(8,128)S(1)}, u32[]{:S(2)}, u32[]{:S(2)}) async-start(f32[32,8,896]{2,1,0:T(8,128)} %broadcast_in_dim.14), calls=%async_computation.1 | async-start | bytes 1835008 | tf_op jit(solution)/shard_map/diag/all_to_all | solution.py:172
  77.5 0.0 all-gather.3.cloned.1.call-start
  77.5 0.0 collective-permute-done.5
  77.6 0.1 broadcast_select_fusion.1
  77.6 1.3 collective-permute-start.6
  79.0 0.6 pad_maximum_fusion
  79.6 0.0 all-gather.3.cloned.1.call-update
  79.6 10.7 %collective-permute-done.6 = f32[256,512]{1,0:T(8,128)S(1)} collective-permute-done((f32[256,512]{1,0:T(8,128)S(1)}, f32[256,512]{1,0:T(8,128)S(1)}, u32[]{:S(2)}, u32[]{:S(2)}) %collective-permute-start.6) | collective-permute-done | bytes 524320 | tf_op jit(solution)/shard_map/rowpanel/ppermute | solution.py:17
  90.3 0.9 broadcast_select_fusion.2
  91.2 2.1 %collective-permute-start.7 = (f32[256,512]{1,0:T(8,128)}, f32[256,512]{1,0:T(8,128)}, u32[]{:S(2)}, u32[]{:S(2)}) collective-permute-start(f32[256,512]{1,0:T(8,128)} %broadcast_select_fusion.2), channel_id=1, source_target_pairs={{0,1},{2,3},{4,5},{6,7},{8,9},{10,11},{12,13},{14,15},{16,17},{18,... | collective-permute-start | bytes 1572872 | tf_op jit(solution)/shard_map/rowpanel/ppermute | solution.py:17
  93.3 0.0 all-to-all-done.1
  93.3 0.1 slice_bitcast_fusion.2.d1_ref
  93.4 30.9 %factor.1 = (f32[512,512]{1,0:T(8,128)S(1)}, f32[512,512]{1,0:T(8,128)S(1)}) custom-call(f32[256,256]{1,0:T(8,128)S(1)} %slice_bitcast_fusion.3.d00_ref, f32[256,512]{1,0:T(8,128)S(1)} %slice_bitcast_fusion.2.d1_ref), custom_call_target="tpu_custom_call" | custom-call | flops 268435456 | bytes 4194304 | tf_op jit(solution)/shard_map/factor/pallas_call | solution.py:123
  124.3 4.5 %gather_fusion = f32[512]{0:T(512)S(1)} fusion(f32[512,512]{1,0:T(8,128)S(1)} %get-tuple-element.5, s32[512]{0:T(512)S(1)} %bitcast.22), kind=kCustom, calls=%fused_computation | custom fusion | bytes 8192 | tf_op jit(solution)/shard_map/terms/jit(diagonal)/cond/branch_0_fun/gather | solution.py:201
  128.8 0.7 fusion.16
  129.4 0.6 log_reduce_fusion
  130.1 0.0 copy-start.2
  130.1 0.9 reshape.37
  131.0 0.0 copy-done.2
  131.7 1.2 multiply_reduce_fusion
  132.9 0.5 negate_multiply_fusion
  133.4 0.0 collective-permute-done.7
  133.4 2.1 %fusion.7 = f32[256,512]{1,0:T(8,128)S(1)} fusion(f32[512,512]{1,0:T(8,128)S(1)} %get-tuple-element.6, f32[256,512]{1,0:T(8,128)} %collective-permute-done.7, f32[256,512]{1,0:T(8,128)} %broadcast_select_fusion.2, pred[]{:T(512)S(6)} %eq.37), kind=kOutput, calls=%fused_computation.16 | convolution fusion | flops 805437440 | bytes 2621441 | tf_op jit(solution)/shard_map/solve/dot_general | solution.py:12
  135.6 0.0 copy-done.1
  135.6 1.2 fusion.2
  136.8 5.7 %all-gather.3.cloned.1.call-done = f32[512,512]{1,0:T(8,128)} async-done(((f32[16,512]{1,0:T(8,128)}), f32[512,512]{1,0:T(8,128)}) %all-gather.3.cloned.1.call-update) | async-done | bytes 1048592 | tf_op jit(solution)/shard_map/columns/all_gather | solution.py:154
  142.6 1.3 slice_bitcast_fusion.1
  143.8 1.8 %fusion.3 = f32[512,512]{1,0:T(8,128)S(1)} fusion(f32[512,512]{1,0:T(8,128)S(1)} %get-tuple-element.6, f32[256,512]{1,0:T(8,128)S(1)} %get-tuple-element.8, f32[256,512]{1,0:T(8,128)S(1)} %get-tuple-element.7), kind=kOutput, calls=%fused_computation.6 | convolution fusion | flops 1610874880 | bytes 3145728 | tf_op jit(solution)/shard_map/solve/dot_general | solution.py:12
  145.7 1.9 %select_select_fusion = f32[256,512]{1,0:T(8,128)} fusion(f32[256,512]{1,0:T(8,128)S(1)} %fusion.7, f32[512,512]{1,0:T(8,128)S(1)} %get-tuple-element.5, f32[256,512]{1,0:T(8,128)S(1)} %copy-done, f32[512,512]{1,0:T(8,128)S(1)} %fusion.3, pred[]{:T(512)S(6)} %eq.36, pred[]{:T(512)S(6)} %le.4, pred[]{:T(512)S(6)} %eq.35), kind=kOutput, calls=%fused_computation.15 | convolution fusion | flops 805961728 | bytes 4194307 | tf_op jit(solution)/shard_map/update/dot_general | solution.py:12
  (16 shorter events, 0.1 us)
Async XLA Ops:
  10.0 10.6 %copy-start = (f32[256,512]{1,0:T(8,128)S(1)}, f32[256,512]{1,0:T(8,128)}, u32[]{:S(2)}) copy-start(f32[256,512]{1,0:T(8,128)} %param.2) | copy-start | bytes 1572868
  10.0 24.2 %all-to-all-start = ((f32[32,8,640]{2,1,0:T(8,128)}), f32[32,8,640]{2,1,0:T(8,128)S(1)}, u32[]{:S(2)}, u32[]{:S(2)}) async-start(f32[32,8,640]{2,1,0:T(8,128)} %select_maximum_fusion), calls=%async_computation | async-start | bytes 1310720 | tf_op jit(solution)/shard_map/scatter/all_to_all | solution.py:149
  20.6 31.0 %collective-permute-start.4 = (f32[256,512]{1,0:T(8,128)S(1)}, f32[256,512]{1,0:T(8,128)S(1)}, u32[]{:S(2)}, u32[]{:S(2)}) collective-permute-start(f32[256,512]{1,0:T(8,128)S(1)} %copy-done), channel_id=1, source_target_pairs={{0,8},{16,24},{32,40},{48,56},{64,72},{80,88},{96,104},{112,120},{... | collective-permute-start | bytes 1572872 | tf_op jit(solution)/shard_map/rowpanel/ppermute | solution.py:17
  34.2 13.8 %collective-permute-start = (f32[8,768]{1,0:T(8,128)S(1)}, f32[8,768]{1,0:T(8,128)S(1)}, u32[]{:S(2)}, u32[]{:S(2)}) collective-permute-start(f32[8,768]{1,0:T(8,128)S(1)} %pad_maximum_fusion.1), channel_id=1, source_target_pairs={{0,8},{16,24},{32,40},{48,56},{64,72},{80,88},{96,104},{112,120},{... | collective-permute-start | bytes 73736 | tf_op jit(solution)/shard_map/diag/ppermute | solution.py:17
  48.0 2.2 %collective-permute-start.1 = (f32[8,768]{1,0:T(8,128)S(1)}, f32[8,768]{1,0:T(8,128)S(1)}, u32[]{:S(2)}, u32[]{:S(2)}) collective-permute-start(f32[8,768]{1,0:T(8,128)S(1)} %broadcast_select_fusion.3), channel_id=1, source_target_pairs={{0,4},{8,12},{16,20},{24,28},{32,36},{40,44},{48,52},{56,60},{64,6... | collective-permute-start | bytes 73736 | tf_op jit(solution)/shard_map/diag/ppermute | solution.py:17
  50.2 9.0 %collective-permute-start.2 = (f32[8,768]{1,0:T(8,128)S(1)}, f32[8,768]{1,0:T(8,128)S(1)}, u32[]{:S(2)}, u32[]{:S(2)}) collective-permute-start(f32[8,768]{1,0:T(8,128)S(1)} %broadcast_select_fusion.4), channel_id=1, source_target_pairs={{0,2},{4,6},{8,10},{12,14},{16,18},{20,22},{24,26},{28,30},{32,34}... | collective-permute-start | bytes 73736 | tf_op jit(solution)/shard_map/diag/ppermute | solution.py:17
  51.6 25.9 %collective-permute-start.5 = (f32[256,512]{1,0:T(8,128)S(1)}, f32[256,512]{1,0:T(8,128)S(1)}, u32[]{:S(2)}, u32[]{:S(2)}) collective-permute-start(f32[256,512]{1,0:T(8,128)S(1)} %broadcast_select_fusion), channel_id=1, source_target_pairs={{0,4},{8,12},{16,20},{24,28},{32,36},{40,44},{48,52},{56,60},{64,6... | collective-permute-start | bytes 1572872 | tf_op jit(solution)/shard_map/rowpanel/ppermute | solution.py:17
  59.2 9.4 %collective-permute-start.3 = (f32[8,768]{1,0:T(8,128)S(1)}, f32[8,768]{1,0:T(8,128)S(1)}, u32[]{:S(2)}, u32[]{:S(2)}) collective-permute-start(f32[8,768]{1,0:T(8,128)S(1)} %broadcast_select_fusion.5), channel_id=1, source_target_pairs={{0,1},{2,3},{4,5},{6,7},{8,9},{10,11},{12,13},{14,15},{16,17},{18,... | collective-permute-start | bytes 73736 | tf_op jit(solution)/shard_map/diag/ppermute | solution.py:17
  69.7 23.6 %all-to-all-start.1 = ((f32[32,8,896]{2,1,0:T(8,128)}), f32[32,8,896]{2,1,0:T(8,128)S(1)}, u32[]{:S(2)}, u32[]{:S(2)}) async-start(f32[32,8,896]{2,1,0:T(8,128)} %broadcast_in_dim.14), calls=%async_computation.1 | async-start | bytes 1835008 | tf_op jit(solution)/shard_map/diag/all_to_all | solution.py:172
  77.5 65.1 %all-gather.3.cloned.1.call-start = ((), (), s32[]{:S(2)}) async-start(), calls=%async_computation.2 | async-start | bytes 1081344 | tf_op jit(solution)/shard_map/columns/all_gather | solution.py:154
  77.6 12.7 %collective-permute-start.6 = (f32[256,512]{1,0:T(8,128)S(1)}, f32[256,512]{1,0:T(8,128)S(1)}, u32[]{:S(2)}, u32[]{:S(2)}) collective-permute-start(f32[256,512]{1,0:T(8,128)S(1)} %broadcast_select_fusion.1), channel_id=1, source_target_pairs={{0,2},{4,6},{8,10},{12,14},{16,18},{20,22},{24,26},{28,30},{32,34}... | collective-permute-start | bytes 1572872 | tf_op jit(solution)/shard_map/rowpanel/ppermute | solution.py:17
  91.2 42.2 %collective-permute-start.7 = (f32[256,512]{1,0:T(8,128)}, f32[256,512]{1,0:T(8,128)}, u32[]{:S(2)}, u32[]{:S(2)}) collective-permute-start(f32[256,512]{1,0:T(8,128)} %broadcast_select_fusion.2), channel_id=1, source_target_pairs={{0,1},{2,3},{4,5},{6,7},{8,9},{10,11},{12,13},{14,15},{16,17},{18,... | collective-permute-start | bytes 1572872 | tf_op jit(solution)/shard_map/rowpanel/ppermute | solution.py:17
  130.1 0.9 copy-start.2
  133.4 2.2 %copy-start.1 = (f32[64,256]{1,0:T(8,128)S(1)}, f32[64,256]{1,0:T(8,128)}, u32[]{:S(2)}) copy-start(f32[64,256]{1,0:T(8,128)} %param.3) | copy-start | bytes 196612
Sparse Core Ops, SparseCore 0:
  81.5 61.0 all-gather.2

commit v3 on v2

v3 whole, which is shorter than its diff:
```python
import jax
import jax.numpy as jnp
from jax import lax
from jax.experimental import pallas as pl
from jax.experimental.pallas import tpu as pltpu
from jax.sharding import PartitionSpec as P

HI = lax.Precision.HIGHEST
SUB = 8
LANES = 128
VMEM = pl.BlockSpec(memory_space=pltpu.VMEM)


def dot(a, b):
    return jnp.dot(a, b, precision=HI, preferred_element_type=jnp.float32)


def dot_t(a, b):
    dims = (((1,), (1,)), ((), ()))
    return lax.dot_general(a, b, dims, precision=HI, preferred_element_type=jnp.float32)


def factor_tile(blocks):
    shape = (SUB, LANES)
    lane = lax.broadcasted_iota(jnp.int32, shape, 1)
    sub = lax.broadcasted_iota(jnp.int32, shape, 0)
    count = len(blocks)
    blocks = list(blocks)
    upper, inverse = [], []
    for b in range(count):
        base = b * SUB
        here = blocks[b]
        across = [jnp.broadcast_to(here[:, base + k : base + k + 1], shape) for k in range(SUB)]
        rows = [jnp.broadcast_to(here[k : k + 1, :], shape) for k in range(SUB)]
        s = {}
        for k in range(SUB):
            for i in range(k, SUB):
                s[i, k] = jnp.broadcast_to(across[k][i : i + 1, :], shape)
        rinv, low, u, w = [], {}, [], []
        for k in range(SUB):
            rinv.append(lax.rsqrt(s[k, k]))
            for i in range(k + 1, SUB):
                low[i, k] = s[i, k] * rinv[k]
            for j in range(k + 1, SUB):
                for i in range(j, SUB):
                    s[i, j] = s[i, j] - low[i, k] * low[j, k]
            uk = rows[k]
            wk = jnp.where(lane < base, rows[k], jnp.where(lane == base + k, 1.0, 0.0))
            for m in range(k):
                uk = uk - low[k, m] * u[m]
                wk = wk - low[k, m] * w[m]
            u.append(uk * rinv[k])
            w.append(wk * rinv[k])
        u_block, w_block = u[0], w[0]
        for k in range(1, SUB):
            u_block = jnp.where(sub == k, u[k], u_block)
            w_block = jnp.where(sub == k, w[k], w_block)
        upper.append(jnp.where(lane >= sub + base, u_block, 0.0))
        inverse.append(w_block)
        if b + 1 == count:
            break
        q = [None] * SUB
        for k in reversed(range(SUB)):
            v = jnp.where(lane < base + SUB, w[k], u[k])
            for m in range(k + 1, SUB):
                v = v - low[m, k] * q[m]
            q[k] = v * rinv[k]
        keep = (lane < base) | (lane >= base + SUB)
        for i in range(b + 1, count):
            old = blocks[i]
            terms = [
                jnp.broadcast_to(old[:, base + k : base + k + 1], shape) * q[k] for k in range(SUB)
            ]
            while len(terms) > 1:
                terms = [terms[t] + terms[t + 1] for t in range(0, len(terms), 2)]
            blocks[i] = jnp.where(keep, old, 0.0) - terms[0]
    return upper, inverse


def eliminate(work, low_ref, inv_ref, diag_ref):
    size = work.shape[0]
    row_id = lax.broadcasted_iota(jnp.int32, (size, LANES), 0)
    col_id = lax.broadcasted_iota(jnp.int32, (LANES, size), 1)
    square = (LANES, LANES)
    on_diag = lax.broadcasted_iota(jnp.int32, square, 0) == lax.broadcasted_iota(
        jnp.int32, square, 1
    )

    def step(t, carry):
        base = pl.multiple_of(t * LANES, LANES)
        tile_rows = pl.ds(base, LANES)
        here = [work[pl.ds(base + SUB * i, SUB), tile_rows] for i in range(LANES // SUB)]
        up, inv = factor_tile(here)
        up = jnp.concatenate(up, axis=0)
        inv = jnp.concatenate(inv, axis=0)
        diag_ref[pl.ds(t, 1), :] = jnp.sum(jnp.where(on_diag, up, 0.0), axis=0, keepdims=True)
        across = dot(inv, work[tile_rows, :])
        below = dot_t(work[:, tile_rows], inv)
        below = jnp.where(row_id >= base + LANES, below, 0.0)
        low_ref[:, tile_rows] = below
        low_ref[tile_rows, tile_rows] = up.T
        inv_ref[tile_rows, :] = jnp.where(col_id < base, across, 0.0)
        inv_ref[tile_rows, tile_rows] = inv
        work[tile_rows, :] = across
        work[tile_rows, tile_rows] = inv
        across = work[tile_rows, :]
        work[:, tile_rows] = jnp.zeros((size, LANES), jnp.float32)
        work[...] = work[...] - dot(below, across)
        return carry

    lax.fori_loop(0, size // LANES, step, 0)


def first_kernel(d0_ref, low_ref, inv_ref, diag_ref, work):
    work[...] = d0_ref[...]
    eliminate(work, low_ref, inv_ref, diag_ref)


def second_kernel(d1_ref, inv0_ref, low_ref, inv_ref, diag_ref, work, low_here, inv_here):
    tile = inv0_ref.shape[0]
    inv0 = inv0_ref[...]
    left = dot_t(d1_ref[:, :tile], inv0)
    low_ref[:, :tile] = left
    work[...] = d1_ref[:, tile:] - dot_t(left, left)
    eliminate(work, low_here, inv_here, diag_ref)
    low_ref[:, tile:] = low_here[...]
    inv1 = inv_here[...]
    inv_ref[:, tile:] = inv1
    inv_ref[:, :tile] = -dot(inv1, dot(low_ref[:, :tile], inv0))


def call(kernel, name, outs, scratch, *args):
    flops = 4 * 256**3
    return pl.pallas_call(
        kernel,
        out_shape=[jax.ShapeDtypeStruct(shape, jnp.float32) for shape in outs],
        in_specs=[VMEM] * len(args),
        out_specs=[VMEM] * len(outs),
        scratch_shapes=[pltpu.VMEM(shape, jnp.float32) for shape in scratch],
        compiler_params=pltpu.CompilerParams(vmem_limit_bytes=32 * 1024 * 1024),
        cost_estimate=pl.CostEstimate(flops=flops, bytes_accessed=40 * 2**20, transcendentals=0),
        name=name,
    )(*args)


def send(value, hop, holders, extent):
    pairs = [(z, (z + hop) % extent) for z in holders]
    return lax.ppermute(value, "col", pairs), [target for _, target in pairs]


def spread_step(value, hops, holders, extent, position):
    arrived, targets = None, []
    for hop in hops:
        moved, reached = send(value, hop, holders, extent)
        arrived = moved if arrived is None else arrived + moved
        targets += reached
    is_new = jnp.zeros((), bool)
    for target in targets:
        is_new = is_new | (position == target)
    return jnp.where(is_new, arrived, value), sorted(set(holders) | set(targets))


def shards(covariance, observations):
    tile, wide = covariance.shape
    nrhs = observations.shape[0]
    rows = lax.axis_size("row")
    cols = lax.axis_size("col")
    row = lax.axis_index("row")
    col = lax.axis_index("col")
    part = tile // rows
    half = part // 2

    with jax.named_scope("scatter"):
        got = lax.all_to_all(
            covariance.reshape(rows, part, wide), "row", split_axis=0, concat_axis=0, tiled=True
        )
        first, second = got[0], got[1]
        obs_got = lax.all_to_all(
            observations.reshape(rows, half, -1), "row", split_axis=0, concat_axis=0, tiled=True
        )
        obs_piece = jnp.concatenate([obs_got[0], obs_got[1]], axis=0)

    with jax.named_scope("diag"):
        piece = jnp.concatenate([first[:, :tile], second], axis=1)
        holders = [0]
        piece, holders = spread_step(piece, (5, -5), holders, cols, col)
        piece, holders = spread_step(piece, (2, -2), holders, cols, col)
        piece, holders = spread_step(piece, (1,), [z for z in holders if (z + 1) % cols not in holders], cols, col)

    with jax.named_scope("columns"):
        col_piece = jnp.concatenate([first, second, obs_piece], axis=1)
        col_sent = jnp.broadcast_to(col_piece[None], (rows,) + col_piece.shape)
        col_all = lax.all_to_all(col_sent, "row", split_axis=0, concat_axis=0, tiled=True)
        col0 = col_all[:, :, :wide].reshape(tile, wide)
        col1 = col_all[:, :, wide : 2 * wide].reshape(tile, wide)
        obs0 = col_all[:, :half, 2 * wide :].reshape(nrhs, tile)
        obs1 = col_all[:, half:, 2 * wide :].reshape(nrhs, tile)

    with jax.named_scope("diag"):
        panel, piece = lax.optimization_barrier((covariance, piece))
        sent = jnp.broadcast_to(piece[None], (rows,) + piece.shape)
        whole = lax.all_to_all(sent, "row", split_axis=0, concat_axis=0, tiled=True)
        diag0 = whole[:, :, :tile].reshape(tile, tile)
        diag1 = whole[:, :, tile:].reshape(tile, wide)

    with jax.named_scope("rowpanel"):
        holders = [0]
        panel, holders = spread_step(panel, (5, -5), holders, cols, col)
        diag0, panel = lax.optimization_barrier((diag0, panel))
        panel, holders = spread_step(panel, (2, -2), holders, cols, col)

    low0, inv0, dg0 = call(
        first_kernel, "factor_first", [(tile, tile), (tile, tile), (tile // LANES, LANES)],
        [(tile, tile)], diag0,
    )
    inv0, panel = lax.optimization_barrier((inv0, panel))
    with jax.named_scope("rowpanel"):
        panel, _ = spread_step(panel, (1,), [z for z in holders if (z + 1) % cols not in holders], cols, col)
    low1, inv1, dg1 = call(
        second_kernel, "factor_second", [(tile, wide), (tile, wide), (tile // LANES, LANES)],
        [(tile, tile)] * 3, diag1, inv0,
    )

    low1, inv1, dg1, panel = lax.optimization_barrier((low1, inv1, dg1, panel))

    with jax.named_scope("solve"):
        y0 = dot(inv0, col0)
        y1 = dot(inv1[:, :tile], col0) + dot(inv1[:, tile:], col1)
        z0 = dot_t(obs0, inv0)
        z1 = dot_t(obs0, inv1[:, :tile]) + dot_t(obs1, inv1[:, tile:])
        x0 = dot_t(panel[:, :tile], inv0)
        x1 = dot_t(panel, inv1)

    with jax.named_scope("update"):
        trail = covariance - dot(x0, y0) - dot(x1, y1)
        first_rows = jnp.where(row == 0, jnp.pad(low0, ((0, 0), (0, tile))), low1)
        edge = jnp.where(row <= 1, first_rows, jnp.concatenate([x0, x1], axis=1))
        other = jnp.where(row <= 1, 0.0, trail)
        factored = jnp.where(col == 0, edge, other)
        reduced = observations - dot_t(z0, x0) - dot_t(z1, x1)
        solved = jnp.where(row == 0, z0, jnp.where(row == 1, z1, reduced))

    with jax.named_scope("terms"):
        logdet = 2.0 * (jnp.sum(jnp.log(dg0)) + jnp.sum(jnp.log(dg1)))
        quad = jnp.sum(z0 * z0, axis=1) + jnp.sum(z1 * z1, axis=1)
        site_terms = -(quad + logdet) / (4.0 * tile)
    return factored, solved, site_terms


def solution(mesh):
    in_specs = (P("row", "col"), P(None, "row"))
    out_specs = (P("row", "col"), P(None, "row"), P())
    return jax.shard_map(shards, mesh=mesh, in_specs=in_specs, out_specs=out_specs, check_vma=False)
```

time: 155 us -> 144 us (0.929)
  blocking collectives: 0 us -> 22.2 us
  between operations: 15 us -> 2.35 us
  waiting for transfers between devices: 26.3 us -> 14.7 us
  starting transfers between devices: 59.7 us -> 48.6 us
  matrix products: 8.32 us -> 14.6 us
  local copies, waits for them, and re-layouts: 9.39 us -> 6.81 us
  Pallas kernels: 30.9 us -> 28.6 us
    all_to_all x0 -> x1, blocking collectives: none -> 22.2 us  [shards(): lax.all_to_all(covariance.reshape(rows, part, wide), 'row', split_axis=0,...]
    ppermute x8 -> x10, waiting for transfers between devices: 20.6 us -> 3.69 us  [send(): return (lax.ppermute(value, 'col', pairs), [target for _, target in pairs])]
    all_to_all x2 -> x3, waiting for transfers between devices: 0.01 us -> 11 us  [the longest x1 7.37 us: shards(): lax.all_to_all(observations.reshape(rows, half, -1), 'row', split_axis=0,...]
    dot_general x5 -> x12, matrix products: 8.32 us -> 14.6 us  [the longest x7 7.94 us: dot_t(): lax.dot_general(a, b, dims, precision=HI, preferred_element_type=jnp.floa...]
    ppermute x8 -> x10, starting transfers between devices: 41.3 us -> 35.1 us  [send(): return (lax.ppermute(value, 'col', pairs), [target for _, target in pairs])]
    all_gather x1 -> x0, waiting for transfers between devices: 5.73 us -> none  [shards(): col_all = lax.all_gather(col_piece, 'row', axis=0, tiled=False)]
    all_to_all x2 -> x3, starting transfers between devices: 18.4 us -> 13.5 us  [the longest x1 5.38 us: shards(): lax.all_to_all(observations.reshape(rows, half, -1), 'row', split_axis=0,...]
    gather x1 -> x0, local copies, waits for them, and re-layouts: 4.52 us -> none  [shards(): logdet = 2.0 * jnp.sum(jnp.log(jnp.diagonal(low)))]
  transfers between devices with their start and end apart: 11 -> 13, of which waited for: 5 -> 5; matrix products, arithmetic and copies ran while one was open for 10% -> 6% of each run, Pallas kernels for 20% -> 20%
where the time goes in v3:
time: 144 us; the launch traced here: 143 us
  starting transfers between devices  48.6 us (34%)
  Pallas kernels  28.6 us (20%)
  blocking collectives  22.2 us (15%)
  waiting for transfers between devices  14.7 us (10%)
  matrix products  14.6 us (10%)
  local copies, waits for them, and re-layouts  6.81 us (5%)
  other arithmetic  5.48 us (4%)
  between operations  2.35 us (2%)
    ppermute x10, starting transfers between devices, send(): return (lax.ppermute(value, 'col', pairs), [target for _, target in pairs])  35.1 us
    pallas_call x2, Pallas kernels, call(): pl.pallas_call(kernel, out_shape=[jax.ShapeDtypeStruct(shape, jnp.float32...  28.6 us
    all_to_all x1, blocking collectives, shards(): lax.all_to_all(covariance.reshape(rows, part, wide), 'row', split_axis=0,...  22.2 us
    dot_general x7, matrix products, dot_t(): lax.dot_general(a, b, dims, precision=HI, preferred_element_type=jnp.floa...  7.94 us
    all_to_all x1, waiting for transfers between devices, shards(): lax.all_to_all(observations.reshape(rows, half, -1), 'row', split_axis=0,...  7.37 us
    dot_general x5, matrix products, dot(): return jnp.dot(a, b, precision=HI, preferred_element_type=jnp.float32)  6.66 us
    all_to_all x1, starting transfers between devices, shards(): lax.all_to_all(observations.reshape(rows, half, -1), 'row', split_axis=0,...  5.38 us
    select_n x6, other arithmetic, spread_step(): jnp.where(is_new, arrived, value)  4.25 us
  transfers between devices with their start and end apart: 13, of which 5 were waited for; matrix products, arithmetic and copies ran while one was open for 6% of the time, Pallas kernels for 20%

profile of v3, /device:TPU:1, one launch (start us, length us, event | category | flops | bytes accessed | tf_op | source)
XLA Modules:
  0.0 143.4 jit_solution(12410339078427735869)
XLA Ops:
  0.6 22.2 %all_to_all.20 = f32[32,8,512]{2,1,0:T(8,128)S(1)} all-to-all(f32[32,8,512]{2,1,0:T(8,128)} %bitcast.36), channel_id=1, replica_groups=mesh['row'=32,'col'=16] {'row'}, dimensions={0} | all-to-all | bytes 1048576 | tf_op jit(solution)/shard_map/scatter/all_to_all | solution.py:174
  22.9 8.2 %collective-permute-start = (f32[8,768]{1,0:T(8,128)S(1)}, f32[8,768]{1,0:T(8,128)S(1)}, u32[]{:S(2)}, u32[]{:S(2)}) collective-permute-start(f32[8,768]{1,0:T(8,128)S(1)} %pad_maximum_fusion), channel_id=1, source_target_pairs={{0,5},{16,21},{32,37},{48,53},{64,69},{80,85},{96,101},{112,117},{... | collective-permute-start | bytes 73736 | tf_op jit(solution)/shard_map/diag/ppermute | solution.py:148
  31.1 4.6 %collective-permute-start.1 = (f32[8,768]{1,0:T(8,128)S(1)}, f32[8,768]{1,0:T(8,128)S(1)}, u32[]{:S(2)}, u32[]{:S(2)}) collective-permute-start(f32[8,768]{1,0:T(8,128)S(1)} %pad_maximum_fusion), channel_id=1, source_target_pairs={{0,11},{16,27},{32,43},{48,59},{64,75},{80,91},{96,107},{112,123},... | collective-permute-start | bytes 73736 | tf_op jit(solution)/shard_map/diag/ppermute | solution.py:148
  35.7 0.9 collective-permute-done.1
  36.7 1.3 collective-permute-start.2
  37.9 1.3 collective-permute-start.3
  39.3 0.9 collective-permute-done.3
  40.2 1.3 collective-permute-start.4
  41.5 0.7 reshape.35
  42.1 5.4 %all-to-all-start.2 = ((f32[32,4,128]{2,1,0:T(4,128)}), f32[32,4,128]{2,1,0:T(4,128)S(1)}, u32[]{:S(2)}, u32[]{:S(2)}) async-start(f32[32,4,128]{2,1,0:T(4,128)} %reshape.35), calls=%async_computation.2 | async-start | bytes 131072 | tf_op jit(solution)/shard_map/scatter/all_to_all | solution.py:178
  47.6 7.4 %all-to-all-done.2 = f32[32,4,128]{2,1,0:T(4,128)S(1)} async-done(((f32[32,4,128]{2,1,0:T(4,128)}), f32[32,4,128]{2,1,0:T(4,128)S(1)}, u32[]{:S(2)}, u32[]{:S(2)}) %all-to-all-start.2) | async-done | bytes 65568 | tf_op jit(solution)/shard_map/scatter/all_to_all | solution.py:178
  55.0 0.9 broadcast_in_dim.7
  55.9 4.0 %all-to-all-start.1 = ((f32[32,8,768]{2,1,0:T(8,128)}), f32[32,8,768]{2,1,0:T(8,128)S(1)}, u32[]{:S(2)}, u32[]{:S(2)}) async-start(f32[32,8,768]{2,1,0:T(8,128)} %broadcast_in_dim.7), calls=%async_computation.1 | async-start | bytes 1572864 | tf_op jit(solution)/shard_map/diag/all_to_all | solution.py:202
  59.9 4.2 %collective-permute-start.5 = (f32[256,512]{1,0:T(8,128)S(1)}, f32[256,512]{1,0:T(8,128)S(1)}, u32[]{:S(2)}, u32[]{:S(2)}) collective-permute-start(f32[256,512]{1,0:T(8,128)S(1)} %copy-done), channel_id=1, source_target_pairs={{0,5},{16,21},{32,37},{48,53},{64,69},{80,85},{96,101},{112,117},{... | collective-permute-start | bytes 1572872 | tf_op jit(solution)/shard_map/rowpanel/ppermute | solution.py:148
  64.1 6.5 %collective-permute-start.6 = (f32[256,512]{1,0:T(8,128)S(1)}, f32[256,512]{1,0:T(8,128)S(1)}, u32[]{:S(2)}, u32[]{:S(2)}) collective-permute-start(f32[256,512]{1,0:T(8,128)S(1)} %copy-done), channel_id=1, source_target_pairs={{0,11},{16,27},{32,43},{48,59},{64,75},{80,91},{96,107},{112,123},... | collective-permute-start | bytes 1572872 | tf_op jit(solution)/shard_map/rowpanel/ppermute | solution.py:148
  70.6 3.6 %all-to-all-done.1 = f32[32,8,768]{2,1,0:T(8,128)S(1)} async-done(((f32[32,8,768]{2,1,0:T(8,128)}), f32[32,8,768]{2,1,0:T(8,128)S(1)}, u32[]{:S(2)}, u32[]{:S(2)}) %all-to-all-start.1) | async-done | bytes 786464 | tf_op jit(solution)/shard_map/diag/all_to_all | solution.py:202
  74.2 1.2 broadcast_in_dim.18
  75.4 4.2 %all-to-all-start.3 = ((f32[32,8,1152]{2,1,0:T(8,128)}), f32[32,8,1152]{2,1,0:T(8,128)S(1)}, u32[]{:S(2)}, u32[]{:S(2)}) async-start(f32[32,8,1152]{2,1,0:T(8,128)} %broadcast_in_dim.18), calls=%async_computation.3 | async-start | bytes 2359296 | tf_op jit(solution)/shard_map/columns/all_to_all | solution.py:193
  79.6 1.9 %collective-permute-done.6 = f32[256,512]{1,0:T(8,128)S(1)} collective-permute-done((f32[256,512]{1,0:T(8,128)S(1)}, f32[256,512]{1,0:T(8,128)S(1)}, u32[]{:S(2)}, u32[]{:S(2)}) %collective-permute-start.6) | collective-permute-done | bytes 524320 | tf_op jit(solution)/shard_map/rowpanel/ppermute | solution.py:148
  81.5 0.9 add_select_fusion.1
  82.4 1.3 collective-permute-start.7
  83.8 4.3 %collective-permute-start.8 = (f32[256,512]{1,0:T(8,128)}, f32[256,512]{1,0:T(8,128)}, u32[]{:S(2)}, u32[]{:S(2)}) collective-permute-start(f32[256,512]{1,0:T(8,128)} %add_select_fusion.1), channel_id=1, source_target_pairs={{0,14},{5,3},{11,9},{16,30},{21,19},{27,25},{32,46},{37,35},{43,41... | collective-permute-start | bytes 1572872 | tf_op jit(solution)/shard_map/rowpanel/ppermute | solution.py:148
  88.1 13.2 %factor_first.1 = (f32[256,256]{1,0:T(8,128)S(1)}, f32[256,256]{1,0:T(8,128)S(1)}, f32[2,128]{1,0:T(2,128)S(1)}) custom-call(f32[256,256]{1,0:T(8,128)S(1)} %slice_bitcast_fusion.6.d0_ref), custom_call_target="tpu_custom_call" | custom-call | flops 67108864 | bytes 41943040 | tf_op jit(solution)/shard_map/factor_first/pallas_call | solution.py:134
  101.3 1.1 slice_bitcast_fusion.3.d1_ref
  102.4 2.2 %add_select_fusion = f32[256,512]{1,0:T(8,128)} fusion(f32[256,512]{1,0:T(8,128)} %add_select_fusion.1, f32[256,512]{1,0:T(8,128)S(1)} %collective-permute-done.7, f32[256,512]{1,0:T(8,128)} %collective-permute-done.8, pred[]{:T(512)S(6)} %or.58), kind=kLoop, calls=%fused_computation.14 | loop fusion | flops 262144 | bytes 2097153 | tf_op jit(solution)/shard_map/rowpanel/jit(_where)/select_n | solution.py:160
  104.6 2.1 %collective-permute-start.9 = (f32[256,512]{1,0:T(8,128)}, f32[256,512]{1,0:T(8,128)}, u32[]{:S(2)}, u32[]{:S(2)}) collective-permute-start(f32[256,512]{1,0:T(8,128)} %add_select_fusion), channel_id=1, source_target_pairs={{0,1},{3,4},{5,6},{7,8},{9,10},{11,12},{14,15},{16,17},{19,20},{21... | collective-permute-start | bytes 1572872 | tf_op jit(solution)/shard_map/rowpanel/ppermute | solution.py:148
  106.7 0.7 reshape.39
  107.4 15.4 %factor_second.1 = (f32[256,512]{1,0:T(8,128)S(1)}, f32[256,512]{1,0:T(8,128)S(1)}, f32[2,128]{1,0:T(2,128)S(1)}) custom-call(f32[256,512]{1,0:T(8,128)S(1)} %slice_bitcast_fusion.3.d1_ref, f32[256,256]{1,0:T(8,128)S(1)} %get-tuple-element.25.inv0_ref), custom_call_target="tpu_custom_call" | custom-call | flops 67108864 | bytes 41943040 | tf_op jit(solution)/shard_map/factor_second/pallas_call | solution.py:134
  122.8 1.1 multiply_reduce_fusion.1
  123.9 1.4 fusion.5
  125.3 1.1 broadcast_select_fusion
  126.5 1.0 fusion.10
  127.5 0.4 fusion.6
  127.9 0.6 fusion.14
  128.5 0.8 copy.5
  129.3 1.7 %convolution_subtract_fusion.3 = f32[64,256]{1,0:T(8,128)} fusion(f32[64,256]{1,0:T(8,128)} %param.3, f32[64,256]{1,0:T(8,128)} %get-tuple-element.42, f32[256,256]{0,1:T(8,128)S(1)} %fusion.6), kind=kOutput, calls=%fused_computation.8 | convolution fusion | flops 50348032 | bytes 458752 | tf_op jit(solution)/shard_map/update/dot_general | solution.py:20
  131.1 0.8 copy.6
  131.9 2.5 %convolution_subtract_fusion.1 = f32[256,512]{1,0:T(8,128)} fusion(f32[256,512]{1,0:T(8,128)S(1)} %copy-done.1, f32[256,256]{0,1:T(8,128)S(1)} %fusion.6, f32[256,512]{1,0:T(8,128)} %fusion.5), kind=kOutput, calls=%fused_computation.4 | convolution fusion | flops 402784256 | bytes 1835008 | tf_op jit(solution)/shard_map/update/dot_general | solution.py:15
  134.4 0.7 log_reduce_fusion
  136.4 1.3 multiply_reduce_fusion
  137.8 0.5 negate_multiply_fusion
  138.3 1.7 %fusion.3 = f32[64,256]{1,0:T(8,128)} fusion(f32[64,256]{1,0:T(8,128)} %get-tuple-element.42, f32[64,256]{1,0:T(8,128)S(1)} %get-tuple-element.44, f32[64,256]{1,0:T(8,128)} %convolution_subtract_fusion.3, f32[256,256]{0,1:T(8,128)S(1)} %fusion.14, pred[]{:T(512)S(6)} %eq.87, pred[]{:T(512)S(6)} %eq.71), kind=kOutput, calls=%fused_computation.7 | convolution fusion | flops 50380800 | bytes 524290 | tf_op jit(solution)/shard_map/update/dot_general | solution.py:20
  140.1 0.6 fusion.4
  140.7 0.6 convolution_add_fusion
  141.3 0.4 copy-done.3
  141.7 0.1 copy-done.4
  141.8 0.1 copy-done.5
  141.9 1.5 %fusion.1 = f32[256,512]{1,0:T(8,128)} fusion(f32[256,512]{1,0:T(8,128)S(1)} %copy-done.3, f32[256,256]{0,1:T(8,128)S(1)} %fusion.14, f32[256,512]{1,0:T(8,128)S(1)} %convolution_add_fusion, f32[256,256]{1,0:T(8,128)S(1)} %copy-done.5, f32[256,256]{1,0:T(8,128)S(1)} %copy-done.4, f32[256,512]{1,0:T(8,128)S(1)} %get-tuple-element.30, ...), kind=kOutput, calls=%fused_computation.2 | convolution fusion | flops 403439616 | bytes 3145731 | tf_op jit(solution)/shard_map/update/dot_general | solution.py:15
  (30 shorter events, 0.2 us)
Async XLA Ops:
  0.6 40.8 %copy-start.6 = (f32[64,256]{1,0:T(8,128)S(1)}, f32[64,256]{1,0:T(8,128)}, u32[]{:S(2)}) copy-start(f32[64,256]{1,0:T(8,128)} %param.3) | copy-start | bytes 196612
  22.9 12.9 %collective-permute-start = (f32[8,768]{1,0:T(8,128)S(1)}, f32[8,768]{1,0:T(8,128)S(1)}, u32[]{:S(2)}, u32[]{:S(2)}) collective-permute-start(f32[8,768]{1,0:T(8,128)S(1)} %pad_maximum_fusion), channel_id=1, source_target_pairs={{0,5},{16,21},{32,37},{48,53},{64,69},{80,85},{96,101},{112,117},{... | collective-permute-start | bytes 73736 | tf_op jit(solution)/shard_map/diag/ppermute | solution.py:148
  31.1 5.5 %collective-permute-start.1 = (f32[8,768]{1,0:T(8,128)S(1)}, f32[8,768]{1,0:T(8,128)S(1)}, u32[]{:S(2)}, u32[]{:S(2)}) collective-permute-start(f32[8,768]{1,0:T(8,128)S(1)} %pad_maximum_fusion), channel_id=1, source_target_pairs={{0,11},{16,27},{32,43},{48,59},{64,75},{80,91},{96,107},{112,123},... | collective-permute-start | bytes 73736 | tf_op jit(solution)/shard_map/diag/ppermute | solution.py:148
  36.7 2.6 %collective-permute-start.2 = (f32[8,768]{1,0:T(8,128)S(1)}, f32[8,768]{1,0:T(8,128)S(1)}, u32[]{:S(2)}, u32[]{:S(2)}) collective-permute-start(f32[8,768]{1,0:T(8,128)S(1)} %add_select_fusion.3), channel_id=1, source_target_pairs={{0,2},{5,7},{11,13},{16,18},{21,23},{27,29},{32,34},{37,39},{43,45... | collective-permute-start | bytes 73736 | tf_op jit(solution)/shard_map/diag/ppermute | solution.py:148
  37.9 2.2 %collective-permute-start.3 = (f32[8,768]{1,0:T(8,128)S(1)}, f32[8,768]{1,0:T(8,128)S(1)}, u32[]{:S(2)}, u32[]{:S(2)}) collective-permute-start(f32[8,768]{1,0:T(8,128)S(1)} %add_select_fusion.3), channel_id=1, source_target_pairs={{0,14},{5,3},{11,9},{16,30},{21,19},{27,25},{32,46},{37,35},{43,41... | collective-permute-start | bytes 73736 | tf_op jit(solution)/shard_map/diag/ppermute | solution.py:148
  40.2 7.4 %collective-permute-start.4 = (f32[8,768]{1,0:T(8,128)S(1)}, f32[8,768]{1,0:T(8,128)S(1)}, u32[]{:S(2)}, u32[]{:S(2)}) collective-permute-start(f32[8,768]{1,0:T(8,128)S(1)} %add_select_fusion.2), channel_id=1, source_target_pairs={{0,1},{3,4},{5,6},{7,8},{9,10},{11,12},{14,15},{16,17},{19,20},{21... | collective-permute-start | bytes 73736 | tf_op jit(solution)/shard_map/diag/ppermute | solution.py:148
  42.1 12.8 %all-to-all-start.2 = ((f32[32,4,128]{2,1,0:T(4,128)}), f32[32,4,128]{2,1,0:T(4,128)S(1)}, u32[]{:S(2)}, u32[]{:S(2)}) async-start(f32[32,4,128]{2,1,0:T(4,128)} %reshape.35), calls=%async_computation.2 | async-start | bytes 131072 | tf_op jit(solution)/shard_map/scatter/all_to_all | solution.py:178
  47.6 12.3 %copy-start = (f32[256,512]{1,0:T(8,128)S(1)}, f32[256,512]{1,0:T(8,128)}, u32[]{:S(2)}) copy-start(f32[256,512]{1,0:T(8,128)} %param.2) | copy-start | bytes 1572868
  55.9 18.3 %all-to-all-start.1 = ((f32[32,8,768]{2,1,0:T(8,128)}), f32[32,8,768]{2,1,0:T(8,128)S(1)}, u32[]{:S(2)}, u32[]{:S(2)}) async-start(f32[32,8,768]{2,1,0:T(8,128)} %broadcast_in_dim.7), calls=%async_computation.1 | async-start | bytes 1572864 | tf_op jit(solution)/shard_map/diag/all_to_all | solution.py:202
  59.9 19.7 %collective-permute-start.5 = (f32[256,512]{1,0:T(8,128)S(1)}, f32[256,512]{1,0:T(8,128)S(1)}, u32[]{:S(2)}, u32[]{:S(2)}) collective-permute-start(f32[256,512]{1,0:T(8,128)S(1)} %copy-done), channel_id=1, source_target_pairs={{0,5},{16,21},{32,37},{48,53},{64,69},{80,85},{96,101},{112,117},{... | collective-permute-start | bytes 1572872 | tf_op jit(solution)/shard_map/rowpanel/ppermute | solution.py:148
  64.1 17.4 %collective-permute-start.6 = (f32[256,512]{1,0:T(8,128)S(1)}, f32[256,512]{1,0:T(8,128)S(1)}, u32[]{:S(2)}, u32[]{:S(2)}) collective-permute-start(f32[256,512]{1,0:T(8,128)S(1)} %copy-done), channel_id=1, source_target_pairs={{0,11},{16,27},{32,43},{48,59},{64,75},{80,91},{96,107},{112,123},... | collective-permute-start | bytes 1572872 | tf_op jit(solution)/shard_map/rowpanel/ppermute | solution.py:148
  74.2 8.2 %copy-start.2 = (f32[32,8,768]{2,1,0:T(8,128)}, f32[32,8,768]{2,1,0:T(8,128)S(1)}, u32[]{:S(2)}) copy-start(f32[32,8,768]{2,1,0:T(8,128)S(1)} %all-to-all-done.1) | copy-start | bytes 2359300
  75.4 31.3 %all-to-all-start.3 = ((f32[32,8,1152]{2,1,0:T(8,128)}), f32[32,8,1152]{2,1,0:T(8,128)S(1)}, u32[]{:S(2)}, u32[]{:S(2)}) async-start(f32[32,8,1152]{2,1,0:T(8,128)} %broadcast_in_dim.18), calls=%async_computation.3 | async-start | bytes 2359296 | tf_op jit(solution)/shard_map/columns/all_to_all | solution.py:193
  82.4 20.0 %collective-permute-start.7 = (f32[256,512]{1,0:T(8,128)}, f32[256,512]{1,0:T(8,128)S(1)}, u32[]{:S(2)}, u32[]{:S(2)}) collective-permute-start(f32[256,512]{1,0:T(8,128)} %add_select_fusion.1), channel_id=1, source_target_pairs={{0,2},{5,7},{11,13},{16,18},{21,23},{27,29},{32,34},{37,39},{43,45... | collective-permute-start | bytes 1572872 | tf_op jit(solution)/shard_map/rowpanel/ppermute | solution.py:148
  83.8 18.6 %collective-permute-start.8 = (f32[256,512]{1,0:T(8,128)}, f32[256,512]{1,0:T(8,128)}, u32[]{:S(2)}, u32[]{:S(2)}) collective-permute-start(f32[256,512]{1,0:T(8,128)} %add_select_fusion.1), channel_id=1, source_target_pairs={{0,14},{5,3},{11,9},{16,30},{21,19},{27,25},{32,46},{37,35},{43,41... | collective-permute-start | bytes 1572872 | tf_op jit(solution)/shard_map/rowpanel/ppermute | solution.py:148
  104.6 20.8 %collective-permute-start.9 = (f32[256,512]{1,0:T(8,128)}, f32[256,512]{1,0:T(8,128)}, u32[]{:S(2)}, u32[]{:S(2)}) collective-permute-start(f32[256,512]{1,0:T(8,128)} %add_select_fusion), channel_id=1, source_target_pairs={{0,1},{3,4},{5,6},{7,8},{9,10},{11,12},{14,15},{16,17},{19,20},{21... | collective-permute-start | bytes 1572872 | tf_op jit(solution)/shard_map/rowpanel/ppermute | solution.py:148
  127.9 4.0 %copy-start.1 = (f32[256,512]{1,0:T(8,128)S(1)}, f32[256,512]{1,0:T(8,128)}, u32[]{:S(2)}) copy-start(f32[256,512]{1,0:T(8,128)} %param.2) | copy-start | bytes 1572868
  140.7 1.0 copy-start.3
  140.7 1.1 copy-start.4
  140.7 1.2 copy-start.5

commit v4 on v3

--- a/solution.py
+++ b/solution.py
@@ -111,17 +111,18 @@
     lax.fori_loop(0, size // LANES, step, 0)
 
 
-def first_kernel(d0_ref, low_ref, inv_ref, diag_ref, work):
-    work[...] = d0_ref[...]
+def first_kernel(d_ref, low_ref, inv_ref, diag_ref, work):
+    tile = work.shape[0]
+    work[...] = d_ref[:, :tile]
     eliminate(work, low_ref, inv_ref, diag_ref)
 
 
-def second_kernel(d1_ref, inv0_ref, low_ref, inv_ref, diag_ref, work, low_here, inv_here):
+def second_kernel(d_ref, inv0_ref, low_ref, inv_ref, diag_ref, work, low_here, inv_here):
     tile = inv0_ref.shape[0]
     inv0 = inv0_ref[...]
-    left = dot_t(d1_ref[:, :tile], inv0)
+    left = dot_t(d_ref[:, tile : 2 * tile], inv0)
     low_ref[:, :tile] = left
-    work[...] = d1_ref[:, tile:] - dot_t(left, left)
+    work[...] = d_ref[:, 2 * tile : 3 * tile] - dot_t(left, left)
     eliminate(work, low_here, inv_here, diag_ref)
     low_ref[:, tile:] = low_here[...]
     inv1 = inv_here[...]
@@ -129,15 +130,82 @@
     inv_ref[:, :tile] = -dot(inv1, dot(low_ref[:, :tile], inv0))
 
 
-def call(kernel, name, outs, scratch, *args):
+def finish_kernel(
+    ids_ref, panel_ref, moved_ref, wide_ref, low0_ref, inv0_ref, diag0_ref, low1_ref, inv1_ref,
+    diag1_ref, cov_ref, obs_ref, out_ref, solved_ref, site_ref, rows_here,
+):
+    tile, wide = cov_ref.shape
+    nrhs = obs_ref.shape[0]
+    row, col, is_new = ids_ref[0], ids_ref[1], ids_ref[2]
+    inv0 = inv0_ref[...]
+    inv10 = inv1_ref[:, :tile]
+    inv11 = inv1_ref[:, tile:]
+
+    rows_here[...] = panel_ref[...]
+
+    @pl.when(is_new == 1)
+    def _():
+        rows_here[...] = moved_ref[...]
+
+    obs_both = wide_ref[:, 2 * wide : 2 * wide + 2 * nrhs]
+    z0 = dot(inv0, obs_both)[:, :nrhs]
+    z1 = dot(inv10, obs_both)[:, :nrhs] + dot(inv11, obs_both)[:, nrhs:]
+    quad = jnp.sum(z0 * z0 + z1 * z1, axis=0, keepdims=True)
+    logs = jnp.log(diag0_ref[...]) + jnp.log(diag1_ref[...])
+    site_ref[...] = -(quad + 2.0 * jnp.sum(logs)) / (4.0 * tile)
+
+    @pl.when(row == 0)
+    def _():
+        solved_ref[...] = z0.T
+
+    @pl.when(row == 1)
+    def _():
+        solved_ref[...] = z1.T
+
+    @pl.when(row <= 1)
+    def _():
+        out_ref[...] = jnp.zeros((tile, wide), jnp.float32)
+
+    @pl.when((row == 0) & (col == 0))
+    def _():
+        out_ref[:, :tile] = low0_ref[...]
+
+    @pl.when((row == 1) & (col == 0))
+    def _():
+        out_ref[...] = low1_ref[...]
+
+    @pl.when(row > 1)
+    def _():
+        x0 = dot_t(rows_here[:, :tile], inv0)
+        x1 = dot_t(rows_here[...], inv1_ref[...])
+        solved_ref[...] = obs_ref[...] - (dot(x0, z0) + dot(x1, z1)).T
+
+        @pl.when(col == 0)
+        def _():
+            out_ref[:, :tile] = x0
+            out_ref[:, tile:] = x1
+
+        @pl.when(col > 0)
+        def _():
+            c0 = wide_ref[:, :wide]
+            y0 = dot(inv0, c0)
+            y1 = dot(inv10, c0) + dot(inv11, wide_ref[:, wide : 2 * wide])
+            out_ref[...] = cov_ref[...] - dot(x0, y0) - dot(x1, y1)
+
+
+def call(kernel, name, outs, scratch, *args, ids=None):
     flops = 4 * 256**3
+    specs = [VMEM] * len(args)
+    if ids is not None:
+        specs = [pl.BlockSpec(memory_space=pltpu.SMEM)] + specs
+        args = (ids,) + args
     return pl.pallas_call(
         kernel,
         out_shape=[jax.ShapeDtypeStruct(shape, jnp.float32) for shape in outs],
-        in_specs=[VMEM] * len(args),
+        in_specs=specs,
         out_specs=[VMEM] * len(outs),
         scratch_shapes=[pltpu.VMEM(shape, jnp.float32) for shape in scratch],
-        compiler_params=pltpu.CompilerParams(vmem_limit_bytes=32 * 1024 * 1024),
+        compiler_params=pltpu.CompilerParams(vmem_limit_bytes=40 * 1024 * 1024),
         cost_estimate=pl.CostEstimate(flops=flops, bytes_accessed=40 * 2**20, transcendentals=0),
         name=name,
     )(*args)
@@ -168,83 +236,63 @@
     row = lax.axis_index("row")
     col = lax.axis_index("col")
     part = tile // rows
-    half = part // 2
+
+    def exchange(value):
+        return lax.all_to_all(value, "row", split_axis=0, concat_axis=0, tiled=True)
 
     with jax.named_scope("scatter"):
-        got = lax.all_to_all(
-            covariance.reshape(rows, part, wide), "row", split_axis=0, concat_axis=0, tiled=True
-        )
+        got = exchange(covariance.reshape(rows, part, wide))
         first, second = got[0], got[1]
-        obs_got = lax.all_to_all(
-            observations.reshape(rows, half, -1), "row", split_axis=0, concat_axis=0, tiled=True
-        )
-        obs_piece = jnp.concatenate([obs_got[0], obs_got[1]], axis=0)
+        obs_parts = jnp.pad(observations.T, ((0, 0), (0, LANES - nrhs))).reshape(rows, part, LANES)
 
     with jax.named_scope("diag"):
         piece = jnp.concatenate([first[:, :tile], second], axis=1)
         holders = [0]
         piece, holders = spread_step(piece, (5, -5), holders, cols, col)
         piece, holders = spread_step(piece, (2, -2), holders, cols, col)
-        piece, holders = spread_step(piece, (1,), [z for z in holders if (z + 1) % cols not in holders], cols, col)
-
-    with jax.named_scope("columns"):
-        col_piece = jnp.concatenate([first, second, obs_piece], axis=1)
-        col_sent = jnp.broadcast_to(col_piece[None], (rows,) + col_piece.shape)
-        col_all = lax.all_to_all(col_sent, "row", split_axis=0, concat_axis=0, tiled=True)
-        col0 = col_all[:, :, :wide].reshape(tile, wide)
-        col1 = col_all[:, :, wide : 2 * wide].reshape(tile, wide)
-        obs0 = col_all[:, :half, 2 * wide :].reshape(nrhs, tile)
-        obs1 = col_all[:, half:, 2 * wide :].reshape(nrhs, tile)
-
-    with jax.named_scope("diag"):
+        last = [z for z in holders if (z + 1) % cols not in holders]
+        piece, _ = spread_step(piece, (1,), last, cols, col)
         panel, piece = lax.optimization_barrier((covariance, piece))
         sent = jnp.broadcast_to(piece[None], (rows,) + piece.shape)
-        whole = lax.all_to_all(sent, "row", split_axis=0, concat_axis=0, tiled=True)
-        diag0 = whole[:, :, :tile].reshape(tile, tile)
-        diag1 = whole[:, :, tile:].reshape(tile, wide)
+        whole = exchange(jnp.concatenate([sent, obs_parts], axis=2))
+        diag = whole.reshape(tile, -1)
+
+    with jax.named_scope("columns"):
+        start = 3 * tile
+        col_piece = jnp.concatenate(
+            [first, second, whole[0, :, start : start + nrhs], whole[1, :, start : start + nrhs]],
+            axis=1,
+        )
+        columns = exchange(jnp.broadcast_to(col_piece[None], (rows,) + col_piece.shape))
+        columns = columns.reshape(tile, -1)
 
     with jax.named_scope("rowpanel"):
-        holders = [0]
-        panel, holders = spread_step(panel, (5, -5), holders, cols, col)
-        diag0, panel = lax.optimization_barrier((diag0, panel))
+        panel, holders = spread_step(panel, (5, -5), [0], cols, col)
+        diag, panel = lax.optimization_barrier((diag, panel))
         panel, holders = spread_step(panel, (2, -2), holders, cols, col)
 
-    low0, inv0, dg0 = call(
+    low0, inv0, diag0 = call(
         first_kernel, "factor_first", [(tile, tile), (tile, tile), (tile // LANES, LANES)],
-        [(tile, tile)], diag0,
+        [(tile, tile)], diag,
     )
     inv0, panel = lax.optimization_barrier((inv0, panel))
     with jax.named_scope("rowpanel"):
-        panel, _ = spread_step(panel, (1,), [z for z in holders if (z + 1) % cols not in holders], cols, col)
-    low1, inv1, dg1 = call(
+        moved, reached = send(panel, 1, last, cols)
+    low1, inv1, diag1 = call(
         second_kernel, "factor_second", [(tile, wide), (tile, wide), (tile // LANES, LANES)],
-        [(tile, tile)] * 3, diag1, inv0,
+        [(tile, tile)] * 3, diag, inv0,
     )
 
-    low1, inv1, dg1, panel = lax.optimization_barrier((low1, inv1, dg1, panel))
-
-    with jax.named_scope("solve"):
-        y0 = dot(inv0, col0)
-        y1 = dot(inv1[:, :tile], col0) + dot(inv1[:, tile:], col1)
-        z0 = dot_t(obs0, inv0)
-        z1 = dot_t(obs0, inv1[:, :tile]) + dot_t(obs1, inv1[:, tile:])
-        x0 = dot_t(panel[:, :tile], inv0)
-        x1 = dot_t(panel, inv1)
-
-    with jax.named_scope("update"):
-        trail = covariance - dot(x0, y0) - dot(x1, y1)
-        first_rows = jnp.where(row == 0, jnp.pad(low0, ((0, 0), (0, tile))), low1)
-        edge = jnp.where(row <= 1, first_rows, jnp.concatenate([x0, x1], axis=1))
-        other = jnp.where(row <= 1, 0.0, trail)
-        factored = jnp.where(col == 0, edge, other)
-        reduced = observations - dot_t(z0, x0) - dot_t(z1, x1)
-        solved = jnp.where(row == 0, z0, jnp.where(row == 1, z1, reduced))
-
-    with jax.named_scope("terms"):
-        logdet = 2.0 * (jnp.sum(jnp.log(dg0)) + jnp.sum(jnp.log(dg1)))
-        quad = jnp.sum(z0 * z0, axis=1) + jnp.sum(z1 * z1, axis=1)
-        site_terms = -(quad + logdet) / (4.0 * tile)
-    return factored, solved, site_terms
+    is_new = jnp.zeros((), bool)
+    for target in reached:
+        is_new = is_new | (col == target)
+    ids = jnp.stack([row, col, is_new.astype(jnp.int32)])
+    factored, solved, site = call(
+        finish_kernel, "finish", [(tile, wide), (nrhs, tile), (1, nrhs)], [(tile, wide)],
+        panel, moved, columns, low0, inv0, diag0, low1, inv1, diag1, covariance, observations,
+        ids=ids,
+    )
+    return factored, solved, site.reshape(nrhs)
 
 
 def solution(mesh):

time: 144 us -> 128 us (0.89); the launches traced: 143 us -> 126 us
  matrix products: 14.6 us -> 0 us
  Pallas kernels: 28.6 us -> 31.6 us
  other arithmetic: 5.48 us -> 2.62 us
  between operations: 2.35 us -> 0.9 us
    dot_general x12 -> x0, matrix products: 14.6 us -> none  [the longest x7 7.94 us: dot_t(): lax.dot_general(a, b, dims, precision=HI, preferred_element_type=jnp.floa...]
    all_to_all x3 -> x2, waiting for transfers between devices: 11 us -> 0.01 us  [exchange(): return lax.all_to_all(value, 'row', split_axis=0, concat_axis=0, tiled=True)]
    ppermute x10, waiting for transfers between devices: 3.69 us -> 13.5 us  [send(): return (lax.ppermute(value, 'col', pairs), [target for _, target in pairs])]
    unnamed x14 -> x21, local copies, waits for them, and re-layouts: 0.55 us -> 5.41 us
    pallas_call x2 -> x3, Pallas kernels: 28.6 us -> 31.6 us  [call(): pl.pallas_call(kernel, out_shape=[jax.ShapeDtypeStruct(shape, jnp.float32...]
    select_n x6 -> x5, other arithmetic: 4.25 us -> 1.52 us  [spread_step(): jnp.where(is_new, arrived, value)]
    reshape x5 -> x1, local copies, waits for them, and re-layouts: 2.44 us -> 0.01 us  [shards(): jnp.pad(observations.T, ((0, 0), (0, LANES - nrhs)))]
    dot_general x2 -> x0, local copies, waits for them, and re-layouts: 1.66 us -> none  [dot_t(): lax.dot_general(a, b, dims, precision=HI, preferred_element_type=jnp.floa...]
  transfers between devices with their start and end apart: 13 -> 12, of which waited for: 5 -> 5; matrix products, arithmetic and copies ran while one was open for 6% -> 2% of each run, Pallas kernels for 20% -> 23%
where the time goes in v4:
time: 128 us; the launch traced here: 126 us
  starting transfers between devices  48.1 us (38%)
  Pallas kernels  31.6 us (25%)
  blocking collectives  22.2 us (17%)
  waiting for transfers between devices  13.5 us (11%)
  local copies, waits for them, and re-layouts  6.69 us (5%)
  other arithmetic  2.62 us (2%)
    ppermute x10, starting transfers between devices, send(): return (lax.ppermute(value, 'col', pairs), [target for _, target in pairs])  33.6 us
    pallas_call x3, Pallas kernels, call(): pl.pallas_call(kernel, out_shape=[jax.ShapeDtypeStruct(shape, jnp.float32...  31.6 us
    all_to_all x1, blocking collectives, exchange(): return lax.all_to_all(value, 'row', split_axis=0, concat_axis=0, tiled=True)  22.2 us
    all_to_all x2, starting transfers between devices, exchange(): return lax.all_to_all(value, 'row', split_axis=0, concat_axis=0, tiled=True)  14.5 us
    ppermute x10, waiting for transfers between devices, send(): return (lax.ppermute(value, 'col', pairs), [target for _, target in pairs])  13.5 us
    unnamed x21, local copies, waits for them, and re-layouts  5.41 us
  transfers between devices with their start and end apart: 12, of which 5 were waited for; matrix products, arithmetic and copies ran while one was open for 2% of the time, Pallas kernels for 23%

profile of v4, /device:TPU:1, one launch (start us, length us, event | category | flops | bytes accessed | tf_op | source)
XLA Modules:
  0.0 125.6 jit_solution(4345496705107266062)
XLA Ops:
  0.6 0.0 copy-start.5
  0.6 22.2 %all_to_all.15 = f32[32,8,512]{2,1,0:T(8,128)S(1)} all-to-all(f32[32,8,512]{2,1,0:T(8,128)} %bitcast.21), channel_id=1, replica_groups=mesh['row'=32,'col'=16] {'row'}, dimensions={0} | all-to-all | bytes 1048576 | tf_op jit(solution)/shard_map/scatter/all_to_all | solution.py:241
  22.9 8.2 %collective-permute-start = (f32[8,768]{1,0:T(8,128)S(1)}, f32[8,768]{1,0:T(8,128)S(1)}, u32[]{:S(2)}, u32[]{:S(2)}) collective-permute-start(f32[8,768]{1,0:T(8,128)S(1)} %pad_maximum_fusion.1), channel_id=1, source_target_pairs={{0,5},{16,21},{32,37},{48,53},{64,69},{80,85},{96,101},{112,117},{... | collective-permute-start | bytes 73736 | tf_op jit(solution)/shard_map/diag/ppermute | solution.py:216
  31.1 4.6 %collective-permute-start.1 = (f32[8,768]{1,0:T(8,128)S(1)}, f32[8,768]{1,0:T(8,128)S(1)}, u32[]{:S(2)}, u32[]{:S(2)}) collective-permute-start(f32[8,768]{1,0:T(8,128)S(1)} %pad_maximum_fusion.1), channel_id=1, source_target_pairs={{0,11},{16,27},{32,43},{48,59},{64,75},{80,91},{96,107},{112,123},... | collective-permute-start | bytes 73736 | tf_op jit(solution)/shard_map/diag/ppermute | solution.py:216
  35.7 0.0 collective-permute-done
  35.7 0.9 collective-permute-done.1
  36.7 1.3 %collective-permute-start.2 = (f32[8,768]{1,0:T(8,128)S(1)}, f32[8,768]{1,0:T(8,128)S(1)}, u32[]{:S(2)}, u32[]{:S(2)}) collective-permute-start(f32[8,768]{1,0:T(8,128)S(1)} %add_select_fusion.3), channel_id=1, source_target_pairs={{0,2},{5,7},{11,13},{16,18},{21,23},{27,29},{32,34},{37,39},{43,45... | collective-permute-start | bytes 73736 | tf_op jit(solution)/shard_map/diag/ppermute | solution.py:216
  37.9 1.3 %collective-permute-start.3 = (f32[8,768]{1,0:T(8,128)S(1)}, f32[8,768]{1,0:T(8,128)S(1)}, u32[]{:S(2)}, u32[]{:S(2)}) collective-permute-start(f32[8,768]{1,0:T(8,128)S(1)} %add_select_fusion.3), channel_id=1, source_target_pairs={{0,14},{5,3},{11,9},{16,30},{21,19},{27,25},{32,46},{37,35},{43,41... | collective-permute-start | bytes 73736 | tf_op jit(solution)/shard_map/diag/ppermute | solution.py:216
  39.2 0.0 copy-done.5
  39.3 0.1 copy.6
  39.4 0.0 collective-permute-done.2
  39.4 0.8 collective-permute-done.3
  40.2 1.3 %collective-permute-start.4 = (f32[8,768]{1,0:T(8,128)S(1)}, f32[8,768]{1,0:T(8,128)S(1)}, u32[]{:S(2)}, u32[]{:S(2)}) collective-permute-start(f32[8,768]{1,0:T(8,128)S(1)} %add_select_fusion.2), channel_id=1, source_target_pairs={{0,1},{3,4},{5,6},{7,8},{9,10},{11,12},{14,15},{16,17},{19,20},{21... | collective-permute-start | bytes 73736 | tf_op jit(solution)/shard_map/diag/ppermute | solution.py:216
  41.5 0.9 collective-permute-done.4
  42.4 0.1 broadcast_in_dim.4
  42.5 1.0 pad_maximum_fusion
  43.5 6.2 %all-to-all-start.1 = ((f32[32,8,896]{2,1,0:T(8,128)}), f32[32,8,896]{2,1,0:T(8,128)S(1)}, u32[]{:S(2)}, u32[]{:S(2)}) async-start(f32[32,8,896]{2,1,0:T(8,128)} %pad_maximum_fusion), calls=%async_computation.1 | async-start | bytes 1835008 | tf_op jit(solution)/shard_map/diag/all_to_all | solution.py:241
  49.6 4.2 %collective-permute-start.5 = (f32[256,512]{1,0:T(8,128)S(1)}, f32[256,512]{1,0:T(8,128)S(1)}, u32[]{:S(2)}, u32[]{:S(2)}) collective-permute-start(f32[256,512]{1,0:T(8,128)S(1)} %copy-done), channel_id=1, source_target_pairs={{0,5},{16,21},{32,37},{48,53},{64,69},{80,85},{96,101},{112,117},{... | collective-permute-start | bytes 1572872 | tf_op jit(solution)/shard_map/rowpanel/ppermute | solution.py:216
  53.8 6.5 %collective-permute-start.6 = (f32[256,512]{1,0:T(8,128)S(1)}, f32[256,512]{1,0:T(8,128)S(1)}, u32[]{:S(2)}, u32[]{:S(2)}) collective-permute-start(f32[256,512]{1,0:T(8,128)S(1)} %copy-done), channel_id=1, source_target_pairs={{0,11},{16,27},{32,43},{48,59},{64,75},{80,91},{96,107},{112,123},... | collective-permute-start | bytes 1572872 | tf_op jit(solution)/shard_map/rowpanel/ppermute | solution.py:216
  60.3 4.4 %collective-permute-done.5 = f32[256,512]{1,0:T(8,128)S(1)} collective-permute-done((f32[256,512]{1,0:T(8,128)S(1)}, f32[256,512]{1,0:T(8,128)S(1)}, u32[]{:S(2)}, u32[]{:S(2)}) %collective-permute-start.5) | collective-permute-done | bytes 524320 | tf_op jit(solution)/shard_map/rowpanel/ppermute | solution.py:216
  64.7 6.5 %collective-permute-done.6 = f32[256,512]{1,0:T(8,128)S(1)} collective-permute-done((f32[256,512]{1,0:T(8,128)S(1)}, f32[256,512]{1,0:T(8,128)S(1)}, u32[]{:S(2)}, u32[]{:S(2)}) %collective-permute-start.6) | collective-permute-done | bytes 524320 | tf_op jit(solution)/shard_map/rowpanel/ppermute | solution.py:216
  71.2 0.1 add_select_fusion.1
  71.4 0.0 copy-start.8
  71.4 0.0 all-to-all-done.1
  71.4 2.1 %collective-permute-start.7 = (f32[256,512]{1,0:T(8,128)S(1)}, f32[256,512]{1,0:T(8,128)}, u32[]{:S(2)}, u32[]{:S(2)}) collective-permute-start(f32[256,512]{1,0:T(8,128)S(1)} %add_select_fusion.1), channel_id=1, source_target_pairs={{0,2},{5,7},{11,13},{16,18},{21,23},{27,29},{32,34},{37,39},{43,45... | collective-permute-start | bytes 1572872 | tf_op jit(solution)/shard_map/rowpanel/ppermute | solution.py:216
  73.5 2.1 %collective-permute-start.8 = (f32[256,512]{1,0:T(8,128)S(1)}, f32[256,512]{1,0:T(8,128)}, u32[]{:S(2)}, u32[]{:S(2)}) collective-permute-start(f32[256,512]{1,0:T(8,128)S(1)} %add_select_fusion.1), channel_id=1, source_target_pairs={{0,14},{5,3},{11,9},{16,30},{21,19},{27,25},{32,46},{37,35},{43,41... | collective-permute-start | bytes 1572872 | tf_op jit(solution)/shard_map/rowpanel/ppermute | solution.py:216
  75.6 0.1 concatenate.11
  75.7 1.1 broadcast_in_dim.5
  76.8 8.3 %all-to-all-start.2 = ((f32[32,8,1152]{2,1,0:T(8,128)}), f32[32,8,1152]{2,1,0:T(8,128)S(1)}, u32[]{:S(2)}, u32[]{:S(2)}) async-start(f32[32,8,1152]{2,1,0:T(8,128)} %broadcast_in_dim.5), calls=%async_computation.2 | async-start | bytes 2359296 | tf_op jit(solution)/shard_map/columns/all_to_all | solution.py:241
  85.1 0.0 copy-start.9
  85.1 13.2 %factor_first.1 = (f32[256,256]{1,0:T(8,128)S(1)}, f32[256,256]{1,0:T(8,128)S(1)}, f32[2,128]{1,0:T(2,128)S(1)}) custom-call(f32[256,896]{1,0:T(8,128)S(1)} %bitcast.18), custom_call_target="tpu_custom_call" | custom-call | flops 67108864 | bytes 41943040 | tf_op jit(solution)/shard_map/factor_first/pallas_call | solution.py:202
  98.4 0.7 copy-done.6
  99.1 0.0 collective-permute-done.7
  99.1 0.0 collective-permute-done.8
  99.1 0.0 copy-done.9
  99.1 1.4 %add_select_fusion.panel_ref = f32[256,512]{1,0:T(8,128)S(1)} fusion(f32[256,512]{1,0:T(8,128)S(1)} %copy-done.9, f32[256,512]{1,0:T(8,128)} %collective-permute-done.7, f32[256,512]{1,0:T(8,128)} %collective-permute-done.8, pred[]{:T(512)S(6)} %or.58), kind=kLoop, calls=%fused_computation.1 | loop fusion | flops 262144 | bytes 2097153 | tf_op jit(solution)/shard_map/rowpanel/jit(_where)/select_n | solution.py:228
  100.4 2.1 %collective-permute-start.9 = (f32[256,512]{1,0:T(8,128)S(1)}, f32[256,512]{1,0:T(8,128)}, u32[]{:S(2)}, u32[]{:S(2)}) collective-permute-start(f32[256,512]{1,0:T(8,128)S(1)} %add_select_fusion.panel_ref), channel_id=1, source_target_pairs={{0,1},{3,4},{5,6},{7,8},{9,10},{11,12},{14,15},{16,17},{19,20},{21... | collective-permute-start | bytes 1572872 | tf_op jit(solution)/shard_map/rowpanel/ppermute | solution.py:216
  102.5 0.1 pad_add_fusion.ids_ref
  102.6 15.4 %factor_second.1 = (f32[256,512]{1,0:T(8,128)S(1)}, f32[256,512]{1,0:T(8,128)S(1)}, f32[2,128]{1,0:T(2,128)S(1)}) custom-call(f32[256,896]{1,0:T(8,128)S(1)} %bitcast.19, f32[256,256]{1,0:T(8,128)S(1)} %get-tuple-element.25.inv0_ref), custom_call_target="tpu_custom_call" | custom-call | flops 67108864 | bytes 41943040 | tf_op jit(solution)/shard_map/factor_second/pallas_call | solution.py:202
  118.0 0.0 copy-start.1
  118.0 0.8 copy-done.1
  118.8 0.8 copy-done.3
  119.6 0.0 collective-permute-done.9.moved_ref
  119.6 0.0 all-to-all-done.2
  119.6 1.0 copy-done.2
  120.6 1.0 copy-done.4
  121.7 0.9 copy-done.7
  122.6 3.0 %finish.1 = (f32[256,512]{1,0:T(8,128)}, f32[64,256]{1,0:T(8,128)}, f32[1,64]{1,0:T(1,128)}) custom-call(s32[3]{0:T(128)S(1)} %pad_add_fusion.ids_ref, f32[256,512]{1,0:T(8,128)S(1)} %add_select_fusion.panel_ref, f32[256,512]{1,0:T(8,128)} %collective-permute-done.9.moved_ref, f32[256,1152]{1,0:T(8,128)S(1)} %bitcast.20, f32[256,256]{1,0:T(8,128)S(1)} %copy-done.7, ...), custom_call_target="tpu_custom_call" | custom-call | flops 67108864 | bytes 41943040 | tf_op jit(solution)/shard_map/finish/pallas_call | solution.py:202
  (16 shorter events, 0.1 us)
Async XLA Ops:
  0.6 38.6 %copy-start.5 = (f32[64,256]{1,0:T(8,128)S(1)}, f32[64,256]{1,0:T(8,128)}, u32[]{:S(2)}) copy-start(f32[64,256]{1,0:T(8,128)} %obs_ref.1) | copy-start | bytes 196612
  22.9 12.9 %collective-permute-start = (f32[8,768]{1,0:T(8,128)S(1)}, f32[8,768]{1,0:T(8,128)S(1)}, u32[]{:S(2)}, u32[]{:S(2)}) collective-permute-start(f32[8,768]{1,0:T(8,128)S(1)} %pad_maximum_fusion.1), channel_id=1, source_target_pairs={{0,5},{16,21},{32,37},{48,53},{64,69},{80,85},{96,101},{112,117},{... | collective-permute-start | bytes 73736 | tf_op jit(solution)/shard_map/diag/ppermute | solution.py:216
  31.1 5.5 %collective-permute-start.1 = (f32[8,768]{1,0:T(8,128)S(1)}, f32[8,768]{1,0:T(8,128)S(1)}, u32[]{:S(2)}, u32[]{:S(2)}) collective-permute-start(f32[8,768]{1,0:T(8,128)S(1)} %pad_maximum_fusion.1), channel_id=1, source_target_pairs={{0,11},{16,27},{32,43},{48,59},{64,75},{80,91},{96,107},{112,123},... | collective-permute-start | bytes 73736 | tf_op jit(solution)/shard_map/diag/ppermute | solution.py:216
  36.7 2.7 %collective-permute-start.2 = (f32[8,768]{1,0:T(8,128)S(1)}, f32[8,768]{1,0:T(8,128)S(1)}, u32[]{:S(2)}, u32[]{:S(2)}) collective-permute-start(f32[8,768]{1,0:T(8,128)S(1)} %add_select_fusion.3), channel_id=1, source_target_pairs={{0,2},{5,7},{11,13},{16,18},{21,23},{27,29},{32,34},{37,39},{43,45... | collective-permute-start | bytes 73736 | tf_op jit(solution)/shard_map/diag/ppermute | solution.py:216
  37.9 2.2 %collective-permute-start.3 = (f32[8,768]{1,0:T(8,128)S(1)}, f32[8,768]{1,0:T(8,128)S(1)}, u32[]{:S(2)}, u32[]{:S(2)}) collective-permute-start(f32[8,768]{1,0:T(8,128)S(1)} %add_select_fusion.3), channel_id=1, source_target_pairs={{0,14},{5,3},{11,9},{16,30},{21,19},{27,25},{32,46},{37,35},{43,41... | collective-permute-start | bytes 73736 | tf_op jit(solution)/shard_map/diag/ppermute | solution.py:216
  40.2 2.2 %collective-permute-start.4 = (f32[8,768]{1,0:T(8,128)S(1)}, f32[8,768]{1,0:T(8,128)S(1)}, u32[]{:S(2)}, u32[]{:S(2)}) collective-permute-start(f32[8,768]{1,0:T(8,128)S(1)} %add_select_fusion.2), channel_id=1, source_target_pairs={{0,1},{3,4},{5,6},{7,8},{9,10},{11,12},{14,15},{16,17},{19,20},{21... | collective-permute-start | bytes 73736 | tf_op jit(solution)/shard_map/diag/ppermute | solution.py:216
  43.5 6.2 %copy-start = (f32[256,512]{1,0:T(8,128)S(1)}, f32[256,512]{1,0:T(8,128)}, u32[]{:S(2)}) copy-start(f32[256,512]{1,0:T(8,128)} %cov_ref.1) | copy-start | bytes 1572868
  43.5 27.9 %all-to-all-start.1 = ((f32[32,8,896]{2,1,0:T(8,128)}), f32[32,8,896]{2,1,0:T(8,128)S(1)}, u32[]{:S(2)}, u32[]{:S(2)}) async-start(f32[32,8,896]{2,1,0:T(8,128)} %pad_maximum_fusion), calls=%async_computation.1 | async-start | bytes 1835008 | tf_op jit(solution)/shard_map/diag/all_to_all | solution.py:241
  49.6 15.1 %collective-permute-start.5 = (f32[256,512]{1,0:T(8,128)S(1)}, f32[256,512]{1,0:T(8,128)S(1)}, u32[]{:S(2)}, u32[]{:S(2)}) collective-permute-start(f32[256,512]{1,0:T(8,128)S(1)} %copy-done), channel_id=1, source_target_pairs={{0,5},{16,21},{32,37},{48,53},{64,69},{80,85},{96,101},{112,117},{... | collective-permute-start | bytes 1572872 | tf_op jit(solution)/shard_map/rowpanel/ppermute | solution.py:216
  53.8 17.4 %collective-permute-start.6 = (f32[256,512]{1,0:T(8,128)S(1)}, f32[256,512]{1,0:T(8,128)S(1)}, u32[]{:S(2)}, u32[]{:S(2)}) collective-permute-start(f32[256,512]{1,0:T(8,128)S(1)} %copy-done), channel_id=1, source_target_pairs={{0,11},{16,27},{32,43},{48,59},{64,75},{80,91},{96,107},{112,123},... | collective-permute-start | bytes 1572872 | tf_op jit(solution)/shard_map/rowpanel/ppermute | solution.py:216
  71.4 5.4 %copy-start.8 = (f32[256,512]{1,0:T(8,128)}, f32[256,512]{1,0:T(8,128)S(1)}, u32[]{:S(2)}) copy-start(f32[256,512]{1,0:T(8,128)S(1)} %add_select_fusion.1) | copy-start | bytes 1572868
  71.4 27.6 %collective-permute-start.7 = (f32[256,512]{1,0:T(8,128)S(1)}, f32[256,512]{1,0:T(8,128)}, u32[]{:S(2)}, u32[]{:S(2)}) collective-permute-start(f32[256,512]{1,0:T(8,128)S(1)} %add_select_fusion.1), channel_id=1, source_target_pairs={{0,2},{5,7},{11,13},{16,18},{21,23},{27,29},{32,34},{37,39},{43,45... | collective-permute-start | bytes 1572872 | tf_op jit(solution)/shard_map/rowpanel/ppermute | solution.py:216
  73.5 25.6 %collective-permute-start.8 = (f32[256,512]{1,0:T(8,128)S(1)}, f32[256,512]{1,0:T(8,128)}, u32[]{:S(2)}, u32[]{:S(2)}) collective-permute-start(f32[256,512]{1,0:T(8,128)S(1)} %add_select_fusion.1), channel_id=1, source_target_pairs={{0,14},{5,3},{11,9},{16,30},{21,19},{27,25},{32,46},{37,35},{43,41... | collective-permute-start | bytes 1572872 | tf_op jit(solution)/shard_map/rowpanel/ppermute | solution.py:216
  76.8 42.8 %all-to-all-start.2 = ((f32[32,8,1152]{2,1,0:T(8,128)}), f32[32,8,1152]{2,1,0:T(8,128)S(1)}, u32[]{:S(2)}, u32[]{:S(2)}) async-start(f32[32,8,1152]{2,1,0:T(8,128)} %broadcast_in_dim.5), calls=%async_computation.2 | async-start | bytes 2359296 | tf_op jit(solution)/shard_map/columns/all_to_all | solution.py:241
  85.1 14.0 %copy-start.9 = (f32[256,512]{1,0:T(8,128)S(1)}, f32[256,512]{1,0:T(8,128)}, u32[]{:S(2)}) copy-start(f32[256,512]{1,0:T(8,128)} %copy-done.8) | copy-start | bytes 1572868
  98.4 0.7 copy-start.6
  100.4 19.1 %collective-permute-start.9 = (f32[256,512]{1,0:T(8,128)S(1)}, f32[256,512]{1,0:T(8,128)}, u32[]{:S(2)}, u32[]{:S(2)}) collective-permute-start(f32[256,512]{1,0:T(8,128)S(1)} %add_select_fusion.panel_ref), channel_id=1, source_target_pairs={{0,1},{3,4},{5,6},{7,8},{9,10},{11,12},{14,15},{16,17},{19,20},{21... | collective-permute-start | bytes 1572872 | tf_op jit(solution)/shard_map/rowpanel/ppermute | solution.py:216
  118.0 0.8 copy-start.1
  118.8 0.8 copy-start.3
  119.6 1.0 copy-start.2
  120.6 1.0 copy-start.4
  121.7 0.9 copy-start.7

commit v5 on v4

--- a/solution.py
+++ b/solution.py
@@ -205,7 +205,7 @@
         in_specs=specs,
         out_specs=[VMEM] * len(outs),
         scratch_shapes=[pltpu.VMEM(shape, jnp.float32) for shape in scratch],
-        compiler_params=pltpu.CompilerParams(vmem_limit_bytes=40 * 1024 * 1024),
+        compiler_params=pltpu.CompilerParams(vmem_limit_bytes=16 * 1024 * 1024),
         cost_estimate=pl.CostEstimate(flops=flops, bytes_accessed=40 * 2**20, transcendentals=0),
         name=name,
     )(*args)
@@ -268,14 +268,13 @@
 
     with jax.named_scope("rowpanel"):
         panel, holders = spread_step(panel, (5, -5), [0], cols, col)
-        diag, panel = lax.optimization_barrier((diag, panel))
         panel, holders = spread_step(panel, (2, -2), holders, cols, col)
 
     low0, inv0, diag0 = call(
         first_kernel, "factor_first", [(tile, tile), (tile, tile), (tile // LANES, LANES)],
         [(tile, tile)], diag,
     )
-    inv0, panel = lax.optimization_barrier((inv0, panel))
+    inv0, panel, columns = lax.optimization_barrier((inv0, panel, columns))
     with jax.named_scope("rowpanel"):
         moved, reached = send(panel, 1, last, cols)
     low1, inv1, diag1 = call(

time: 128 us -> 120 us (0.938)
  the two profiles are of different devices: /device:TPU:1 before, /device:TPU:99 now
where the time goes in v5:
time: 120 us; the launch traced here: 119 us
  Pallas kernels  36 us (30%)
  waiting for transfers between devices  32.6 us (27%)
  starting transfers between devices  26.3 us (22%)
  blocking collectives  18.8 us (16%)
  other arithmetic  2.45 us (2%)
  local copies, waits for them, and re-layouts  2.07 us (2%)
    pallas_call x3, Pallas kernels, call(): pl.pallas_call(kernel, out_shape=[jax.ShapeDtypeStruct(shape, jnp.float32...  36 us
    ppermute x10, waiting for transfers between devices, send(): return (lax.ppermute(value, 'col', pairs), [target for _, target in pairs])  19.9 us
    all_to_all x1, blocking collectives, exchange(): return lax.all_to_all(value, 'row', split_axis=0, concat_axis=0, tiled=True)  18.8 us
    ppermute x10, starting transfers between devices, send(): return (lax.ppermute(value, 'col', pairs), [target for _, target in pairs])  13.8 us
    all_to_all x2, waiting for transfers between devices, exchange(): return lax.all_to_all(value, 'row', split_axis=0, concat_axis=0, tiled=True)  12.7 us
    all_to_all x2, starting transfers between devices, exchange(): return lax.all_to_all(value, 'row', split_axis=0, concat_axis=0, tiled=True)  12.6 us
  transfers between devices with their start and end apart: 12, of which 4 were waited for; matrix products, arithmetic and copies ran while one was open for 2% of the time, Pallas kernels for 24%

profile of v5, /device:TPU:99, one launch (start us, length us, event | category | flops | bytes accessed | tf_op | source)
XLA Modules:
  0.0 119.1 jit_solution(6318941828741631103)
XLA Ops:
  0.6 0.0 copy-start.1
  0.6 18.8 %all_to_all.15 = f32[32,8,512]{2,1,0:T(8,128)S(1)} all-to-all(f32[32,8,512]{2,1,0:T(8,128)} %bitcast.21), channel_id=1, replica_groups=mesh['row'=32,'col'=16] {'row'}, dimensions={0} | all-to-all | bytes 1048576 | tf_op jit(solution)/shard_map/scatter/all_to_all | solution.py:241
  19.4 0.7 collective-permute-start.1
  20.1 0.7 collective-permute-start
  20.8 0.0 collective-permute-done.1
  20.8 0.0 collective-permute-done
  20.8 1.3 %collective-permute-start.3 = (f32[8,768]{1,0:T(8,128)S(1)}, f32[8,768]{1,0:T(8,128)S(1)}, u32[]{:S(2)}, u32[]{:S(2)}) collective-permute-start(f32[8,768]{1,0:T(8,128)S(1)} %add_select_fusion.3), channel_id=1, source_target_pairs={{0,14},{5,3},{11,9},{16,30},{21,19},{27,25},{32,46},{37,35},{43,41... | collective-permute-start | bytes 73736 | tf_op jit(solution)/shard_map/diag/ppermute | solution.py:216
  22.1 0.7 collective-permute-start.2
  22.8 0.0 copy-done.1
  22.8 0.1 copy.6
  22.9 17.8 %collective-permute-done.3 = f32[8,768]{1,0:T(8,128)S(1)} collective-permute-done((f32[8,768]{1,0:T(8,128)S(1)}, f32[8,768]{1,0:T(8,128)S(1)}, u32[]{:S(2)}, u32[]{:S(2)}) %collective-permute-start.3) | collective-permute-done | bytes 24608 | tf_op jit(solution)/shard_map/diag/ppermute | solution.py:216
  40.7 0.0 collective-permute-done.2
  40.8 1.3 %collective-permute-start.4 = (f32[8,768]{1,0:T(8,128)S(1)}, f32[8,768]{1,0:T(8,128)S(1)}, u32[]{:S(2)}, u32[]{:S(2)}) collective-permute-start(f32[8,768]{1,0:T(8,128)S(1)} %add_select_fusion.2), channel_id=1, source_target_pairs={{0,1},{3,4},{5,6},{7,8},{9,10},{11,12},{14,15},{16,17},{19,20},{21... | collective-permute-start | bytes 73736 | tf_op jit(solution)/shard_map/diag/ppermute | solution.py:216
  42.1 0.9 collective-permute-done.4
  43.0 0.1 broadcast_in_dim.4
  43.0 1.0 pad_maximum_fusion
  44.0 0.0 copy-start
  44.1 7.6 %all-to-all-start.1 = ((f32[32,8,896]{2,1,0:T(8,128)}), f32[32,8,896]{2,1,0:T(8,128)S(1)}, u32[]{:S(2)}, u32[]{:S(2)}) async-start(f32[32,8,896]{2,1,0:T(8,128)} %pad_maximum_fusion), calls=%async_computation.1 | async-start | bytes 1835008 | tf_op jit(solution)/shard_map/diag/all_to_all | solution.py:241
  51.7 0.0 copy-done
  51.7 0.7 collective-permute-start.6
  52.4 1.5 %collective-permute-start.5 = (f32[256,512]{1,0:T(8,128)S(1)}, f32[256,512]{1,0:T(8,128)}, u32[]{:S(2)}, u32[]{:S(2)}) collective-permute-start(f32[256,512]{1,0:T(8,128)S(1)} %copy-done), channel_id=1, source_target_pairs={{0,5},{16,21},{32,37},{48,53},{64,69},{80,85},{96,101},{112,117},{... | collective-permute-start | bytes 1572872 | tf_op jit(solution)/shard_map/rowpanel/ppermute | solution.py:216
  53.9 12.7 %all-to-all-done.1 = f32[32,8,896]{2,1,0:T(8,128)S(1)} async-done(((f32[32,8,896]{2,1,0:T(8,128)}), f32[32,8,896]{2,1,0:T(8,128)S(1)}, u32[]{:S(2)}, u32[]{:S(2)}) %all-to-all-start.1) | async-done | bytes 917536 | tf_op jit(solution)/shard_map/diag/all_to_all | solution.py:241
  66.5 0.1 concatenate.11
  66.6 1.1 broadcast_in_dim.5
  67.7 5.0 %all-to-all-start.2 = ((f32[32,8,1152]{2,1,0:T(8,128)}), f32[32,8,1152]{2,1,0:T(8,128)S(1)}, u32[]{:S(2)}, u32[]{:S(2)}) async-start(f32[32,8,1152]{2,1,0:T(8,128)} %broadcast_in_dim.5), calls=%async_computation.2 | async-start | bytes 2359296 | tf_op jit(solution)/shard_map/columns/all_to_all | solution.py:241
  72.7 0.0 collective-permute-done.6
  72.7 0.0 collective-permute-done.5
  72.7 1.2 %add_select_fusion.1 = f32[256,512]{1,0:T(8,128)S(1)} fusion(f32[256,512]{1,0:T(8,128)S(1)} %copy-done, f32[256,512]{1,0:T(8,128)} %collective-permute-done.5, f32[256,512]{1,0:T(8,128)S(1)} %collective-permute-done.6, pred[]{:T(512)S(6)} %or.59), kind=kLoop, calls=%fused_computation.2 | loop fusion | flops 262144 | bytes 2097153 | tf_op jit(solution)/shard_map/rowpanel/jit(_where)/select_n | solution.py:228
  73.9 1.3 %collective-permute-start.8 = (f32[256,512]{1,0:T(8,128)S(1)}, f32[256,512]{1,0:T(8,128)S(1)}, u32[]{:S(2)}, u32[]{:S(2)}) collective-permute-start(f32[256,512]{1,0:T(8,128)S(1)} %add_select_fusion.1), channel_id=1, source_target_pairs={{0,14},{5,3},{11,9},{16,30},{21,19},{27,25},{32,46},{37,35},{43,41... | collective-permute-start | bytes 1572872 | tf_op jit(solution)/shard_map/rowpanel/ppermute | solution.py:216
  75.2 0.7 collective-permute-start.7
  75.9 13.2 %factor_first.1 = (f32[256,256]{1,0:T(8,128)S(1)}, f32[256,256]{1,0:T(8,128)S(1)}, f32[2,128]{1,0:T(2,128)S(1)}) custom-call(f32[256,896]{1,0:T(8,128)S(1)} %bitcast.18), custom_call_target="tpu_custom_call" | custom-call | flops 67108864 | bytes 41943040 | tf_op jit(solution)/shard_map/factor_first/pallas_call | solution.py:202
  89.2 0.0 copy-start.2
  89.2 0.7 copy-done.2
  89.9 1.2 %collective-permute-done.8 = f32[256,512]{1,0:T(8,128)S(1)} collective-permute-done((f32[256,512]{1,0:T(8,128)S(1)}, f32[256,512]{1,0:T(8,128)S(1)}, u32[]{:S(2)}, u32[]{:S(2)}) %collective-permute-start.8) | collective-permute-done | bytes 524320 | tf_op jit(solution)/shard_map/rowpanel/ppermute | solution.py:216
  91.1 0.0 collective-permute-done.7
  91.1 0.1 add_select_fusion.panel_ref
  91.2 0.0 all-to-all-done.2
  91.3 5.0 %collective-permute-start.9 = (f32[256,512]{1,0:T(8,128)S(1)}, f32[256,512]{1,0:T(8,128)}, u32[]{:S(2)}, u32[]{:S(2)}) collective-permute-start(f32[256,512]{1,0:T(8,128)S(1)} %add_select_fusion.panel_ref), channel_id=1, source_target_pairs={{0,1},{3,4},{5,6},{7,8},{9,10},{11,12},{14,15},{16,17},{19,20},{21... | collective-permute-start | bytes 1572872 | tf_op jit(solution)/shard_map/rowpanel/ppermute | solution.py:216
  96.3 0.0 copy-start.3
  96.3 0.1 pad_add_fusion.ids_ref
  96.4 15.4 %factor_second.1 = (f32[256,512]{1,0:T(8,128)S(1)}, f32[256,512]{1,0:T(8,128)S(1)}, f32[2,128]{1,0:T(2,128)S(1)}) custom-call(f32[256,896]{1,0:T(8,128)S(1)} %bitcast.19, f32[256,256]{1,0:T(8,128)S(1)} %get-tuple-element.23.inv0_ref), custom_call_target="tpu_custom_call" | custom-call | flops 67108864 | bytes 41943040 | tf_op jit(solution)/shard_map/factor_second/pallas_call | solution.py:202
  111.8 0.0 collective-permute-done.9.moved_ref
  111.8 0.0 copy-done.3
  111.8 7.4 %finish.1 = (f32[256,512]{1,0:T(8,128)}, f32[64,256]{1,0:T(8,128)}, f32[1,64]{1,0:T(1,128)}) custom-call(s32[3]{0:T(128)S(1)} %pad_add_fusion.ids_ref, f32[256,512]{1,0:T(8,128)S(1)} %add_select_fusion.panel_ref, f32[256,512]{1,0:T(8,128)} %collective-permute-done.9.moved_ref, f32[256,1152]{1,0:T(8,128)S(1)} %bitcast.20, f32[256,256]{1,0:T(8,128)S(1)} %copy-done.3, ...), custom_call_target="tpu_custom_call" | custom-call | flops 67108864 | bytes 41943040 | tf_op jit(solution)/shard_map/finish/pallas_call | solution.py:202
  (8 shorter events, 0.0 us)
Async XLA Ops:
  0.6 22.2 %copy-start.1 = (f32[64,256]{1,0:T(8,128)S(1)}, f32[64,256]{1,0:T(8,128)}, u32[]{:S(2)}) copy-start(f32[64,256]{1,0:T(8,128)} %obs_ref.1) | copy-start | bytes 196612
  19.4 1.4 %collective-permute-start.1 = (f32[8,768]{1,0:T(8,128)S(1)}, f32[8,768]{1,0:T(8,128)S(1)}, u32[]{:S(2)}, u32[]{:S(2)}) collective-permute-start(f32[8,768]{1,0:T(8,128)S(1)} %pad_maximum_fusion.1), channel_id=1, source_target_pairs={{0,11},{16,27},{32,43},{48,59},{64,75},{80,91},{96,107},{112,123},... | collective-permute-start | bytes 73736 | tf_op jit(solution)/shard_map/diag/ppermute | solution.py:216
  20.1 0.7 collective-permute-start
  20.8 19.9 %collective-permute-start.3 = (f32[8,768]{1,0:T(8,128)S(1)}, f32[8,768]{1,0:T(8,128)S(1)}, u32[]{:S(2)}, u32[]{:S(2)}) collective-permute-start(f32[8,768]{1,0:T(8,128)S(1)} %add_select_fusion.3), channel_id=1, source_target_pairs={{0,14},{5,3},{11,9},{16,30},{21,19},{27,25},{32,46},{37,35},{43,41... | collective-permute-start | bytes 73736 | tf_op jit(solution)/shard_map/diag/ppermute | solution.py:216
  22.1 18.6 %collective-permute-start.2 = (f32[8,768]{1,0:T(8,128)S(1)}, f32[8,768]{1,0:T(8,128)S(1)}, u32[]{:S(2)}, u32[]{:S(2)}) collective-permute-start(f32[8,768]{1,0:T(8,128)S(1)} %add_select_fusion.3), channel_id=1, source_target_pairs={{0,2},{5,7},{11,13},{16,18},{21,23},{27,29},{32,34},{37,39},{43,45... | collective-permute-start | bytes 73736 | tf_op jit(solution)/shard_map/diag/ppermute | solution.py:216
  40.8 2.2 %collective-permute-start.4 = (f32[8,768]{1,0:T(8,128)S(1)}, f32[8,768]{1,0:T(8,128)S(1)}, u32[]{:S(2)}, u32[]{:S(2)}) collective-permute-start(f32[8,768]{1,0:T(8,128)S(1)} %add_select_fusion.2), channel_id=1, source_target_pairs={{0,1},{3,4},{5,6},{7,8},{9,10},{11,12},{14,15},{16,17},{19,20},{21... | collective-permute-start | bytes 73736 | tf_op jit(solution)/shard_map/diag/ppermute | solution.py:216
  44.0 7.6 %copy-start = (f32[256,512]{1,0:T(8,128)S(1)}, f32[256,512]{1,0:T(8,128)}, u32[]{:S(2)}) copy-start(f32[256,512]{1,0:T(8,128)} %cov_ref.1) | copy-start | bytes 1572868
  44.1 22.5 %all-to-all-start.1 = ((f32[32,8,896]{2,1,0:T(8,128)}), f32[32,8,896]{2,1,0:T(8,128)S(1)}, u32[]{:S(2)}, u32[]{:S(2)}) async-start(f32[32,8,896]{2,1,0:T(8,128)} %pad_maximum_fusion), calls=%async_computation.1 | async-start | bytes 1835008 | tf_op jit(solution)/shard_map/diag/all_to_all | solution.py:241
  51.7 21.1 %collective-permute-start.6 = (f32[256,512]{1,0:T(8,128)S(1)}, f32[256,512]{1,0:T(8,128)S(1)}, u32[]{:S(2)}, u32[]{:S(2)}) collective-permute-start(f32[256,512]{1,0:T(8,128)S(1)} %copy-done), channel_id=1, source_target_pairs={{0,11},{16,27},{32,43},{48,59},{64,75},{80,91},{96,107},{112,123},... | collective-permute-start | bytes 1572872 | tf_op jit(solution)/shard_map/rowpanel/ppermute | solution.py:216
  52.4 20.4 %collective-permute-start.5 = (f32[256,512]{1,0:T(8,128)S(1)}, f32[256,512]{1,0:T(8,128)}, u32[]{:S(2)}, u32[]{:S(2)}) collective-permute-start(f32[256,512]{1,0:T(8,128)S(1)} %copy-done), channel_id=1, source_target_pairs={{0,5},{16,21},{32,37},{48,53},{64,69},{80,85},{96,101},{112,117},{... | collective-permute-start | bytes 1572872 | tf_op jit(solution)/shard_map/rowpanel/ppermute | solution.py:216
  67.7 23.5 %all-to-all-start.2 = ((f32[32,8,1152]{2,1,0:T(8,128)}), f32[32,8,1152]{2,1,0:T(8,128)S(1)}, u32[]{:S(2)}, u32[]{:S(2)}) async-start(f32[32,8,1152]{2,1,0:T(8,128)} %broadcast_in_dim.5), calls=%async_computation.2 | async-start | bytes 2359296 | tf_op jit(solution)/shard_map/columns/all_to_all | solution.py:241
  73.9 17.2 %collective-permute-start.8 = (f32[256,512]{1,0:T(8,128)S(1)}, f32[256,512]{1,0:T(8,128)S(1)}, u32[]{:S(2)}, u32[]{:S(2)}) collective-permute-start(f32[256,512]{1,0:T(8,128)S(1)} %add_select_fusion.1), channel_id=1, source_target_pairs={{0,14},{5,3},{11,9},{16,30},{21,19},{27,25},{32,46},{37,35},{43,41... | collective-permute-start | bytes 1572872 | tf_op jit(solution)/shard_map/rowpanel/ppermute | solution.py:216
  75.2 15.9 %collective-permute-start.7 = (f32[256,512]{1,0:T(8,128)S(1)}, f32[256,512]{1,0:T(8,128)S(1)}, u32[]{:S(2)}, u32[]{:S(2)}) collective-permute-start(f32[256,512]{1,0:T(8,128)S(1)} %add_select_fusion.1), channel_id=1, source_target_pairs={{0,2},{5,7},{11,13},{16,18},{21,23},{27,29},{32,34},{37,39},{43,45... | collective-permute-start | bytes 1572872 | tf_op jit(solution)/shard_map/rowpanel/ppermute | solution.py:216
  89.2 0.7 copy-start.2
  91.3 20.5 %collective-permute-start.9 = (f32[256,512]{1,0:T(8,128)S(1)}, f32[256,512]{1,0:T(8,128)}, u32[]{:S(2)}, u32[]{:S(2)}) collective-permute-start(f32[256,512]{1,0:T(8,128)S(1)} %add_select_fusion.panel_ref), channel_id=1, source_target_pairs={{0,1},{3,4},{5,6},{7,8},{9,10},{11,12},{14,15},{16,17},{19,20},{21... | collective-permute-start | bytes 1572872 | tf_op jit(solution)/shard_map/rowpanel/ppermute | solution.py:216
  96.3 15.5 %copy-start.3 = (f32[256,256]{1,0:T(8,128)S(1)}, f32[256,256]{1,0:T(8,128)}, u32[]{:S(2)}) copy-start(f32[256,256]{1,0:T(8,128)} %copy-done.2) | copy-start | bytes 786436

commit v6 on v5

--- a/solution.py
+++ b/solution.py
@@ -7,6 +7,7 @@
 
 HI = lax.Precision.HIGHEST
 SUB = 8
+GROUP = 4
 LANES = 128
 VMEM = pl.BlockSpec(memory_space=pltpu.VMEM)
 
@@ -26,9 +27,11 @@
     sub = lax.broadcasted_iota(jnp.int32, shape, 0)
     count = len(blocks)
     blocks = list(blocks)
-    upper, inverse = [], []
+    upper, inverse, left, right = [], [], [], []
     for b in range(count):
         base = b * SUB
+        start = b // GROUP * GROUP
+        stop = start + GROUP
         here = blocks[b]
         across = [jnp.broadcast_to(here[:, base + k : base + k + 1], shape) for k in range(SUB)]
         rows = [jnp.broadcast_to(here[k : k + 1, :], shape) for k in range(SUB)]
@@ -57,8 +60,18 @@
             w_block = jnp.where(sub == k, w[k], w_block)
         upper.append(jnp.where(lane >= sub + base, u_block, 0.0))
         inverse.append(w_block)
-        if b + 1 == count:
-            break
+        left.append(u_block)
+        right.append(jnp.where(lane < stop * SUB, w_block, u_block))
+        if b + 1 == stop:
+            if stop < count:
+                far = lax.dot_general(
+                    jnp.concatenate(left[start:], axis=0), jnp.concatenate(right[start:], axis=0),
+                    (((0,), (0,)), ((), ())), precision=HI, preferred_element_type=jnp.float32,
+                )
+                keep = (lane < start * SUB) | (lane >= stop * SUB)
+                for i in range(stop, count):
+                    blocks[i] = jnp.where(keep, blocks[i], 0.0) - far[i * SUB : (i + 1) * SUB]
+            continue
         q = [None] * SUB
         for k in reversed(range(SUB)):
             v = jnp.where(lane < base + SUB, w[k], u[k])
@@ -66,7 +79,7 @@
                 v = v - low[m, k] * q[m]
             q[k] = v * rinv[k]
         keep = (lane < base) | (lane >= base + SUB)
-        for i in range(b + 1, count):
+        for i in range(b + 1, stop):
             old = blocks[i]
             terms = [
                 jnp.broadcast_to(old[:, base + k : base + k + 1], shape) * q[k] for k in range(SUB)

time: 120 us -> 118 us (0.983)
  Pallas kernels: 36 us -> 31.7 us
  waiting for transfers between devices: 32.6 us -> 34.8 us
    pallas_call x3, Pallas kernels: 36 us -> 31.7 us  [call(): pl.pallas_call(kernel, out_shape=[jax.ShapeDtypeStruct(shape, jnp.float32...]
    ppermute x10, waiting for transfers between devices: 19.9 us -> 22.1 us  [send(): return (lax.ppermute(value, 'col', pairs), [target for _, target in pairs])]
  transfers between devices with their start and end apart: 12 -> 12, of which waited for: 4 -> 4; matrix products, arithmetic and copies ran while one was open for 2% -> 2% of each run, Pallas kernels for 24% -> 21%
where the time goes in v6:
time: 118 us; the launch traced here: 117 us
  waiting for transfers between devices  34.8 us (29%)
  Pallas kernels  31.7 us (27%)
  starting transfers between devices  26.3 us (22%)
  blocking collectives  18.8 us (16%)
  other arithmetic  2.45 us (2%)
  local copies, waits for them, and re-layouts  2.07 us (2%)
    pallas_call x3, Pallas kernels, call(): pl.pallas_call(kernel, out_shape=[jax.ShapeDtypeStruct(shape, jnp.float32...  31.7 us
    ppermute x10, waiting for transfers between devices, send(): return (lax.ppermute(value, 'col', pairs), [target for _, target in pairs])  22.1 us
    all_to_all x1, blocking collectives, exchange(): return lax.all_to_all(value, 'row', split_axis=0, concat_axis=0, tiled=True)  18.8 us
    ppermute x10, starting transfers between devices, send(): return (lax.ppermute(value, 'col', pairs), [target for _, target in pairs])  13.8 us
    all_to_all x2, waiting for transfers between devices, exchange(): return lax.all_to_all(value, 'row', split_axis=0, concat_axis=0, tiled=True)  12.7 us
    all_to_all x2, starting transfers between devices, exchange(): return lax.all_to_all(value, 'row', split_axis=0, concat_axis=0, tiled=True)  12.6 us
  transfers between devices with their start and end apart: 12, of which 4 were waited for; matrix products, arithmetic and copies ran while one was open for 2% of the time, Pallas kernels for 21%

profile of v6, /device:TPU:99, one launch (start us, length us, event | category | flops | bytes accessed | tf_op | source)
XLA Modules:
  0.0 117.1 jit_solution(5288458578833402705)
XLA Ops:
  0.6 0.0 copy-start.1
  0.6 18.8 %all_to_all.15 = f32[32,8,512]{2,1,0:T(8,128)S(1)} all-to-all(f32[32,8,512]{2,1,0:T(8,128)} %bitcast.21), channel_id=1, replica_groups=mesh['row'=32,'col'=16] {'row'}, dimensions={0} | all-to-all | bytes 1048576 | tf_op jit(solution)/shard_map/scatter/all_to_all | solution.py:254
  19.4 0.7 collective-permute-start.1
  20.1 0.7 collective-permute-start
  20.8 0.0 collective-permute-done.1
  20.8 0.0 collective-permute-done
  20.8 1.3 %collective-permute-start.3 = (f32[8,768]{1,0:T(8,128)S(1)}, f32[8,768]{1,0:T(8,128)S(1)}, u32[]{:S(2)}, u32[]{:S(2)}) collective-permute-start(f32[8,768]{1,0:T(8,128)S(1)} %add_select_fusion.3), channel_id=1, source_target_pairs={{0,14},{5,3},{11,9},{16,30},{21,19},{27,25},{32,46},{37,35},{43,41... | collective-permute-start | bytes 73736 | tf_op jit(solution)/shard_map/diag/ppermute | solution.py:229
  22.1 0.7 collective-permute-start.2
  22.8 0.0 copy-done.1
  22.8 0.1 copy.6
  22.9 17.8 %collective-permute-done.3 = f32[8,768]{1,0:T(8,128)S(1)} collective-permute-done((f32[8,768]{1,0:T(8,128)S(1)}, f32[8,768]{1,0:T(8,128)S(1)}, u32[]{:S(2)}, u32[]{:S(2)}) %collective-permute-start.3) | collective-permute-done | bytes 24608 | tf_op jit(solution)/shard_map/diag/ppermute | solution.py:229
  40.7 0.0 collective-permute-done.2
  40.8 1.3 %collective-permute-start.4 = (f32[8,768]{1,0:T(8,128)S(1)}, f32[8,768]{1,0:T(8,128)S(1)}, u32[]{:S(2)}, u32[]{:S(2)}) collective-permute-start(f32[8,768]{1,0:T(8,128)S(1)} %add_select_fusion.2), channel_id=1, source_target_pairs={{0,1},{3,4},{5,6},{7,8},{9,10},{11,12},{14,15},{16,17},{19,20},{21... | collective-permute-start | bytes 73736 | tf_op jit(solution)/shard_map/diag/ppermute | solution.py:229
  42.1 0.9 collective-permute-done.4
  43.0 0.1 broadcast_in_dim.4
  43.0 1.0 pad_maximum_fusion
  44.0 0.0 copy-start
  44.1 7.6 %all-to-all-start.1 = ((f32[32,8,896]{2,1,0:T(8,128)}), f32[32,8,896]{2,1,0:T(8,128)S(1)}, u32[]{:S(2)}, u32[]{:S(2)}) async-start(f32[32,8,896]{2,1,0:T(8,128)} %pad_maximum_fusion), calls=%async_computation.1 | async-start | bytes 1835008 | tf_op jit(solution)/shard_map/diag/all_to_all | solution.py:254
  51.7 0.0 copy-done
  51.7 0.7 collective-permute-start.6
  52.4 1.5 %collective-permute-start.5 = (f32[256,512]{1,0:T(8,128)S(1)}, f32[256,512]{1,0:T(8,128)}, u32[]{:S(2)}, u32[]{:S(2)}) collective-permute-start(f32[256,512]{1,0:T(8,128)S(1)} %copy-done), channel_id=1, source_target_pairs={{0,5},{16,21},{32,37},{48,53},{64,69},{80,85},{96,101},{112,117},{... | collective-permute-start | bytes 1572872 | tf_op jit(solution)/shard_map/rowpanel/ppermute | solution.py:229
  53.9 12.7 %all-to-all-done.1 = f32[32,8,896]{2,1,0:T(8,128)S(1)} async-done(((f32[32,8,896]{2,1,0:T(8,128)}), f32[32,8,896]{2,1,0:T(8,128)S(1)}, u32[]{:S(2)}, u32[]{:S(2)}) %all-to-all-start.1) | async-done | bytes 917536 | tf_op jit(solution)/shard_map/diag/all_to_all | solution.py:254
  66.5 0.1 concatenate.11
  66.6 1.1 broadcast_in_dim.5
  67.7 5.0 %all-to-all-start.2 = ((f32[32,8,1152]{2,1,0:T(8,128)}), f32[32,8,1152]{2,1,0:T(8,128)S(1)}, u32[]{:S(2)}, u32[]{:S(2)}) async-start(f32[32,8,1152]{2,1,0:T(8,128)} %broadcast_in_dim.5), calls=%async_computation.2 | async-start | bytes 2359296 | tf_op jit(solution)/shard_map/columns/all_to_all | solution.py:254
  72.7 0.0 collective-permute-done.6
  72.7 0.0 collective-permute-done.5
  72.7 1.2 %add_select_fusion.1 = f32[256,512]{1,0:T(8,128)S(1)} fusion(f32[256,512]{1,0:T(8,128)S(1)} %copy-done, f32[256,512]{1,0:T(8,128)} %collective-permute-done.5, f32[256,512]{1,0:T(8,128)S(1)} %collective-permute-done.6, pred[]{:T(512)S(6)} %or.59), kind=kLoop, calls=%fused_computation.2 | loop fusion | flops 262144 | bytes 2097153 | tf_op jit(solution)/shard_map/rowpanel/jit(_where)/select_n | solution.py:241
  73.9 1.3 %collective-permute-start.8 = (f32[256,512]{1,0:T(8,128)S(1)}, f32[256,512]{1,0:T(8,128)S(1)}, u32[]{:S(2)}, u32[]{:S(2)}) collective-permute-start(f32[256,512]{1,0:T(8,128)S(1)} %add_select_fusion.1), channel_id=1, source_target_pairs={{0,14},{5,3},{11,9},{16,30},{21,19},{27,25},{32,46},{37,35},{43,41... | collective-permute-start | bytes 1572872 | tf_op jit(solution)/shard_map/rowpanel/ppermute | solution.py:229
  75.2 0.7 collective-permute-start.7
  75.9 11.0 %factor_first.1 = (f32[256,256]{1,0:T(8,128)S(1)}, f32[256,256]{1,0:T(8,128)S(1)}, f32[2,128]{1,0:T(2,128)S(1)}) custom-call(f32[256,896]{1,0:T(8,128)S(1)} %bitcast.18), custom_call_target="tpu_custom_call" | custom-call | flops 67108864 | bytes 41943040 | tf_op jit(solution)/shard_map/factor_first/pallas_call | solution.py:215
  86.9 0.0 copy-start.2
  86.9 0.7 copy-done.2
  87.6 3.4 %collective-permute-done.8 = f32[256,512]{1,0:T(8,128)S(1)} collective-permute-done((f32[256,512]{1,0:T(8,128)S(1)}, f32[256,512]{1,0:T(8,128)S(1)}, u32[]{:S(2)}, u32[]{:S(2)}) %collective-permute-start.8) | collective-permute-done | bytes 524320 | tf_op jit(solution)/shard_map/rowpanel/ppermute | solution.py:229
  91.1 0.0 collective-permute-done.7
  91.1 0.1 add_select_fusion.panel_ref
  91.2 0.0 all-to-all-done.2
  91.3 5.0 %collective-permute-start.9 = (f32[256,512]{1,0:T(8,128)S(1)}, f32[256,512]{1,0:T(8,128)}, u32[]{:S(2)}, u32[]{:S(2)}) collective-permute-start(f32[256,512]{1,0:T(8,128)S(1)} %add_select_fusion.panel_ref), channel_id=1, source_target_pairs={{0,1},{3,4},{5,6},{7,8},{9,10},{11,12},{14,15},{16,17},{19,20},{21... | collective-permute-start | bytes 1572872 | tf_op jit(solution)/shard_map/rowpanel/ppermute | solution.py:229
  96.3 0.0 copy-start.3
  96.3 0.1 pad_add_fusion.ids_ref
  96.4 13.2 %factor_second.1 = (f32[256,512]{1,0:T(8,128)S(1)}, f32[256,512]{1,0:T(8,128)S(1)}, f32[2,128]{1,0:T(2,128)S(1)}) custom-call(f32[256,896]{1,0:T(8,128)S(1)} %bitcast.19, f32[256,256]{1,0:T(8,128)S(1)} %get-tuple-element.23.inv0_ref), custom_call_target="tpu_custom_call" | custom-call | flops 67108864 | bytes 41943040 | tf_op jit(solution)/shard_map/factor_second/pallas_call | solution.py:215
  109.5 0.0 collective-permute-done.9.moved_ref
  109.5 0.0 copy-done.3
  109.5 7.5 %finish.1 = (f32[256,512]{1,0:T(8,128)}, f32[64,256]{1,0:T(8,128)}, f32[1,64]{1,0:T(1,128)}) custom-call(s32[3]{0:T(128)S(1)} %pad_add_fusion.ids_ref, f32[256,512]{1,0:T(8,128)S(1)} %add_select_fusion.panel_ref, f32[256,512]{1,0:T(8,128)} %collective-permute-done.9.moved_ref, f32[256,1152]{1,0:T(8,128)S(1)} %bitcast.20, f32[256,256]{1,0:T(8,128)S(1)} %copy-done.3, ...), custom_call_target="tpu_custom_call" | custom-call | flops 67108864 | bytes 41943040 | tf_op jit(solution)/shard_map/finish/pallas_call | solution.py:215
  (8 shorter events, 0.0 us)
Async XLA Ops:
  0.6 22.2 %copy-start.1 = (f32[64,256]{1,0:T(8,128)S(1)}, f32[64,256]{1,0:T(8,128)}, u32[]{:S(2)}) copy-start(f32[64,256]{1,0:T(8,128)} %obs_ref.1) | copy-start | bytes 196612
  19.4 1.4 %collective-permute-start.1 = (f32[8,768]{1,0:T(8,128)S(1)}, f32[8,768]{1,0:T(8,128)S(1)}, u32[]{:S(2)}, u32[]{:S(2)}) collective-permute-start(f32[8,768]{1,0:T(8,128)S(1)} %pad_maximum_fusion.1), channel_id=1, source_target_pairs={{0,11},{16,27},{32,43},{48,59},{64,75},{80,91},{96,107},{112,123},... | collective-permute-start | bytes 73736 | tf_op jit(solution)/shard_map/diag/ppermute | solution.py:229
  20.1 0.7 collective-permute-start
  20.8 19.9 %collective-permute-start.3 = (f32[8,768]{1,0:T(8,128)S(1)}, f32[8,768]{1,0:T(8,128)S(1)}, u32[]{:S(2)}, u32[]{:S(2)}) collective-permute-start(f32[8,768]{1,0:T(8,128)S(1)} %add_select_fusion.3), channel_id=1, source_target_pairs={{0,14},{5,3},{11,9},{16,30},{21,19},{27,25},{32,46},{37,35},{43,41... | collective-permute-start | bytes 73736 | tf_op jit(solution)/shard_map/diag/ppermute | solution.py:229
  22.1 18.6 %collective-permute-start.2 = (f32[8,768]{1,0:T(8,128)S(1)}, f32[8,768]{1,0:T(8,128)S(1)}, u32[]{:S(2)}, u32[]{:S(2)}) collective-permute-start(f32[8,768]{1,0:T(8,128)S(1)} %add_select_fusion.3), channel_id=1, source_target_pairs={{0,2},{5,7},{11,13},{16,18},{21,23},{27,29},{32,34},{37,39},{43,45... | collective-permute-start | bytes 73736 | tf_op jit(solution)/shard_map/diag/ppermute | solution.py:229
  40.8 2.2 %collective-permute-start.4 = (f32[8,768]{1,0:T(8,128)S(1)}, f32[8,768]{1,0:T(8,128)S(1)}, u32[]{:S(2)}, u32[]{:S(2)}) collective-permute-start(f32[8,768]{1,0:T(8,128)S(1)} %add_select_fusion.2), channel_id=1, source_target_pairs={{0,1},{3,4},{5,6},{7,8},{9,10},{11,12},{14,15},{16,17},{19,20},{21... | collective-permute-start | bytes 73736 | tf_op jit(solution)/shard_map/diag/ppermute | solution.py:229
  44.0 7.6 %copy-start = (f32[256,512]{1,0:T(8,128)S(1)}, f32[256,512]{1,0:T(8,128)}, u32[]{:S(2)}) copy-start(f32[256,512]{1,0:T(8,128)} %cov_ref.1) | copy-start | bytes 1572868
  44.1 22.5 %all-to-all-start.1 = ((f32[32,8,896]{2,1,0:T(8,128)}), f32[32,8,896]{2,1,0:T(8,128)S(1)}, u32[]{:S(2)}, u32[]{:S(2)}) async-start(f32[32,8,896]{2,1,0:T(8,128)} %pad_maximum_fusion), calls=%async_computation.1 | async-start | bytes 1835008 | tf_op jit(solution)/shard_map/diag/all_to_all | solution.py:254
  51.7 21.1 %collective-permute-start.6 = (f32[256,512]{1,0:T(8,128)S(1)}, f32[256,512]{1,0:T(8,128)S(1)}, u32[]{:S(2)}, u32[]{:S(2)}) collective-permute-start(f32[256,512]{1,0:T(8,128)S(1)} %copy-done), channel_id=1, source_target_pairs={{0,11},{16,27},{32,43},{48,59},{64,75},{80,91},{96,107},{112,123},... | collective-permute-start | bytes 1572872 | tf_op jit(solution)/shard_map/rowpanel/ppermute | solution.py:229
  52.4 20.4 %collective-permute-start.5 = (f32[256,512]{1,0:T(8,128)S(1)}, f32[256,512]{1,0:T(8,128)}, u32[]{:S(2)}, u32[]{:S(2)}) collective-permute-start(f32[256,512]{1,0:T(8,128)S(1)} %copy-done), channel_id=1, source_target_pairs={{0,5},{16,21},{32,37},{48,53},{64,69},{80,85},{96,101},{112,117},{... | collective-permute-start | bytes 1572872 | tf_op jit(solution)/shard_map/rowpanel/ppermute | solution.py:229
  67.7 23.5 %all-to-all-start.2 = ((f32[32,8,1152]{2,1,0:T(8,128)}), f32[32,8,1152]{2,1,0:T(8,128)S(1)}, u32[]{:S(2)}, u32[]{:S(2)}) async-start(f32[32,8,1152]{2,1,0:T(8,128)} %broadcast_in_dim.5), calls=%async_computation.2 | async-start | bytes 2359296 | tf_op jit(solution)/shard_map/columns/all_to_all | solution.py:254
  73.9 17.2 %collective-permute-start.8 = (f32[256,512]{1,0:T(8,128)S(1)}, f32[256,512]{1,0:T(8,128)S(1)}, u32[]{:S(2)}, u32[]{:S(2)}) collective-permute-start(f32[256,512]{1,0:T(8,128)S(1)} %add_select_fusion.1), channel_id=1, source_target_pairs={{0,14},{5,3},{11,9},{16,30},{21,19},{27,25},{32,46},{37,35},{43,41... | collective-permute-start | bytes 1572872 | tf_op jit(solution)/shard_map/rowpanel/ppermute | solution.py:229
  75.2 15.9 %collective-permute-start.7 = (f32[256,512]{1,0:T(8,128)S(1)}, f32[256,512]{1,0:T(8,128)S(1)}, u32[]{:S(2)}, u32[]{:S(2)}) collective-permute-start(f32[256,512]{1,0:T(8,128)S(1)} %add_select_fusion.1), channel_id=1, source_target_pairs={{0,2},{5,7},{11,13},{16,18},{21,23},{27,29},{32,34},{37,39},{43,45... | collective-permute-start | bytes 1572872 | tf_op jit(solution)/shard_map/rowpanel/ppermute | solution.py:229
  86.9 0.7 copy-start.2
  91.3 18.3 %collective-permute-start.9 = (f32[256,512]{1,0:T(8,128)S(1)}, f32[256,512]{1,0:T(8,128)}, u32[]{:S(2)}, u32[]{:S(2)}) collective-permute-start(f32[256,512]{1,0:T(8,128)S(1)} %add_select_fusion.panel_ref), channel_id=1, source_target_pairs={{0,1},{3,4},{5,6},{7,8},{9,10},{11,12},{14,15},{16,17},{19,20},{21... | collective-permute-start | bytes 1572872 | tf_op jit(solution)/shard_map/rowpanel/ppermute | solution.py:229
  96.3 13.3 %copy-start.3 = (f32[256,256]{1,0:T(8,128)S(1)}, f32[256,256]{1,0:T(8,128)}, u32[]{:S(2)}) copy-start(f32[256,256]{1,0:T(8,128)} %copy-done.2) | copy-start | bytes 786436

commit v7 on v6

--- a/solution.py
+++ b/solution.py
@@ -229,6 +229,13 @@
     return lax.ppermute(value, "col", pairs), [target for _, target in pairs]
 
 
+def pick(value, moved, targets, position):
+    is_new = jnp.zeros((), bool)
+    for target in targets:
+        is_new = is_new | (position == target)
+    return jnp.where(is_new, moved, value)
+
+
 def spread_step(value, hops, holders, extent, position):
     arrived, targets = None, []
     for hop in hops:
@@ -260,10 +267,19 @@
 
     with jax.named_scope("diag"):
         piece = jnp.concatenate([first[:, :tile], second], axis=1)
-        holders = [0]
-        piece, holders = spread_step(piece, (5, -5), holders, cols, col)
-        piece, holders = spread_step(piece, (2, -2), holders, cols, col)
-        last = [z for z in holders if (z + 1) % cols not in holders]
+        near, reached = send(piece, 5, [0], cols)
+        piece, near, reached = pick(piece, near, reached, col), piece, [0] + reached
+        back, backs = send(piece, -2, reached, cols)
+        ahead, aheads = send(piece, 2, reached, cols)
+        near, piece = lax.optimization_barrier((near, piece))
+        far, fars = send(near, -5, [0], cols)
+        piece = pick(piece, far, fars, col)
+        far_back, far_backs = send(piece, -2, fars, cols)
+        far_ahead, far_aheads = send(piece, 2, fars, cols)
+        piece = pick(pick(piece, back, backs, col), ahead, aheads, col)
+        piece = pick(pick(piece, far_back, far_backs, col), far_ahead, far_aheads, col)
+        last = [z for z in range(cols) if z in reached + backs + aheads + fars + far_backs + far_aheads]
+        last = [z for z in last if (z + 1) % cols not in last]
         piece, _ = spread_step(piece, (1,), last, cols, col)
         panel, piece = lax.optimization_barrier((covariance, piece))
         sent = jnp.broadcast_to(piece[None], (rows,) + piece.shape)
@@ -280,7 +296,7 @@
         columns = columns.reshape(tile, -1)
 
     with jax.named_scope("rowpanel"):
-        panel, holders = spread_step(panel, (5, -5), [0], cols, col)
+        panel, holders = spread_step(panel, (-5, 5), [0], cols, col)
         panel, holders = spread_step(panel, (2, -2), holders, cols, col)
 
     low0, inv0, diag0 = call(

time: 118 us -> 114 us (0.966)
  waiting for transfers between devices: 34.8 us -> 28.3 us
  other arithmetic: 2.45 us -> 3.81 us
    ppermute x10 -> x12, waiting for transfers between devices: 22.1 us -> 15.6 us  [send(): return (lax.ppermute(value, 'col', pairs), [target for _, target in pairs])]
    select_n x5 -> x3, other arithmetic: 1.36 us -> 2.7 us  [spread_step(): jnp.where(is_new, arrived, value)]
    ppermute x10 -> x12, starting transfers between devices: 13.8 us -> 14.3 us  [send(): return (lax.ppermute(value, 'col', pairs), [target for _, target in pairs])]
  transfers between devices with their start and end apart: 12 -> 14, of which waited for: 4 -> 4; matrix products, arithmetic and copies ran while one was open for 2% -> 4% of each run, Pallas kernels for 21% -> 21%
where the time goes in v7:
time: 114 us; the launch traced here: 113 us
  Pallas kernels  31.7 us (28%)
  waiting for transfers between devices  28.3 us (25%)
  starting transfers between devices  26.9 us (24%)
  blocking collectives  18.8 us (16%)
  other arithmetic  3.81 us (3%)
  local copies, waits for them, and re-layouts  2.89 us (3%)
    pallas_call x3, Pallas kernels, call(): pl.pallas_call(kernel, out_shape=[jax.ShapeDtypeStruct(shape, jnp.float32...  31.7 us
    all_to_all x1, blocking collectives, exchange(): return lax.all_to_all(value, 'row', split_axis=0, concat_axis=0, tiled=True)  18.8 us
    ppermute x12, waiting for transfers between devices, send(): return (lax.ppermute(value, 'col', pairs), [target for _, target in pairs])  15.6 us
    ppermute x12, starting transfers between devices, send(): return (lax.ppermute(value, 'col', pairs), [target for _, target in pairs])  14.3 us
    all_to_all x2, waiting for transfers between devices, exchange(): return lax.all_to_all(value, 'row', split_axis=0, concat_axis=0, tiled=True)  12.7 us
    all_to_all x2, starting transfers between devices, exchange(): return lax.all_to_all(value, 'row', split_axis=0, concat_axis=0, tiled=True)  12.6 us
    select_n x3, other arithmetic, spread_step(): jnp.where(is_new, arrived, value)  2.7 us
  transfers between devices with their start and end apart: 14, of which 4 were waited for; matrix products, arithmetic and copies ran while one was open for 4% of the time, Pallas kernels for 21%

profile of v7, /device:TPU:99, one launch (start us, length us, event | category | flops | bytes accessed | tf_op | source)
XLA Modules:
  0.0 113.3 jit_solution(2711025994492691781)
XLA Ops:
  0.6 0.0 copy-start.1
  0.6 18.8 %all_to_all.15 = f32[32,8,512]{2,1,0:T(8,128)S(1)} all-to-all(f32[32,8,512]{2,1,0:T(8,128)} %bitcast.21), channel_id=1, replica_groups=mesh['row'=32,'col'=16] {'row'}, dimensions={0} | all-to-all | bytes 1048576 | tf_op jit(solution)/shard_map/scatter/all_to_all | solution.py:261
  19.4 0.7 collective-permute-start
  20.1 0.0 collective-permute-done
  20.1 0.7 collective-permute-start.1
  20.8 1.3 %collective-permute-start.5 = (f32[8,768]{1,0:T(8,128)S(1)}, f32[8,768]{1,0:T(8,128)S(1)}, u32[]{:S(2)}, u32[]{:S(2)}) collective-permute-start(f32[8,768]{1,0:T(8,128)S(1)} %broadcast_select_fusion), channel_id=1, source_target_pairs={{0,14},{5,3},{16,30},{21,19},{32,46},{37,35},{48,62},{53,51},{64,7... | collective-permute-start | bytes 73736 | tf_op jit(solution)/shard_map/diag/ppermute | solution.py:229
  22.1 0.7 collective-permute-start.4
  22.8 0.0 collective-permute-done.1
  22.8 0.7 collective-permute-start.3
  23.5 0.7 collective-permute-start.2
  24.2 0.0 copy-done.1
  24.2 0.1 copy.6
  24.3 11.9 %collective-permute-done.5 = f32[8,768]{1,0:T(8,128)S(1)} collective-permute-done((f32[8,768]{1,0:T(8,128)S(1)}, f32[8,768]{1,0:T(8,128)S(1)}, u32[]{:S(2)}, u32[]{:S(2)}) %collective-permute-start.5) | collective-permute-done | bytes 24608 | tf_op jit(solution)/shard_map/diag/ppermute | solution.py:229
  36.2 0.0 collective-permute-done.4
  36.2 0.0 collective-permute-done.3
  36.2 0.0 collective-permute-done.2
  36.2 1.3 %collective-permute-start.6 = (f32[8,768]{1,0:T(8,128)S(1)}, f32[8,768]{1,0:T(8,128)S(1)}, u32[]{:S(2)}, u32[]{:S(2)}) collective-permute-start(f32[8,768]{1,0:T(8,128)S(1)} %select_select_fusion), channel_id=1, source_target_pairs={{0,1},{3,4},{5,6},{7,8},{9,10},{11,12},{14,15},{16,17},{19,20},{21... | collective-permute-start | bytes 73736 | tf_op jit(solution)/shard_map/diag/ppermute | solution.py:229
  37.6 0.9 collective-permute-done.6
  38.4 0.1 broadcast_in_dim.4
  38.5 1.0 pad_maximum_fusion
  39.5 7.6 %all-to-all-start.1 = ((f32[32,8,896]{2,1,0:T(8,128)}), f32[32,8,896]{2,1,0:T(8,128)S(1)}, u32[]{:S(2)}, u32[]{:S(2)}) async-start(f32[32,8,896]{2,1,0:T(8,128)} %pad_maximum_fusion), calls=%async_computation.1 | async-start | bytes 1835008 | tf_op jit(solution)/shard_map/diag/all_to_all | solution.py:261
  47.1 0.0 copy-done
  47.1 0.7 collective-permute-start.8
  47.8 1.5 %collective-permute-start.7 = (f32[256,512]{1,0:T(8,128)S(1)}, f32[256,512]{1,0:T(8,128)}, u32[]{:S(2)}, u32[]{:S(2)}) collective-permute-start(f32[256,512]{1,0:T(8,128)S(1)} %copy-done), channel_id=1, source_target_pairs={{0,11},{16,27},{32,43},{48,59},{64,75},{80,91},{96,107},{112,123},... | collective-permute-start | bytes 1572872 | tf_op jit(solution)/shard_map/rowpanel/ppermute | solution.py:229
  49.3 12.7 %all-to-all-done.1 = f32[32,8,896]{2,1,0:T(8,128)S(1)} async-done(((f32[32,8,896]{2,1,0:T(8,128)}), f32[32,8,896]{2,1,0:T(8,128)S(1)}, u32[]{:S(2)}, u32[]{:S(2)}) %all-to-all-start.1) | async-done | bytes 917536 | tf_op jit(solution)/shard_map/diag/all_to_all | solution.py:261
  62.0 0.1 concatenate.11
  62.1 1.1 broadcast_in_dim.5
  63.2 5.0 %all-to-all-start.2 = ((f32[32,8,1152]{2,1,0:T(8,128)}), f32[32,8,1152]{2,1,0:T(8,128)S(1)}, u32[]{:S(2)}, u32[]{:S(2)}) async-start(f32[32,8,1152]{2,1,0:T(8,128)} %broadcast_in_dim.5), calls=%async_computation.2 | async-start | bytes 2359296 | tf_op jit(solution)/shard_map/columns/all_to_all | solution.py:261
  68.2 0.0 collective-permute-done.8
  68.2 0.0 copy-start.5
  68.2 0.8 copy-done.5
  69.0 0.0 collective-permute-done.7
  69.0 1.3 %add_select_fusion.1 = f32[256,512]{1,0:T(8,128)S(1)} fusion(f32[256,512]{1,0:T(8,128)S(1)} %copy-done, f32[256,512]{1,0:T(8,128)} %collective-permute-done.7, f32[256,512]{1,0:T(8,128)} %copy-done.5, pred[]{:T(512)S(6)} %or.58), kind=kLoop, calls=%fused_computation.2 | loop fusion | flops 262144 | bytes 2097153 | tf_op jit(solution)/shard_map/rowpanel/jit(_where)/select_n | solution.py:248
  70.4 0.0 copy-start.4
  70.4 1.3 %collective-permute-start.10 = (f32[256,512]{1,0:T(8,128)S(1)}, f32[256,512]{1,0:T(8,128)}, u32[]{:S(2)}, u32[]{:S(2)}) collective-permute-start(f32[256,512]{1,0:T(8,128)S(1)} %add_select_fusion.1), channel_id=1, source_target_pairs={{0,14},{5,3},{11,9},{16,30},{21,19},{27,25},{32,46},{37,35},{43,41... | collective-permute-start | bytes 1572872 | tf_op jit(solution)/shard_map/rowpanel/ppermute | solution.py:229
  71.7 1.5 %collective-permute-start.9 = (f32[256,512]{1,0:T(8,128)S(1)}, f32[256,512]{1,0:T(8,128)}, u32[]{:S(2)}, u32[]{:S(2)}) collective-permute-start(f32[256,512]{1,0:T(8,128)S(1)} %add_select_fusion.1), channel_id=1, source_target_pairs={{0,2},{5,7},{11,13},{16,18},{21,23},{27,29},{32,34},{37,39},{43,45... | collective-permute-start | bytes 1572872 | tf_op jit(solution)/shard_map/rowpanel/ppermute | solution.py:229
  73.1 11.0 %factor_first.1 = (f32[256,256]{1,0:T(8,128)S(1)}, f32[256,256]{1,0:T(8,128)S(1)}, f32[2,128]{1,0:T(2,128)S(1)}) custom-call(f32[256,896]{1,0:T(8,128)S(1)} %bitcast.18), custom_call_target="tpu_custom_call" | custom-call | flops 67108864 | bytes 41943040 | tf_op jit(solution)/shard_map/factor_first/pallas_call | solution.py:215
  84.1 0.7 copy-done.2
  84.8 2.8 %collective-permute-done.10 = f32[256,512]{1,0:T(8,128)} collective-permute-done((f32[256,512]{1,0:T(8,128)S(1)}, f32[256,512]{1,0:T(8,128)}, u32[]{:S(2)}, u32[]{:S(2)}) %collective-permute-start.10) | collective-permute-done | bytes 524320 | tf_op jit(solution)/shard_map/rowpanel/ppermute | solution.py:229
  87.6 0.0 copy-done.4
  87.6 0.0 collective-permute-done.9
  87.6 1.3 %add_select_fusion.panel_ref = f32[256,512]{1,0:T(8,128)S(1)} fusion(f32[256,512]{1,0:T(8,128)} %copy-done.4, f32[256,512]{1,0:T(8,128)} %collective-permute-done.9, f32[256,512]{1,0:T(8,128)} %collective-permute-done.10, pred[]{:T(512)S(6)} %or.57), kind=kLoop, calls=%fused_computation.1 | loop fusion | flops 262144 | bytes 2097153 | tf_op jit(solution)/shard_map/rowpanel/jit(_where)/select_n | solution.py:248
  89.0 0.0 all-to-all-done.2
  89.0 3.5 %collective-permute-start.11 = (f32[256,512]{1,0:T(8,128)S(1)}, f32[256,512]{1,0:T(8,128)}, u32[]{:S(2)}, u32[]{:S(2)}) collective-permute-start(f32[256,512]{1,0:T(8,128)S(1)} %add_select_fusion.panel_ref), channel_id=1, source_target_pairs={{0,1},{3,4},{5,6},{7,8},{9,10},{11,12},{14,15},{16,17},{19,20},{21... | collective-permute-start | bytes 1572872 | tf_op jit(solution)/shard_map/rowpanel/ppermute | solution.py:229
  92.5 0.1 pad_add_fusion.ids_ref
  92.6 13.2 %factor_second.1 = (f32[256,512]{1,0:T(8,128)S(1)}, f32[256,512]{1,0:T(8,128)S(1)}, f32[2,128]{1,0:T(2,128)S(1)}) custom-call(f32[256,896]{1,0:T(8,128)S(1)} %bitcast.19, f32[256,256]{1,0:T(8,128)S(1)} %get-tuple-element.27.inv0_ref), custom_call_target="tpu_custom_call" | custom-call | flops 67108864 | bytes 41943040 | tf_op jit(solution)/shard_map/factor_second/pallas_call | solution.py:215
  105.7 0.0 collective-permute-done.11.moved_ref
  105.7 7.5 %finish.1 = (f32[256,512]{1,0:T(8,128)}, f32[64,256]{1,0:T(8,128)}, f32[1,64]{1,0:T(1,128)}) custom-call(s32[3]{0:T(128)S(1)} %pad_add_fusion.ids_ref, f32[256,512]{1,0:T(8,128)S(1)} %add_select_fusion.panel_ref, f32[256,512]{1,0:T(8,128)} %collective-permute-done.11.moved_ref, f32[256,1152]{1,0:T(8,128)S(1)} %bitcast.20, f32[256,256]{1,0:T(8,128)S(1)} %copy-done.3, ...), custom_call_target="tpu_custom_call" | custom-call | flops 67108864 | bytes 41943040 | tf_op jit(solution)/shard_map/finish/pallas_call | solution.py:215
  (13 shorter events, 0.1 us)
Async XLA Ops:
  0.6 23.5 %copy-start.1 = (f32[64,256]{1,0:T(8,128)S(1)}, f32[64,256]{1,0:T(8,128)}, u32[]{:S(2)}) copy-start(f32[64,256]{1,0:T(8,128)} %obs_ref.1) | copy-start | bytes 196612
  19.4 0.7 collective-permute-start
  20.1 2.6 %collective-permute-start.1 = (f32[8,768]{1,0:T(8,128)S(1)}, f32[8,768]{1,0:T(8,128)S(1)}, u32[]{:S(2)}, u32[]{:S(2)}) collective-permute-start(f32[8,768]{1,0:T(8,128)S(1)} %pad_maximum_fusion.1), channel_id=1, source_target_pairs={{0,11},{16,27},{32,43},{48,59},{64,75},{80,91},{96,107},{112,123},... | collective-permute-start | bytes 73736 | tf_op jit(solution)/shard_map/diag/ppermute | solution.py:229
  20.8 15.4 %collective-permute-start.5 = (f32[8,768]{1,0:T(8,128)S(1)}, f32[8,768]{1,0:T(8,128)S(1)}, u32[]{:S(2)}, u32[]{:S(2)}) collective-permute-start(f32[8,768]{1,0:T(8,128)S(1)} %broadcast_select_fusion), channel_id=1, source_target_pairs={{0,14},{5,3},{16,30},{21,19},{32,46},{37,35},{48,62},{53,51},{64,7... | collective-permute-start | bytes 73736 | tf_op jit(solution)/shard_map/diag/ppermute | solution.py:229
  22.1 14.1 %collective-permute-start.4 = (f32[8,768]{1,0:T(8,128)S(1)}, f32[8,768]{1,0:T(8,128)S(1)}, u32[]{:S(2)}, u32[]{:S(2)}) collective-permute-start(f32[8,768]{1,0:T(8,128)S(1)} %broadcast_select_fusion), channel_id=1, source_target_pairs={{0,2},{5,7},{16,18},{21,23},{32,34},{37,39},{48,50},{53,55},{64,66... | collective-permute-start | bytes 73736 | tf_op jit(solution)/shard_map/diag/ppermute | solution.py:229
  22.8 13.4 %collective-permute-start.3 = (f32[8,768]{1,0:T(8,128)S(1)}, f32[8,768]{1,0:T(8,128)S(1)}, u32[]{:S(2)}, u32[]{:S(2)}) collective-permute-start(f32[8,768]{1,0:T(8,128)S(1)} %broadcast_select_fusion.1), channel_id=1, source_target_pairs={{11,9},{27,25},{43,41},{59,57},{75,73},{91,89},{107,105},{123,121}... | collective-permute-start | bytes 73736 | tf_op jit(solution)/shard_map/diag/ppermute | solution.py:229
  23.5 12.7 %collective-permute-start.2 = (f32[8,768]{1,0:T(8,128)S(1)}, f32[8,768]{1,0:T(8,128)S(1)}, u32[]{:S(2)}, u32[]{:S(2)}) collective-permute-start(f32[8,768]{1,0:T(8,128)S(1)} %broadcast_select_fusion.1), channel_id=1, source_target_pairs={{11,13},{27,29},{43,45},{59,61},{75,77},{91,93},{107,109},{123,125... | collective-permute-start | bytes 73736 | tf_op jit(solution)/shard_map/diag/ppermute | solution.py:229
  36.2 2.2 %collective-permute-start.6 = (f32[8,768]{1,0:T(8,128)S(1)}, f32[8,768]{1,0:T(8,128)S(1)}, u32[]{:S(2)}, u32[]{:S(2)}) collective-permute-start(f32[8,768]{1,0:T(8,128)S(1)} %select_select_fusion), channel_id=1, source_target_pairs={{0,1},{3,4},{5,6},{7,8},{9,10},{11,12},{14,15},{16,17},{19,20},{21... | collective-permute-start | bytes 73736 | tf_op jit(solution)/shard_map/diag/ppermute | solution.py:229
  39.5 7.6 %copy-start = (f32[256,512]{1,0:T(8,128)S(1)}, f32[256,512]{1,0:T(8,128)}, u32[]{:S(2)}) copy-start(f32[256,512]{1,0:T(8,128)} %cov_ref.1) | copy-start | bytes 1572868
  39.5 22.5 %all-to-all-start.1 = ((f32[32,8,896]{2,1,0:T(8,128)}), f32[32,8,896]{2,1,0:T(8,128)S(1)}, u32[]{:S(2)}, u32[]{:S(2)}) async-start(f32[32,8,896]{2,1,0:T(8,128)} %pad_maximum_fusion), calls=%async_computation.1 | async-start | bytes 1835008 | tf_op jit(solution)/shard_map/diag/all_to_all | solution.py:261
  47.1 21.1 %collective-permute-start.8 = (f32[256,512]{1,0:T(8,128)S(1)}, f32[256,512]{1,0:T(8,128)S(1)}, u32[]{:S(2)}, u32[]{:S(2)}) collective-permute-start(f32[256,512]{1,0:T(8,128)S(1)} %copy-done), channel_id=1, source_target_pairs={{0,5},{16,21},{32,37},{48,53},{64,69},{80,85},{96,101},{112,117},{... | collective-permute-start | bytes 1572872 | tf_op jit(solution)/shard_map/rowpanel/ppermute | solution.py:229
  47.8 21.2 %collective-permute-start.7 = (f32[256,512]{1,0:T(8,128)S(1)}, f32[256,512]{1,0:T(8,128)}, u32[]{:S(2)}, u32[]{:S(2)}) collective-permute-start(f32[256,512]{1,0:T(8,128)S(1)} %copy-done), channel_id=1, source_target_pairs={{0,11},{16,27},{32,43},{48,59},{64,75},{80,91},{96,107},{112,123},... | collective-permute-start | bytes 1572872 | tf_op jit(solution)/shard_map/rowpanel/ppermute | solution.py:229
  63.2 25.8 %all-to-all-start.2 = ((f32[32,8,1152]{2,1,0:T(8,128)}), f32[32,8,1152]{2,1,0:T(8,128)S(1)}, u32[]{:S(2)}, u32[]{:S(2)}) async-start(f32[32,8,1152]{2,1,0:T(8,128)} %broadcast_in_dim.5), calls=%async_computation.2 | async-start | bytes 2359296 | tf_op jit(solution)/shard_map/columns/all_to_all | solution.py:261
  68.2 0.8 copy-start.5
  70.4 17.3 %copy-start.4 = (f32[256,512]{1,0:T(8,128)}, f32[256,512]{1,0:T(8,128)S(1)}, u32[]{:S(2)}) copy-start(f32[256,512]{1,0:T(8,128)S(1)} %add_select_fusion.1) | copy-start | bytes 1572868
  70.4 17.3 %collective-permute-start.10 = (f32[256,512]{1,0:T(8,128)S(1)}, f32[256,512]{1,0:T(8,128)}, u32[]{:S(2)}, u32[]{:S(2)}) collective-permute-start(f32[256,512]{1,0:T(8,128)S(1)} %add_select_fusion.1), channel_id=1, source_target_pairs={{0,14},{5,3},{11,9},{16,30},{21,19},{27,25},{32,46},{37,35},{43,41... | collective-permute-start | bytes 1572872 | tf_op jit(solution)/shard_map/rowpanel/ppermute | solution.py:229
  71.7 16.0 %collective-permute-start.9 = (f32[256,512]{1,0:T(8,128)S(1)}, f32[256,512]{1,0:T(8,128)}, u32[]{:S(2)}, u32[]{:S(2)}) collective-permute-start(f32[256,512]{1,0:T(8,128)S(1)} %add_select_fusion.1), channel_id=1, source_target_pairs={{0,2},{5,7},{11,13},{16,18},{21,23},{27,29},{32,34},{37,39},{43,45... | collective-permute-start | bytes 1572872 | tf_op jit(solution)/shard_map/rowpanel/ppermute | solution.py:229
  84.1 0.7 copy-start.2
  89.0 16.7 %collective-permute-start.11 = (f32[256,512]{1,0:T(8,128)S(1)}, f32[256,512]{1,0:T(8,128)}, u32[]{:S(2)}, u32[]{:S(2)}) collective-permute-start(f32[256,512]{1,0:T(8,128)S(1)} %add_select_fusion.panel_ref), channel_id=1, source_target_pairs={{0,1},{3,4},{5,6},{7,8},{9,10},{11,12},{14,15},{16,17},{19,20},{21... | collective-permute-start | bytes 1572872 | tf_op jit(solution)/shard_map/rowpanel/ppermute | solution.py:229
  92.5 13.3 %copy-start.3 = (f32[256,256]{1,0:T(8,128)S(1)}, f32[256,256]{1,0:T(8,128)}, u32[]{:S(2)}) copy-start(f32[256,256]{1,0:T(8,128)} %copy-done.2) | copy-start | bytes 786436

commit v8 on v7

--- a/solution.py
+++ b/solution.py
@@ -19,6 +19,23 @@
 def dot_t(a, b):
     dims = (((1,), (1,)), ((), ()))
     return lax.dot_general(a, b, dims, precision=HI, preferred_element_type=jnp.float32)
+
+
+def split(value):
+    high = value.astype(jnp.bfloat16)
+    rest = value - high.astype(jnp.float32)
+    middle = rest.astype(jnp.bfloat16)
+    low = (rest - middle.astype(jnp.float32)).astype(jnp.bfloat16)
+    return high, middle, low
+
+
+def outer_sum(left, right):
+    a1, a2, a3 = split(jnp.concatenate(left, axis=0))
+    b1, b2, b3 = split(jnp.concatenate(right, axis=0))
+    a = jnp.concatenate([a1, a1, a2, a1, a2, a3], axis=0)
+    b = jnp.concatenate([b1, b2, b1, b3, b2, b1], axis=0)
+    dims = (((0,), (0,)), ((), ()))
+    return lax.dot_general(a, b, dims, preferred_element_type=jnp.float32)
 
 
 def factor_tile(blocks):
@@ -64,10 +81,7 @@
         right.append(jnp.where(lane < stop * SUB, w_block, u_block))
         if b + 1 == stop:
             if stop < count:
-                far = lax.dot_general(
-                    jnp.concatenate(left[start:], axis=0), jnp.concatenate(right[start:], axis=0),
-                    (((0,), (0,)), ((), ())), precision=HI, preferred_element_type=jnp.float32,
-                )
+                far = outer_sum(left[start:], right[start:])
                 keep = (lane < start * SUB) | (lane >= stop * SUB)
                 for i in range(stop, count):
                     blocks[i] = jnp.where(keep, blocks[i], 0.0) - far[i * SUB : (i + 1) * SUB]
@@ -90,53 +104,64 @@
     return upper, inverse
 
 
-def eliminate(work, low_ref, inv_ref, diag_ref):
-    size = work.shape[0]
-    row_id = lax.broadcasted_iota(jnp.int32, (size, LANES), 0)
-    col_id = lax.broadcasted_iota(jnp.int32, (LANES, size), 1)
+def eliminate(corner, below, last, low_ref, inv_ref, diag_ref, tile_here, mid_here):
     square = (LANES, LANES)
     on_diag = lax.broadcasted_iota(jnp.int32, square, 0) == lax.broadcasted_iota(
         jnp.int32, square, 1
     )
+    zero = jnp.zeros(square, jnp.float32)
+    low_ref[:LANES, LANES:] = zero
+    inv_ref[:LANES, LANES:] = zero
+    tile_here[...] = corner()
 
     def step(t, carry):
-        base = pl.multiple_of(t * LANES, LANES)
-        tile_rows = pl.ds(base, LANES)
-        here = [work[pl.ds(base + SUB * i, SUB), tile_rows] for i in range(LANES // SUB)]
-        up, inv = factor_tile(here)
+        tile_rows = pl.ds(pl.multiple_of(t * LANES, LANES), LANES)
+        up, inv = factor_tile(
+            [tile_here[SUB * i : SUB * (i + 1), :] for i in range(LANES // SUB)]
+        )
         up = jnp.concatenate(up, axis=0)
         inv = jnp.concatenate(inv, axis=0)
         diag_ref[pl.ds(t, 1), :] = jnp.sum(jnp.where(on_diag, up, 0.0), axis=0, keepdims=True)
-        across = dot(inv, work[tile_rows, :])
-        below = dot_t(work[:, tile_rows], inv)
-        below = jnp.where(row_id >= base + LANES, below, 0.0)
-        low_ref[:, tile_rows] = below
         low_ref[tile_rows, tile_rows] = up.T
-        inv_ref[tile_rows, :] = jnp.where(col_id < base, across, 0.0)
         inv_ref[tile_rows, tile_rows] = inv
-        work[tile_rows, :] = across
-        work[tile_rows, tile_rows] = inv
-        across = work[tile_rows, :]
-        work[:, tile_rows] = jnp.zeros((size, LANES), jnp.float32)
-        work[...] = work[...] - dot(below, across)
+
+        @pl.when(t == 0)
+        def _():
+            left = dot_t(below(), inv)
+            low_ref[LANES:, :LANES] = left
+            tile_here[...] = last() - dot_t(left, left)
+            mid_here[...] = dot(left, inv)
+
+        @pl.when(t == 1)
+        def _():
+            inv_ref[LANES:, :LANES] = -dot(inv, mid_here[...])
+
         return carry
 
-    lax.fori_loop(0, size // LANES, step, 0)
-
-
-def first_kernel(d_ref, low_ref, inv_ref, diag_ref, work):
+    lax.fori_loop(0, 2, step, 0)
+
+
+def first_kernel(d_ref, both_ref, diag_ref, tile_here, mid_here):
+    size = 2 * LANES
+    eliminate(
+        lambda: d_ref[:LANES, :LANES], lambda: d_ref[LANES:, :LANES],
+        lambda: d_ref[LANES:, LANES:size], both_ref.at[:, :size], both_ref.at[:, size:],
+        diag_ref, tile_here, mid_here,
+    )
+
+
+def second_kernel(
+    d_ref, both0_ref, low_ref, inv_ref, diag_ref, work, low_here, inv_here, tile_here, mid_here
+):
     tile = work.shape[0]
-    work[...] = d_ref[:, :tile]
-    eliminate(work, low_ref, inv_ref, diag_ref)
-
-
-def second_kernel(d_ref, inv0_ref, low_ref, inv_ref, diag_ref, work, low_here, inv_here):
-    tile = inv0_ref.shape[0]
-    inv0 = inv0_ref[...]
+    inv0 = both0_ref[:, tile:]
     left = dot_t(d_ref[:, tile : 2 * tile], inv0)
     low_ref[:, :tile] = left
     work[...] = d_ref[:, 2 * tile : 3 * tile] - dot_t(left, left)
-    eliminate(work, low_here, inv_here, diag_ref)
+    eliminate(
+        lambda: work[:LANES, :LANES], lambda: work[LANES:, :LANES], lambda: work[LANES:, LANES:],
+        low_here, inv_here, diag_ref, tile_here, mid_here,
+    )
     low_ref[:, tile:] = low_here[...]
     inv1 = inv_here[...]
     inv_ref[:, tile:] = inv1
@@ -144,13 +169,13 @@
 
 
 def finish_kernel(
-    ids_ref, panel_ref, moved_ref, wide_ref, low0_ref, inv0_ref, diag0_ref, low1_ref, inv1_ref,
+    ids_ref, panel_ref, moved_ref, wide_ref, both0_ref, diag0_ref, low1_ref, inv1_ref,
     diag1_ref, cov_ref, obs_ref, out_ref, solved_ref, site_ref, rows_here,
 ):
     tile, wide = cov_ref.shape
     nrhs = obs_ref.shape[0]
     row, col, is_new = ids_ref[0], ids_ref[1], ids_ref[2]
-    inv0 = inv0_ref[...]
+    inv0 = both0_ref[:, tile:]
     inv10 = inv1_ref[:, :tile]
     inv11 = inv1_ref[:, tile:]
 
@@ -181,7 +206,7 @@
 
     @pl.when((row == 0) & (col == 0))
     def _():
-        out_ref[:, :tile] = low0_ref[...]
+        out_ref[:, :tile] = both0_ref[:, :tile]
 
     @pl.when((row == 1) & (col == 0))
     def _():
@@ -237,15 +262,12 @@
 
 
 def spread_step(value, hops, holders, extent, position):
-    arrived, targets = None, []
-    for hop in hops:
-        moved, reached = send(value, hop, holders, extent)
-        arrived = moved if arrived is None else arrived + moved
-        targets += reached
-    is_new = jnp.zeros((), bool)
-    for target in targets:
-        is_new = is_new | (position == target)
-    return jnp.where(is_new, arrived, value), sorted(set(holders) | set(targets))
+    sent = [send(value, hop, holders, extent) for hop in hops]
+    reached = set(holders)
+    for moved, targets in sent:
+        value = pick(value, moved, targets, position)
+        reached |= set(targets)
+    return value, sorted(reached)
 
 
 def shards(covariance, observations):
@@ -296,19 +318,19 @@
         columns = columns.reshape(tile, -1)
 
     with jax.named_scope("rowpanel"):
-        panel, holders = spread_step(panel, (-5, 5), [0], cols, col)
-        panel, holders = spread_step(panel, (2, -2), holders, cols, col)
-
-    low0, inv0, diag0 = call(
-        first_kernel, "factor_first", [(tile, tile), (tile, tile), (tile // LANES, LANES)],
-        [(tile, tile)], diag,
-    )
-    inv0, panel, columns = lax.optimization_barrier((inv0, panel, columns))
+        panel, holders = spread_step(panel, (5, -5), [0], cols, col)
+        panel, holders = spread_step(panel, (-2, 2), holders, cols, col)
+
+    square = (LANES, LANES)
+    both0, diag0 = call(
+        first_kernel, "factor_first", [(tile, wide), (tile // LANES, LANES)], [square] * 2, diag
+    )
+    both0, panel, columns = lax.optimization_barrier((both0, panel, columns))
     with jax.named_scope("rowpanel"):
         moved, reached = send(panel, 1, last, cols)
     low1, inv1, diag1 = call(
         second_kernel, "factor_second", [(tile, wide), (tile, wide), (tile // LANES, LANES)],
-        [(tile, tile)] * 3, diag, inv0,
+        [(tile, tile)] * 3 + [square] * 2, diag, both0,
     )
 
     is_new = jnp.zeros((), bool)
@@ -317,7 +339,7 @@
     ids = jnp.stack([row, col, is_new.astype(jnp.int32)])
     factored, solved, site = call(
         finish_kernel, "finish", [(tile, wide), (nrhs, tile), (1, nrhs)], [(tile, wide)],
-        panel, moved, columns, low0, inv0, diag0, low1, inv1, diag1, covariance, observations,
+        panel, moved, columns, both0, diag0, low1, inv1, diag1, covariance, observations,
         ids=ids,
     )
     return factored, solved, site.reshape(nrhs)

time: 114 us -> 112 us (0.982)
  the two profiles are of different devices: /device:TPU:99 before, /device:TPU:66 now
where the time goes in v8:
time: 112 us; the launch traced here: 111 us
  waiting for transfers between devices  35.6 us (32%)
  Pallas kernels  29.2 us (26%)
  starting transfers between devices  21.9 us (20%)
  blocking collectives  18.3 us (16%)
  other arithmetic  4.2 us (4%)
  local copies, waits for them, and re-layouts  1.37 us (1%)
    pallas_call x3, Pallas kernels, call(): pl.pallas_call(kernel, out_shape=[jax.ShapeDtypeStruct(shape, jnp.float32...  29.2 us
    ppermute x12, waiting for transfers between devices, send(): return (lax.ppermute(value, 'col', pairs), [target for _, target in pairs])  22.9 us
    all_to_all x1, blocking collectives, exchange(): return lax.all_to_all(value, 'row', split_axis=0, concat_axis=0, tiled=True)  18.3 us
    all_to_all x2, waiting for transfers between devices, exchange(): return lax.all_to_all(value, 'row', split_axis=0, concat_axis=0, tiled=True)  12.6 us
    ppermute x12, starting transfers between devices, send(): return (lax.ppermute(value, 'col', pairs), [target for _, target in pairs])  11.6 us
    all_to_all x2, starting transfers between devices, exchange(): return lax.all_to_all(value, 'row', split_axis=0, concat_axis=0, tiled=True)  10.2 us
    select_n x6, other arithmetic, pick(): return jnp.where(is_new, moved, value)  3.12 us
  transfers between devices with their start and end apart: 14, of which 3 were waited for; matrix products, arithmetic and copies ran while one was open for 4% of the time, Pallas kernels for 19%

profile of v8, /device:TPU:66, one launch (start us, length us, event | category | flops | bytes accessed | tf_op | source)
XLA Modules:
  0.0 111.5 jit_solution(3439060700075238985)
XLA Ops:
  0.6 0.0 copy-start.2
  0.6 18.3 %all_to_all.15 = f32[32,8,512]{2,1,0:T(8,128)S(1)} all-to-all(f32[32,8,512]{2,1,0:T(8,128)} %bitcast.21), channel_id=1, replica_groups=mesh['row'=32,'col'=16] {'row'}, dimensions={0} | all-to-all | bytes 1048576 | tf_op jit(solution)/shard_map/scatter/all_to_all | solution.py:283
  18.9 0.7 collective-permute-start
  19.6 0.0 collective-permute-done
  19.6 0.7 collective-permute-start.1
  20.3 0.7 collective-permute-start.5
  21.0 1.3 %collective-permute-start.4 = (f32[8,768]{1,0:T(8,128)S(1)}, f32[8,768]{1,0:T(8,128)S(1)}, u32[]{:S(2)}, u32[]{:S(2)}) collective-permute-start(f32[8,768]{1,0:T(8,128)S(1)} %broadcast_select_fusion), channel_id=1, source_target_pairs={{0,2},{5,7},{16,18},{21,23},{32,34},{37,39},{48,50},{53,55},{64,66... | collective-permute-start | bytes 73736 | tf_op jit(solution)/shard_map/diag/ppermute | solution.py:254
  22.3 0.0 collective-permute-done.1
  22.3 0.7 collective-permute-start.3
  23.0 0.7 collective-permute-start.2
  23.6 0.0 copy-done.2
  23.7 0.1 copy.6
  23.8 0.0 collective-permute-done.5
  23.8 14.3 %collective-permute-done.4 = f32[8,768]{1,0:T(8,128)S(1)} collective-permute-done((f32[8,768]{1,0:T(8,128)S(1)}, f32[8,768]{1,0:T(8,128)S(1)}, u32[]{:S(2)}, u32[]{:S(2)}) %collective-permute-start.4) | collective-permute-done | bytes 24608 | tf_op jit(solution)/shard_map/diag/ppermute | solution.py:254
  38.1 0.0 collective-permute-done.3
  38.1 0.0 collective-permute-done.2
  38.1 0.7 collective-permute-start.6
  38.8 0.0 collective-permute-done.6
  38.8 0.1 broadcast_in_dim.4
  38.9 1.0 pad_maximum_fusion
  39.9 0.0 copy-start
  39.9 5.2 %all-to-all-start.1 = ((f32[32,8,896]{2,1,0:T(8,128)}), f32[32,8,896]{2,1,0:T(8,128)S(1)}, u32[]{:S(2)}, u32[]{:S(2)}) async-start(f32[32,8,896]{2,1,0:T(8,128)} %pad_maximum_fusion), calls=%async_computation.1 | async-start | bytes 1835008 | tf_op jit(solution)/shard_map/diag/all_to_all | solution.py:283
  45.1 0.0 copy-done
  45.1 0.7 collective-permute-start.8
  45.8 1.5 %collective-permute-start.7 = (f32[256,512]{1,0:T(8,128)S(1)}, f32[256,512]{1,0:T(8,128)}, u32[]{:S(2)}, u32[]{:S(2)}) collective-permute-start(f32[256,512]{1,0:T(8,128)S(1)} %copy-done), channel_id=1, source_target_pairs={{0,11},{16,27},{32,43},{48,59},{64,75},{80,91},{96,107},{112,123},... | collective-permute-start | bytes 1572872 | tf_op jit(solution)/shard_map/rowpanel/ppermute | solution.py:254
  47.3 12.6 %all-to-all-done.1 = f32[32,8,896]{2,1,0:T(8,128)S(1)} async-done(((f32[32,8,896]{2,1,0:T(8,128)}), f32[32,8,896]{2,1,0:T(8,128)S(1)}, u32[]{:S(2)}, u32[]{:S(2)}) %all-to-all-start.1) | async-done | bytes 917536 | tf_op jit(solution)/shard_map/diag/all_to_all | solution.py:283
  59.9 0.1 concatenate.11
  60.0 1.1 broadcast_in_dim.5
  61.1 5.1 %all-to-all-start.2 = ((f32[32,8,1152]{2,1,0:T(8,128)}), f32[32,8,1152]{2,1,0:T(8,128)S(1)}, u32[]{:S(2)}, u32[]{:S(2)}) async-start(f32[32,8,1152]{2,1,0:T(8,128)} %broadcast_in_dim.5), calls=%async_computation.2 | async-start | bytes 2359296 | tf_op jit(solution)/shard_map/columns/all_to_all | solution.py:283
  66.2 0.0 collective-permute-done.8
  66.2 0.0 collective-permute-done.7
  66.2 1.0 select_select_fusion.1
  67.1 1.5 %collective-permute-start.10 = (f32[256,512]{1,0:T(8,128)}, f32[256,512]{1,0:T(8,128)}, u32[]{:S(2)}, u32[]{:S(2)}) collective-permute-start(f32[256,512]{1,0:T(8,128)} %select_select_fusion.1), channel_id=1, source_target_pairs={{0,14},{5,3},{11,9},{16,30},{21,19},{27,25},{32,46},{37,35},{43,41... | collective-permute-start | bytes 1572872 | tf_op jit(solution)/shard_map/rowpanel/ppermute | solution.py:254
  68.6 1.3 %collective-permute-start.9 = (f32[256,512]{1,0:T(8,128)}, f32[256,512]{1,0:T(8,128)}, u32[]{:S(2)}, u32[]{:S(2)}) collective-permute-start(f32[256,512]{1,0:T(8,128)} %select_select_fusion.1), channel_id=1, source_target_pairs={{0,2},{5,7},{11,13},{16,18},{21,23},{27,29},{32,34},{37,39},{43,45... | collective-permute-start | bytes 1572872 | tf_op jit(solution)/shard_map/rowpanel/ppermute | solution.py:254
  69.9 9.8 %factor_first.1 = (f32[256,512]{1,0:T(8,128)S(1)}, f32[2,128]{1,0:T(2,128)S(1)}) custom-call(f32[256,896]{1,0:T(8,128)S(1)} %bitcast.18), custom_call_target="tpu_custom_call" | custom-call | flops 67108864 | bytes 41943040 | tf_op jit(solution)/shard_map/factor_first/pallas_call | solution.py:240
  79.6 0.0 collective-permute-done.10
  79.7 8.6 %collective-permute-done.9 = f32[256,512]{1,0:T(8,128)} collective-permute-done((f32[256,512]{1,0:T(8,128)}, f32[256,512]{1,0:T(8,128)}, u32[]{:S(2)}, u32[]{:S(2)}) %collective-permute-start.9) | collective-permute-done | bytes 524320 | tf_op jit(solution)/shard_map/rowpanel/ppermute | solution.py:254
  88.3 2.1 %select_select_fusion.panel_ref = f32[256,512]{1,0:T(8,128)} fusion(f32[256,512]{1,0:T(8,128)} %collective-permute-done.9, f32[256,512]{1,0:T(8,128)} %collective-permute-done.10, f32[256,512]{1,0:T(8,128)} %select_select_fusion.1, pred[]{:T(512)S(6)} %or.47, pred[]{:T(512)S(6)} %or.46), kind=kLoop, calls=%fused_computation.1 | loop fusion | flops 262144 | bytes 2097154 | tf_op jit(solution)/shard_map/rowpanel/jit(_where)/select_n | solution.py:261
  90.4 0.0 all-to-all-done.2
  90.4 1.5 %collective-permute-start.11 = (f32[256,512]{1,0:T(8,128)}, f32[256,512]{1,0:T(8,128)}, u32[]{:S(2)}, u32[]{:S(2)}) collective-permute-start(f32[256,512]{1,0:T(8,128)} %select_select_fusion.panel_ref), channel_id=1, source_target_pairs={{0,1},{3,4},{5,6},{7,8},{9,10},{11,12},{14,15},{16,17},{19,20},{21... | collective-permute-start | bytes 1572872 | tf_op jit(solution)/shard_map/rowpanel/ppermute | solution.py:254
  91.9 0.0 copy-start.1
  91.9 0.1 pad_add_fusion.ids_ref
  92.0 11.9 %factor_second.1 = (f32[256,512]{1,0:T(8,128)S(1)}, f32[256,512]{1,0:T(8,128)S(1)}, f32[2,128]{1,0:T(2,128)S(1)}) custom-call(f32[256,896]{1,0:T(8,128)S(1)} %bitcast.19, f32[256,512]{1,0:T(8,128)S(1)} %get-tuple-element.25.both0_ref), custom_call_target="tpu_custom_call" | custom-call | flops 67108864 | bytes 41943040 | tf_op jit(solution)/shard_map/factor_second/pallas_call | solution.py:240
  103.9 0.0 collective-permute-done.11.moved_ref
  103.9 0.0 copy-done.1
  103.9 7.5 %finish.1 = (f32[256,512]{1,0:T(8,128)}, f32[64,256]{1,0:T(8,128)}, f32[1,64]{1,0:T(1,128)}) custom-call(s32[3]{0:T(128)S(1)} %pad_add_fusion.ids_ref, f32[256,512]{1,0:T(8,128)S(1)} %copy-done.1, f32[256,512]{1,0:T(8,128)} %collective-permute-done.11.moved_ref, f32[256,1152]{1,0:T(8,128)S(1)} %bitcast.20, f32[256,512]{1,0:T(8,128)S(1)} %get-tuple-element.25.both0_ref, ...), custom_call_target="tpu_custom_call" | custom-call | flops 67108864 | bytes 41943040 | tf_op jit(solution)/shard_map/finish/pallas_call | solution.py:240
  (9 shorter events, 0.1 us)
Async XLA Ops:
  0.6 23.0 %copy-start.2 = (f32[64,256]{1,0:T(8,128)S(1)}, f32[64,256]{1,0:T(8,128)}, u32[]{:S(2)}) copy-start(f32[64,256]{1,0:T(8,128)} %obs_ref.1) | copy-start | bytes 196612
  18.9 0.7 collective-permute-start
  19.6 2.6 %collective-permute-start.1 = (f32[8,768]{1,0:T(8,128)S(1)}, f32[8,768]{1,0:T(8,128)S(1)}, u32[]{:S(2)}, u32[]{:S(2)}) collective-permute-start(f32[8,768]{1,0:T(8,128)S(1)} %pad_maximum_fusion.1), channel_id=1, source_target_pairs={{0,11},{16,27},{32,43},{48,59},{64,75},{80,91},{96,107},{112,123},... | collective-permute-start | bytes 73736 | tf_op jit(solution)/shard_map/diag/ppermute | solution.py:254
  20.3 3.5 %collective-permute-start.5 = (f32[8,768]{1,0:T(8,128)S(1)}, f32[8,768]{1,0:T(8,128)S(1)}, u32[]{:S(2)}, u32[]{:S(2)}) collective-permute-start(f32[8,768]{1,0:T(8,128)S(1)} %broadcast_select_fusion), channel_id=1, source_target_pairs={{0,14},{5,3},{16,30},{21,19},{32,46},{37,35},{48,62},{53,51},{64,7... | collective-permute-start | bytes 73736 | tf_op jit(solution)/shard_map/diag/ppermute | solution.py:254
  21.0 17.1 %collective-permute-start.4 = (f32[8,768]{1,0:T(8,128)S(1)}, f32[8,768]{1,0:T(8,128)S(1)}, u32[]{:S(2)}, u32[]{:S(2)}) collective-permute-start(f32[8,768]{1,0:T(8,128)S(1)} %broadcast_select_fusion), channel_id=1, source_target_pairs={{0,2},{5,7},{16,18},{21,23},{32,34},{37,39},{48,50},{53,55},{64,66... | collective-permute-start | bytes 73736 | tf_op jit(solution)/shard_map/diag/ppermute | solution.py:254
  22.3 15.8 %collective-permute-start.3 = (f32[8,768]{1,0:T(8,128)S(1)}, f32[8,768]{1,0:T(8,128)S(1)}, u32[]{:S(2)}, u32[]{:S(2)}) collective-permute-start(f32[8,768]{1,0:T(8,128)S(1)} %broadcast_select_fusion.1), channel_id=1, source_target_pairs={{11,9},{27,25},{43,41},{59,57},{75,73},{91,89},{107,105},{123,121}... | collective-permute-start | bytes 73736 | tf_op jit(solution)/shard_map/diag/ppermute | solution.py:254
  23.0 15.1 %collective-permute-start.2 = (f32[8,768]{1,0:T(8,128)S(1)}, f32[8,768]{1,0:T(8,128)S(1)}, u32[]{:S(2)}, u32[]{:S(2)}) collective-permute-start(f32[8,768]{1,0:T(8,128)S(1)} %broadcast_select_fusion.1), channel_id=1, source_target_pairs={{11,13},{27,29},{43,45},{59,61},{75,77},{91,93},{107,109},{123,125... | collective-permute-start | bytes 73736 | tf_op jit(solution)/shard_map/diag/ppermute | solution.py:254
  38.1 0.7 collective-permute-start.6
  39.9 5.2 %copy-start = (f32[256,512]{1,0:T(8,128)S(1)}, f32[256,512]{1,0:T(8,128)}, u32[]{:S(2)}) copy-start(f32[256,512]{1,0:T(8,128)} %cov_ref.1) | copy-start | bytes 1572868
  39.9 20.0 %all-to-all-start.1 = ((f32[32,8,896]{2,1,0:T(8,128)}), f32[32,8,896]{2,1,0:T(8,128)S(1)}, u32[]{:S(2)}, u32[]{:S(2)}) async-start(f32[32,8,896]{2,1,0:T(8,128)} %pad_maximum_fusion), calls=%async_computation.1 | async-start | bytes 1835008 | tf_op jit(solution)/shard_map/diag/all_to_all | solution.py:283
  45.1 21.1 %collective-permute-start.8 = (f32[256,512]{1,0:T(8,128)S(1)}, f32[256,512]{1,0:T(8,128)S(1)}, u32[]{:S(2)}, u32[]{:S(2)}) collective-permute-start(f32[256,512]{1,0:T(8,128)S(1)} %copy-done), channel_id=1, source_target_pairs={{0,5},{16,21},{32,37},{48,53},{64,69},{80,85},{96,101},{112,117},{... | collective-permute-start | bytes 1572872 | tf_op jit(solution)/shard_map/rowpanel/ppermute | solution.py:254
  45.8 20.4 %collective-permute-start.7 = (f32[256,512]{1,0:T(8,128)S(1)}, f32[256,512]{1,0:T(8,128)}, u32[]{:S(2)}, u32[]{:S(2)}) collective-permute-start(f32[256,512]{1,0:T(8,128)S(1)} %copy-done), channel_id=1, source_target_pairs={{0,11},{16,27},{32,43},{48,59},{64,75},{80,91},{96,107},{112,123},... | collective-permute-start | bytes 1572872 | tf_op jit(solution)/shard_map/rowpanel/ppermute | solution.py:254
  61.1 29.3 %all-to-all-start.2 = ((f32[32,8,1152]{2,1,0:T(8,128)}), f32[32,8,1152]{2,1,0:T(8,128)S(1)}, u32[]{:S(2)}, u32[]{:S(2)}) async-start(f32[32,8,1152]{2,1,0:T(8,128)} %broadcast_in_dim.5), calls=%async_computation.2 | async-start | bytes 2359296 | tf_op jit(solution)/shard_map/columns/all_to_all | solution.py:283
  67.1 12.5 %collective-permute-start.10 = (f32[256,512]{1,0:T(8,128)}, f32[256,512]{1,0:T(8,128)}, u32[]{:S(2)}, u32[]{:S(2)}) collective-permute-start(f32[256,512]{1,0:T(8,128)} %select_select_fusion.1), channel_id=1, source_target_pairs={{0,14},{5,3},{11,9},{16,30},{21,19},{27,25},{32,46},{37,35},{43,41... | collective-permute-start | bytes 1572872 | tf_op jit(solution)/shard_map/rowpanel/ppermute | solution.py:254
  68.6 19.7 %collective-permute-start.9 = (f32[256,512]{1,0:T(8,128)}, f32[256,512]{1,0:T(8,128)}, u32[]{:S(2)}, u32[]{:S(2)}) collective-permute-start(f32[256,512]{1,0:T(8,128)} %select_select_fusion.1), channel_id=1, source_target_pairs={{0,2},{5,7},{11,13},{16,18},{21,23},{27,29},{32,34},{37,39},{43,45... | collective-permute-start | bytes 1572872 | tf_op jit(solution)/shard_map/rowpanel/ppermute | solution.py:254
  90.4 13.5 %collective-permute-start.11 = (f32[256,512]{1,0:T(8,128)}, f32[256,512]{1,0:T(8,128)}, u32[]{:S(2)}, u32[]{:S(2)}) collective-permute-start(f32[256,512]{1,0:T(8,128)} %select_select_fusion.panel_ref), channel_id=1, source_target_pairs={{0,1},{3,4},{5,6},{7,8},{9,10},{11,12},{14,15},{16,17},{19,20},{21... | collective-permute-start | bytes 1572872 | tf_op jit(solution)/shard_map/rowpanel/ppermute | solution.py:254
  91.9 12.0 %copy-start.1 = (f32[256,512]{1,0:T(8,128)S(1)}, f32[256,512]{1,0:T(8,128)}, u32[]{:S(2)}) copy-start(f32[256,512]{1,0:T(8,128)} %select_select_fusion.panel_ref) | copy-start | bytes 1572868

commit v9 on v8

--- a/solution.py
+++ b/solution.py
@@ -168,26 +168,42 @@
     inv_ref[:, :tile] = -dot(inv1, dot(low_ref[:, :tile], inv0))
 
 
+def parts_dot(a, b):
+    a1, a2, a3 = split(a)
+    b1, b2, b3 = split(b)
+    a = jnp.concatenate([a1, a1, a2, a1, a2, a3], axis=1)
+    b = jnp.concatenate([b1, b2, b1, b3, b2, b1], axis=0)
+    return jnp.dot(a, b, preferred_element_type=jnp.float32)
+
+
+def parts_dot_t(a, b):
+    a1, a2, a3 = split(a)
+    b1, b2, b3 = split(b)
+    a = jnp.concatenate([a1, a1, a2, a1, a2, a3], axis=1)
+    b = jnp.concatenate([b1, b2, b1, b3, b2, b1], axis=1)
+    dims = (((1,), (1,)), ((), ()))
+    return lax.dot_general(a, b, dims, preferred_element_type=jnp.float32)
+
+
 def finish_kernel(
-    ids_ref, panel_ref, moved_ref, wide_ref, both0_ref, diag0_ref, low1_ref, inv1_ref,
+    ids_ref, panel_ref, back_ref, ahead_ref, next_ref, prior_ref, rest_ref, wide_ref, both0_ref, diag0_ref, low1_ref, inv1_ref,
     diag1_ref, cov_ref, obs_ref, out_ref, solved_ref, site_ref, rows_here,
 ):
     tile, wide = cov_ref.shape
     nrhs = obs_ref.shape[0]
-    row, col, is_new = ids_ref[0], ids_ref[1], ids_ref[2]
+    row, col, source = ids_ref[0], ids_ref[1], ids_ref[2]
     inv0 = both0_ref[:, tile:]
     inv10 = inv1_ref[:, :tile]
     inv11 = inv1_ref[:, tile:]
 
-    rows_here[...] = panel_ref[...]
-
-    @pl.when(is_new == 1)
-    def _():
-        rows_here[...] = moved_ref[...]
+    for place, ref in enumerate([panel_ref, back_ref, ahead_ref, next_ref, prior_ref, rest_ref]):
+        @pl.when(source == place)
+        def _(ref=ref):
+            rows_here[...] = ref[...]
 
     obs_both = wide_ref[:, 2 * wide : 2 * wide + 2 * nrhs]
-    z0 = dot(inv0, obs_both)[:, :nrhs]
-    z1 = dot(inv10, obs_both)[:, :nrhs] + dot(inv11, obs_both)[:, nrhs:]
+    z0 = parts_dot(inv0, obs_both)[:, :nrhs]
+    z1 = parts_dot(inv10, obs_both)[:, :nrhs] + parts_dot(inv11, obs_both)[:, nrhs:]
     quad = jnp.sum(z0 * z0 + z1 * z1, axis=0, keepdims=True)
     logs = jnp.log(diag0_ref[...]) + jnp.log(diag1_ref[...])
     site_ref[...] = -(quad + 2.0 * jnp.sum(logs)) / (4.0 * tile)
@@ -214,9 +230,9 @@
 
     @pl.when(row > 1)
     def _():
-        x0 = dot_t(rows_here[:, :tile], inv0)
-        x1 = dot_t(rows_here[...], inv1_ref[...])
-        solved_ref[...] = obs_ref[...] - (dot(x0, z0) + dot(x1, z1)).T
+        x0 = parts_dot_t(rows_here[:, :tile], inv0)
+        x1 = parts_dot_t(rows_here[...], inv1_ref[...])
+        solved_ref[...] = obs_ref[...] - (parts_dot(x0, z0) + parts_dot(x1, z1)).T
 
         @pl.when(col == 0)
         def _():
@@ -226,9 +242,9 @@
         @pl.when(col > 0)
         def _():
             c0 = wide_ref[:, :wide]
-            y0 = dot(inv0, c0)
-            y1 = dot(inv10, c0) + dot(inv11, wide_ref[:, wide : 2 * wide])
-            out_ref[...] = cov_ref[...] - dot(x0, y0) - dot(x1, y1)
+            y0 = parts_dot(inv0, c0)
+            y1 = parts_dot(inv10, c0) + parts_dot(inv11, wide_ref[:, wide : 2 * wide])
+            out_ref[...] = cov_ref[...] - parts_dot(x0, y0) - parts_dot(x1, y1)
 
 
 def call(kernel, name, outs, scratch, *args, ids=None):
@@ -319,7 +335,7 @@
 
     with jax.named_scope("rowpanel"):
         panel, holders = spread_step(panel, (5, -5), [0], cols, col)
-        panel, holders = spread_step(panel, (-2, 2), holders, cols, col)
+        sends = [send(panel, hop, holders, cols) for hop in (-2, 2)]
 
     square = (LANES, LANES)
     both0, diag0 = call(
@@ -327,19 +343,24 @@
     )
     both0, panel, columns = lax.optimization_barrier((both0, panel, columns))
     with jax.named_scope("rowpanel"):
-        moved, reached = send(panel, 1, last, cols)
+        sends += [send(panel, hop, holders, cols) for hop in (1, -1)]
+        back, backs = sends[0]
+        covered = set(holders).union(*[targets for _, targets in sends])
+        rest = [z for z in backs if (z - 1) % cols not in covered]
+        sends.append(send(back, -1, rest, cols))
     low1, inv1, diag1 = call(
         second_kernel, "factor_second", [(tile, wide), (tile, wide), (tile // LANES, LANES)],
         [(tile, tile)] * 3 + [square] * 2, diag, both0,
     )
 
-    is_new = jnp.zeros((), bool)
-    for target in reached:
-        is_new = is_new | (col == target)
-    ids = jnp.stack([row, col, is_new.astype(jnp.int32)])
+    source = jnp.zeros((), jnp.int32)
+    for place, (_, targets) in enumerate(sends):
+        for target in targets:
+            source = jnp.where(col == target, place + 1, source)
+    ids = jnp.stack([row, col, source])
     factored, solved, site = call(
         finish_kernel, "finish", [(tile, wide), (nrhs, tile), (1, nrhs)], [(tile, wide)],
-        panel, moved, columns, both0, diag0, low1, inv1, diag1, covariance, observations,
+        panel, *[moved for moved, _ in sends], columns, both0, diag0, low1, inv1, diag1, covariance, observations,
         ids=ids,
     )
     return factored, solved, site.reshape(nrhs)

time: 112 us -> 114 us (1.018)
  the two profiles are of different devices: /device:TPU:66 before, /device:TPU:1 now
where the time goes in v9:
time: 114 us; the launch traced here: 112 us
  starting transfers between devices  53.3 us (47%)
  Pallas kernels  25.5 us (22%)
  blocking collectives  22.2 us (19%)
  waiting for transfers between devices  5.25 us (5%)
  local copies, waits for them, and re-layouts  4 us (4%)
  other arithmetic  1.26 us (1%)
    ppermute x14, starting transfers between devices, send(): return (lax.ppermute(value, 'col', pairs), [target for _, target in pairs])  43.5 us
    pallas_call x3, Pallas kernels, call(): pl.pallas_call(kernel, out_shape=[jax.ShapeDtypeStruct(shape, jnp.float32...  25.5 us
    all_to_all x1, blocking collectives, exchange(): return lax.all_to_all(value, 'row', split_axis=0, concat_axis=0, tiled=True)  22.2 us
    all_to_all x2, starting transfers between devices, exchange(): return lax.all_to_all(value, 'row', split_axis=0, concat_axis=0, tiled=True)  9.8 us
    all_to_all x2, waiting for transfers between devices, exchange(): return lax.all_to_all(value, 'row', split_axis=0, concat_axis=0, tiled=True)  2.9 us
    unnamed x11, local copies, waits for them, and re-layouts  2.72 us
    ppermute x14, waiting for transfers between devices, send(): return (lax.ppermute(value, 'col', pairs), [target for _, target in pairs])  2.35 us
  transfers between devices with their start and end apart: 16, of which 4 were waited for; matrix products, arithmetic and copies ran while one was open for 1% of the time, Pallas kernels for 19%

profile of v9, /device:TPU:1, one launch (start us, length us, event | category | flops | bytes accessed | tf_op | source)
XLA Modules:
  0.0 112.5 jit_solution(2726874860435944912)
XLA Ops:
  0.6 22.2 %all_to_all.15 = f32[32,8,512]{2,1,0:T(8,128)S(1)} all-to-all(f32[32,8,512]{2,1,0:T(8,128)} %bitcast.20), channel_id=1, replica_groups=mesh['row'=32,'col'=16] {'row'}, dimensions={0} | all-to-all | bytes 1048576 | tf_op jit(solution)/shard_map/scatter/all_to_all | solution.py:299
  22.9 8.2 %collective-permute-start = (f32[8,768]{1,0:T(8,128)S(1)}, f32[8,768]{1,0:T(8,128)S(1)}, u32[]{:S(2)}, u32[]{:S(2)}) collective-permute-start(f32[8,768]{1,0:T(8,128)S(1)} %pad_maximum_fusion.1), channel_id=1, source_target_pairs={{0,5},{16,21},{32,37},{48,53},{64,69},{80,85},{96,101},{112,117},{... | collective-permute-start | bytes 73736 | tf_op jit(solution)/shard_map/diag/ppermute | solution.py:270
  31.1 0.9 collective-permute-done
  32.0 3.7 %collective-permute-start.1 = (f32[8,768]{1,0:T(8,128)S(1)}, f32[8,768]{1,0:T(8,128)S(1)}, u32[]{:S(2)}, u32[]{:S(2)}) collective-permute-start(f32[8,768]{1,0:T(8,128)S(1)} %pad_maximum_fusion.1), channel_id=1, source_target_pairs={{0,11},{16,27},{32,43},{48,59},{64,75},{80,91},{96,107},{112,123},... | collective-permute-start | bytes 73736 | tf_op jit(solution)/shard_map/diag/ppermute | solution.py:270
  35.8 1.3 %collective-permute-start.5 = (f32[8,768]{1,0:T(8,128)S(1)}, f32[8,768]{1,0:T(8,128)S(1)}, u32[]{:S(2)}, u32[]{:S(2)}) collective-permute-start(f32[8,768]{1,0:T(8,128)S(1)} %broadcast_select_fusion), channel_id=1, source_target_pairs={{0,14},{5,3},{16,30},{21,19},{32,46},{37,35},{48,62},{53,51},{64,7... | collective-permute-start | bytes 73736 | tf_op jit(solution)/shard_map/diag/ppermute | solution.py:270
  37.1 1.3 %collective-permute-start.4 = (f32[8,768]{1,0:T(8,128)S(1)}, f32[8,768]{1,0:T(8,128)S(1)}, u32[]{:S(2)}, u32[]{:S(2)}) collective-permute-start(f32[8,768]{1,0:T(8,128)S(1)} %broadcast_select_fusion), channel_id=1, source_target_pairs={{0,2},{5,7},{16,18},{21,23},{32,34},{37,39},{48,50},{53,55},{64,66... | collective-permute-start | bytes 73736 | tf_op jit(solution)/shard_map/diag/ppermute | solution.py:270
  38.4 0.0 collective-permute-done.1
  38.4 0.7 collective-permute-start.3
  39.0 0.7 collective-permute-start.2
  39.7 0.1 copy.6
  39.9 0.0 collective-permute-done.5
  39.9 0.0 collective-permute-done.4
  39.9 0.0 collective-permute-done.3
  39.9 0.0 collective-permute-done.2
  39.9 1.3 %collective-permute-start.6 = (f32[8,768]{1,0:T(8,128)S(1)}, f32[8,768]{1,0:T(8,128)S(1)}, u32[]{:S(2)}, u32[]{:S(2)}) collective-permute-start(f32[8,768]{1,0:T(8,128)S(1)} %select_select_fusion.1), channel_id=1, source_target_pairs={{0,1},{3,4},{5,6},{7,8},{9,10},{11,12},{14,15},{16,17},{19,20},{21... | collective-permute-start | bytes 73736 | tf_op jit(solution)/shard_map/diag/ppermute | solution.py:270
  41.3 0.9 collective-permute-done.6
  42.1 0.1 broadcast_in_dim.4
  42.2 1.0 pad_maximum_fusion
  43.2 5.0 %all-to-all-start.1 = ((f32[32,8,896]{2,1,0:T(8,128)}), f32[32,8,896]{2,1,0:T(8,128)S(1)}, u32[]{:S(2)}, u32[]{:S(2)}) async-start(f32[32,8,896]{2,1,0:T(8,128)} %pad_maximum_fusion), calls=%async_computation.1 | async-start | bytes 1835008 | tf_op jit(solution)/shard_map/diag/all_to_all | solution.py:299
  48.2 6.3 %collective-permute-start.8 = (f32[256,512]{1,0:T(8,128)S(1)}, f32[256,512]{1,0:T(8,128)S(1)}, u32[]{:S(2)}, u32[]{:S(2)}) collective-permute-start(f32[256,512]{1,0:T(8,128)S(1)} %copy-done), channel_id=1, source_target_pairs={{0,5},{16,21},{32,37},{48,53},{64,69},{80,85},{96,101},{112,117},{... | collective-permute-start | bytes 1572872 | tf_op jit(solution)/shard_map/rowpanel/ppermute | solution.py:270
  54.5 6.7 %collective-permute-start.7 = (f32[256,512]{1,0:T(8,128)S(1)}, f32[256,512]{1,0:T(8,128)}, u32[]{:S(2)}, u32[]{:S(2)}) collective-permute-start(f32[256,512]{1,0:T(8,128)S(1)} %copy-done), channel_id=1, source_target_pairs={{0,11},{16,27},{32,43},{48,59},{64,75},{80,91},{96,107},{112,123},... | collective-permute-start | bytes 1572872 | tf_op jit(solution)/shard_map/rowpanel/ppermute | solution.py:270
  61.2 2.9 %all-to-all-done.1 = f32[32,8,896]{2,1,0:T(8,128)S(1)} async-done(((f32[32,8,896]{2,1,0:T(8,128)}), f32[32,8,896]{2,1,0:T(8,128)S(1)}, u32[]{:S(2)}, u32[]{:S(2)}) %all-to-all-start.1) | async-done | bytes 917536 | tf_op jit(solution)/shard_map/diag/all_to_all | solution.py:299
  64.1 0.1 concatenate.11
  64.2 1.1 %broadcast_in_dim.5 = f32[32,8,1152]{2,1,0:T(8,128)} broadcast(f32[8,1152]{1,0:T(8,128)S(1)} %concatenate.11), dimensions={1,2} | broadcast | bytes 1216512 | tf_op jit(solution)/shard_map/columns/broadcast_in_dim | solution.py:333
  65.3 4.8 %all-to-all-start.2 = ((f32[32,8,1152]{2,1,0:T(8,128)}), f32[32,8,1152]{2,1,0:T(8,128)S(1)}, u32[]{:S(2)}, u32[]{:S(2)}) async-start(f32[32,8,1152]{2,1,0:T(8,128)} %broadcast_in_dim.5), calls=%async_computation.2 | async-start | bytes 2359296 | tf_op jit(solution)/shard_map/columns/all_to_all | solution.py:299
  70.1 0.0 collective-permute-done.8
  70.1 0.0 copy-start.4
  70.1 0.8 copy-done.4
  70.9 0.5 collective-permute-done.7
  71.4 0.2 select_select_fusion.panel_ref
  71.6 4.2 %collective-permute-start.9 = (f32[256,512]{1,0:T(8,128)S(1)}, f32[256,512]{1,0:T(8,128)}, u32[]{:S(2)}, u32[]{:S(2)}) collective-permute-start(f32[256,512]{1,0:T(8,128)S(1)} %select_select_fusion.panel_ref), channel_id=1, source_target_pairs={{0,14},{5,3},{11,9},{16,30},{21,19},{27,25},{32,46},{37,35},{43,41... | collective-permute-start | bytes 1572872 | tf_op jit(solution)/shard_map/rowpanel/ppermute | solution.py:270
  75.8 2.1 %collective-permute-start.10 = (f32[256,512]{1,0:T(8,128)S(1)}, f32[256,512]{1,0:T(8,128)}, u32[]{:S(2)}, u32[]{:S(2)}) collective-permute-start(f32[256,512]{1,0:T(8,128)S(1)} %select_select_fusion.panel_ref), channel_id=1, source_target_pairs={{0,2},{5,7},{11,13},{16,18},{21,23},{27,29},{32,34},{37,39},{43,45... | collective-permute-start | bytes 1572872 | tf_op jit(solution)/shard_map/rowpanel/ppermute | solution.py:270
  77.9 9.8 %factor_first.1 = (f32[256,512]{1,0:T(8,128)S(1)}, f32[2,128]{1,0:T(2,128)S(1)}) custom-call(f32[256,896]{1,0:T(8,128)S(1)} %bitcast.18), custom_call_target="tpu_custom_call" | custom-call | flops 67108864 | bytes 41943040 | tf_op jit(solution)/shard_map/factor_first/pallas_call | solution.py:256
  87.6 0.0 copy-start.1
  87.6 0.8 copy-done.1
  88.4 0.0 collective-permute-done.9.back_ref
  88.4 1.5 %collective-permute-start.13 = (f32[256,512]{1,0:T(8,128)}, f32[256,512]{1,0:T(8,128)}, u32[]{:S(2)}, u32[]{:S(2)}) collective-permute-start(f32[256,512]{1,0:T(8,128)} %collective-permute-done.9.back_ref), channel_id=1, source_target_pairs={{9,8},{25,24},{41,40},{57,56},{73,72},{89,88},{105,104},{121,120},... | collective-permute-start | bytes 1572872 | tf_op jit(solution)/shard_map/rowpanel/ppermute | solution.py:270
  89.9 0.0 all-to-all-done.2
  89.9 3.6 %collective-permute-start.12 = (f32[256,512]{1,0:T(8,128)S(1)}, f32[256,512]{1,0:T(8,128)}, u32[]{:S(2)}, u32[]{:S(2)}) collective-permute-start(f32[256,512]{1,0:T(8,128)S(1)} %select_select_fusion.panel_ref), channel_id=1, source_target_pairs={{0,15},{5,4},{11,10},{16,31},{21,20},{27,26},{32,47},{37,36},{43,4... | collective-permute-start | bytes 1572872 | tf_op jit(solution)/shard_map/rowpanel/ppermute | solution.py:270
  93.5 2.1 %collective-permute-start.11 = (f32[256,512]{1,0:T(8,128)S(1)}, f32[256,512]{1,0:T(8,128)}, u32[]{:S(2)}, u32[]{:S(2)}) collective-permute-start(f32[256,512]{1,0:T(8,128)S(1)} %select_select_fusion.panel_ref), channel_id=1, source_target_pairs={{0,1},{5,6},{11,12},{16,17},{21,22},{27,28},{32,33},{37,38},{43,44... | collective-permute-start | bytes 1572872 | tf_op jit(solution)/shard_map/rowpanel/ppermute | solution.py:270
  95.6 0.1 pad_add_fusion.ids_ref
  95.6 1.0 copy-done.2
  96.7 11.9 %factor_second.1 = (f32[256,512]{1,0:T(8,128)S(1)}, f32[256,512]{1,0:T(8,128)S(1)}, f32[2,128]{1,0:T(2,128)S(1)}) custom-call(f32[256,896]{1,0:T(8,128)S(1)} %bitcast.19, f32[256,512]{1,0:T(8,128)S(1)} %copy-done.2), custom_call_target="tpu_custom_call" | custom-call | flops 67108864 | bytes 41943040 | tf_op jit(solution)/shard_map/factor_second/pallas_call | solution.py:256
  108.6 0.0 collective-permute-done.10.ahead_ref
  108.6 0.0 collective-permute-done.13.rest_ref
  108.7 0.0 collective-permute-done.12.prior_ref
  108.7 0.0 collective-permute-done.11.next_ref
  108.7 3.8 %finish.1 = (f32[256,512]{1,0:T(8,128)}, f32[64,256]{1,0:T(8,128)}, f32[1,64]{1,0:T(1,128)}) custom-call(s32[3]{0:T(128)S(1)} %pad_add_fusion.ids_ref, f32[256,512]{1,0:T(8,128)S(1)} %select_select_fusion.panel_ref, f32[256,512]{1,0:T(8,128)} %collective-permute-done.9.back_ref, f32[256,512]{1,0:T(8,128)} %collective-permute-done.10.ahead_ref, ...), custom_call_target="tpu_custom_call" | custom-call | flops 67108864 | bytes 41943040 | tf_op jit(solution)/shard_map/finish/pallas_call | solution.py:256
  (14 shorter events, 0.1 us)
Async XLA Ops:
  0.6 39.1 %copy-start.3 = (f32[64,256]{1,0:T(8,128)S(1)}, f32[64,256]{1,0:T(8,128)}, u32[]{:S(2)}) copy-start(f32[64,256]{1,0:T(8,128)} %obs_ref.1) | copy-start | bytes 196612
  22.9 9.2 %collective-permute-start = (f32[8,768]{1,0:T(8,128)S(1)}, f32[8,768]{1,0:T(8,128)S(1)}, u32[]{:S(2)}, u32[]{:S(2)}) collective-permute-start(f32[8,768]{1,0:T(8,128)S(1)} %pad_maximum_fusion.1), channel_id=1, source_target_pairs={{0,5},{16,21},{32,37},{48,53},{64,69},{80,85},{96,101},{112,117},{... | collective-permute-start | bytes 73736 | tf_op jit(solution)/shard_map/diag/ppermute | solution.py:270
  32.0 6.3 %collective-permute-start.1 = (f32[8,768]{1,0:T(8,128)S(1)}, f32[8,768]{1,0:T(8,128)S(1)}, u32[]{:S(2)}, u32[]{:S(2)}) collective-permute-start(f32[8,768]{1,0:T(8,128)S(1)} %pad_maximum_fusion.1), channel_id=1, source_target_pairs={{0,11},{16,27},{32,43},{48,59},{64,75},{80,91},{96,107},{112,123},... | collective-permute-start | bytes 73736 | tf_op jit(solution)/shard_map/diag/ppermute | solution.py:270
  35.8 4.1 %collective-permute-start.5 = (f32[8,768]{1,0:T(8,128)S(1)}, f32[8,768]{1,0:T(8,128)S(1)}, u32[]{:S(2)}, u32[]{:S(2)}) collective-permute-start(f32[8,768]{1,0:T(8,128)S(1)} %broadcast_select_fusion), channel_id=1, source_target_pairs={{0,14},{5,3},{16,30},{21,19},{32,46},{37,35},{48,62},{53,51},{64,7... | collective-permute-start | bytes 73736 | tf_op jit(solution)/shard_map/diag/ppermute | solution.py:270
  37.1 2.8 %collective-permute-start.4 = (f32[8,768]{1,0:T(8,128)S(1)}, f32[8,768]{1,0:T(8,128)S(1)}, u32[]{:S(2)}, u32[]{:S(2)}) collective-permute-start(f32[8,768]{1,0:T(8,128)S(1)} %broadcast_select_fusion), channel_id=1, source_target_pairs={{0,2},{5,7},{16,18},{21,23},{32,34},{37,39},{48,50},{53,55},{64,66... | collective-permute-start | bytes 73736 | tf_op jit(solution)/shard_map/diag/ppermute | solution.py:270
  38.4 1.5 %collective-permute-start.3 = (f32[8,768]{1,0:T(8,128)S(1)}, f32[8,768]{1,0:T(8,128)S(1)}, u32[]{:S(2)}, u32[]{:S(2)}) collective-permute-start(f32[8,768]{1,0:T(8,128)S(1)} %broadcast_select_fusion.1), channel_id=1, source_target_pairs={{11,9},{27,25},{43,41},{59,57},{75,73},{91,89},{107,105},{123,121}... | collective-permute-start | bytes 73736 | tf_op jit(solution)/shard_map/diag/ppermute | solution.py:270
  39.0 0.8 collective-permute-start.2
  39.9 2.2 %collective-permute-start.6 = (f32[8,768]{1,0:T(8,128)S(1)}, f32[8,768]{1,0:T(8,128)S(1)}, u32[]{:S(2)}, u32[]{:S(2)}) collective-permute-start(f32[8,768]{1,0:T(8,128)S(1)} %select_select_fusion.1), channel_id=1, source_target_pairs={{0,1},{3,4},{5,6},{7,8},{9,10},{11,12},{14,15},{16,17},{19,20},{21... | collective-permute-start | bytes 73736 | tf_op jit(solution)/shard_map/diag/ppermute | solution.py:270
  43.2 5.0 %copy-start = (f32[256,512]{1,0:T(8,128)S(1)}, f32[256,512]{1,0:T(8,128)}, u32[]{:S(2)}) copy-start(f32[256,512]{1,0:T(8,128)} %cov_ref.1) | copy-start | bytes 1572868
  43.2 20.9 %all-to-all-start.1 = ((f32[32,8,896]{2,1,0:T(8,128)}), f32[32,8,896]{2,1,0:T(8,128)S(1)}, u32[]{:S(2)}, u32[]{:S(2)}) async-start(f32[32,8,896]{2,1,0:T(8,128)} %pad_maximum_fusion), calls=%async_computation.1 | async-start | bytes 1835008 | tf_op jit(solution)/shard_map/diag/all_to_all | solution.py:299
  48.2 21.9 %collective-permute-start.8 = (f32[256,512]{1,0:T(8,128)S(1)}, f32[256,512]{1,0:T(8,128)S(1)}, u32[]{:S(2)}, u32[]{:S(2)}) collective-permute-start(f32[256,512]{1,0:T(8,128)S(1)} %copy-done), channel_id=1, source_target_pairs={{0,5},{16,21},{32,37},{48,53},{64,69},{80,85},{96,101},{112,117},{... | collective-permute-start | bytes 1572872 | tf_op jit(solution)/shard_map/rowpanel/ppermute | solution.py:270
  54.5 16.9 %collective-permute-start.7 = (f32[256,512]{1,0:T(8,128)S(1)}, f32[256,512]{1,0:T(8,128)}, u32[]{:S(2)}, u32[]{:S(2)}) collective-permute-start(f32[256,512]{1,0:T(8,128)S(1)} %copy-done), channel_id=1, source_target_pairs={{0,11},{16,27},{32,43},{48,59},{64,75},{80,91},{96,107},{112,123},... | collective-permute-start | bytes 1572872 | tf_op jit(solution)/shard_map/rowpanel/ppermute | solution.py:270
  65.3 24.6 %all-to-all-start.2 = ((f32[32,8,1152]{2,1,0:T(8,128)}), f32[32,8,1152]{2,1,0:T(8,128)S(1)}, u32[]{:S(2)}, u32[]{:S(2)}) async-start(f32[32,8,1152]{2,1,0:T(8,128)} %broadcast_in_dim.5), calls=%async_computation.2 | async-start | bytes 2359296 | tf_op jit(solution)/shard_map/columns/all_to_all | solution.py:299
  70.1 0.8 copy-start.4
  71.6 16.8 %collective-permute-start.9 = (f32[256,512]{1,0:T(8,128)S(1)}, f32[256,512]{1,0:T(8,128)}, u32[]{:S(2)}, u32[]{:S(2)}) collective-permute-start(f32[256,512]{1,0:T(8,128)S(1)} %select_select_fusion.panel_ref), channel_id=1, source_target_pairs={{0,14},{5,3},{11,9},{16,30},{21,19},{27,25},{32,46},{37,35},{43,41... | collective-permute-start | bytes 1572872 | tf_op jit(solution)/shard_map/rowpanel/ppermute | solution.py:270
  75.8 32.9 %collective-permute-start.10 = (f32[256,512]{1,0:T(8,128)S(1)}, f32[256,512]{1,0:T(8,128)}, u32[]{:S(2)}, u32[]{:S(2)}) collective-permute-start(f32[256,512]{1,0:T(8,128)S(1)} %select_select_fusion.panel_ref), channel_id=1, source_target_pairs={{0,2},{5,7},{11,13},{16,18},{21,23},{27,29},{32,34},{37,39},{43,45... | collective-permute-start | bytes 1572872 | tf_op jit(solution)/shard_map/rowpanel/ppermute | solution.py:270
  87.6 0.8 copy-start.1
  88.4 20.2 %collective-permute-start.13 = (f32[256,512]{1,0:T(8,128)}, f32[256,512]{1,0:T(8,128)}, u32[]{:S(2)}, u32[]{:S(2)}) collective-permute-start(f32[256,512]{1,0:T(8,128)} %collective-permute-done.9.back_ref), channel_id=1, source_target_pairs={{9,8},{25,24},{41,40},{57,56},{73,72},{89,88},{105,104},{121,120},... | collective-permute-start | bytes 1572872 | tf_op jit(solution)/shard_map/rowpanel/ppermute | solution.py:270
  89.9 18.8 %collective-permute-start.12 = (f32[256,512]{1,0:T(8,128)S(1)}, f32[256,512]{1,0:T(8,128)}, u32[]{:S(2)}, u32[]{:S(2)}) collective-permute-start(f32[256,512]{1,0:T(8,128)S(1)} %select_select_fusion.panel_ref), channel_id=1, source_target_pairs={{0,15},{5,4},{11,10},{16,31},{21,20},{27,26},{32,47},{37,36},{43,4... | collective-permute-start | bytes 1572872 | tf_op jit(solution)/shard_map/rowpanel/ppermute | solution.py:270
  93.5 15.2 %collective-permute-start.11 = (f32[256,512]{1,0:T(8,128)S(1)}, f32[256,512]{1,0:T(8,128)}, u32[]{:S(2)}, u32[]{:S(2)}) collective-permute-start(f32[256,512]{1,0:T(8,128)S(1)} %select_select_fusion.panel_ref), channel_id=1, source_target_pairs={{0,1},{5,6},{11,12},{16,17},{21,22},{27,28},{32,33},{37,38},{43,44... | collective-permute-start | bytes 1572872 | tf_op jit(solution)/shard_map/rowpanel/ppermute | solution.py:270
  95.6 1.0 copy-start.2

commit v10 on v9

--- a/solution.py
+++ b/solution.py
@@ -186,7 +186,7 @@
 
 
 def finish_kernel(
-    ids_ref, panel_ref, back_ref, ahead_ref, next_ref, prior_ref, rest_ref, wide_ref, both0_ref, diag0_ref, low1_ref, inv1_ref,
+    ids_ref, panel_ref, ahead_ref, next_ref, rest_ref, wide_ref, both0_ref, diag0_ref, low1_ref, inv1_ref,
     diag1_ref, cov_ref, obs_ref, out_ref, solved_ref, site_ref, rows_here,
 ):
     tile, wide = cov_ref.shape
@@ -196,7 +196,7 @@
     inv10 = inv1_ref[:, :tile]
     inv11 = inv1_ref[:, tile:]
 
-    for place, ref in enumerate([panel_ref, back_ref, ahead_ref, next_ref, prior_ref, rest_ref]):
+    for place, ref in enumerate([panel_ref, ahead_ref, next_ref, rest_ref]):
         @pl.when(source == place)
         def _(ref=ref):
             rows_here[...] = ref[...]
@@ -335,7 +335,8 @@
 
     with jax.named_scope("rowpanel"):
         panel, holders = spread_step(panel, (5, -5), [0], cols, col)
-        sends = [send(panel, hop, holders, cols) for hop in (-2, 2)]
+        ahead = send(panel, 2, holders, cols)
+        panel, holders = spread_step(panel, (-2,), holders, cols, col)
 
     square = (LANES, LANES)
     both0, diag0 = call(
@@ -343,11 +344,12 @@
     )
     both0, panel, columns = lax.optimization_barrier((both0, panel, columns))
     with jax.named_scope("rowpanel"):
-        sends += [send(panel, hop, holders, cols) for hop in (1, -1)]
-        back, backs = sends[0]
-        covered = set(holders).union(*[targets for _, targets in sends])
-        rest = [z for z in backs if (z - 1) % cols not in covered]
-        sends.append(send(back, -1, rest, cols))
+        covered = set(holders) | set(ahead[1])
+        after = [z for z in holders if (z + 1) % cols not in covered]
+        sends = [ahead, send(panel, 1, after, cols)]
+        covered |= set(sends[1][1])
+        rest = [z for z in holders if (z - 1) % cols not in covered]
+        sends.append(send(panel, -1, rest, cols))
     low1, inv1, diag1 = call(
         second_kernel, "factor_second", [(tile, wide), (tile, wide), (tile // LANES, LANES)],
         [(tile, tile)] * 3 + [square] * 2, diag, both0,

time: 114 us -> 114 us (level)
  the two profiles are of different devices: /device:TPU:1 before, /device:TPU:99 now
where the time goes in v10:
time: 114 us
  waiting for transfers between devices  29.6 us (26%)
  Pallas kernels  29 us (25%)
  starting transfers between devices  28.8 us (25%)
  blocking collectives  18.8 us (16%)
  local copies, waits for them, and re-layouts  3.2 us (3%)
  other arithmetic  3.2 us (3%)
    pallas_call x3, Pallas kernels, call(): pl.pallas_call(kernel, out_shape=[jax.ShapeDtypeStruct(shape, jnp.float32...  29 us
    all_to_all x1, blocking collectives, exchange(): return lax.all_to_all(value, 'row', split_axis=0, concat_axis=0, tiled=True)  18.8 us
    ppermute x13, waiting for transfers between devices, send(): return (lax.ppermute(value, 'col', pairs), [target for _, target in pairs])  16.9 us
    ppermute x13, starting transfers between devices, send(): return (lax.ppermute(value, 'col', pairs), [target for _, target in pairs])  16.3 us
    all_to_all x2, waiting for transfers between devices, exchange(): return lax.all_to_all(value, 'row', split_axis=0, concat_axis=0, tiled=True)  12.7 us
    all_to_all x2, starting transfers between devices, exchange(): return lax.all_to_all(value, 'row', split_axis=0, concat_axis=0, tiled=True)  12.6 us
  transfers between devices with their start and end apart: 15, of which 4 were waited for; matrix products, arithmetic and copies ran while one was open for 3% of the time, Pallas kernels for 19%

profile of v10, /device:TPU:99, one launch (start us, length us, event | category | flops | bytes accessed | tf_op | source)
XLA Modules:
  0.0 113.6 jit_solution(5757009954614624689)
XLA Ops:
  0.6 0.0 copy-start.3
  0.6 18.8 %all_to_all.15 = f32[32,8,512]{2,1,0:T(8,128)S(1)} all-to-all(f32[32,8,512]{2,1,0:T(8,128)} %bitcast.21), channel_id=1, replica_groups=mesh['row'=32,'col'=16] {'row'}, dimensions={0} | all-to-all | bytes 1048576 | tf_op jit(solution)/shard_map/scatter/all_to_all | solution.py:299
  19.4 0.7 collective-permute-start
  20.1 0.0 collective-permute-done
  20.1 0.7 collective-permute-start.1
  20.8 1.3 %collective-permute-start.5 = (f32[8,768]{1,0:T(8,128)S(1)}, f32[8,768]{1,0:T(8,128)S(1)}, u32[]{:S(2)}, u32[]{:S(2)}) collective-permute-start(f32[8,768]{1,0:T(8,128)S(1)} %broadcast_select_fusion.1), channel_id=1, source_target_pairs={{0,14},{5,3},{16,30},{21,19},{32,46},{37,35},{48,62},{53,51},{64,7... | collective-permute-start | bytes 73736 | tf_op jit(solution)/shard_map/diag/ppermute | solution.py:270
  22.1 0.7 collective-permute-start.4
  22.8 0.0 collective-permute-done.1
  22.8 0.7 collective-permute-start.3
  23.5 0.7 collective-permute-start.2
  24.2 0.0 copy-done.3
  24.2 0.1 copy.6
  24.3 11.9 %collective-permute-done.5 = f32[8,768]{1,0:T(8,128)S(1)} collective-permute-done((f32[8,768]{1,0:T(8,128)S(1)}, f32[8,768]{1,0:T(8,128)S(1)}, u32[]{:S(2)}, u32[]{:S(2)}) %collective-permute-start.5) | collective-permute-done | bytes 24608 | tf_op jit(solution)/shard_map/diag/ppermute | solution.py:270
  36.2 0.0 collective-permute-done.4
  36.2 0.0 collective-permute-done.3
  36.2 0.0 collective-permute-done.2
  36.2 1.3 %collective-permute-start.6 = (f32[8,768]{1,0:T(8,128)S(1)}, f32[8,768]{1,0:T(8,128)S(1)}, u32[]{:S(2)}, u32[]{:S(2)}) collective-permute-start(f32[8,768]{1,0:T(8,128)S(1)} %select_select_fusion.1), channel_id=1, source_target_pairs={{0,1},{3,4},{5,6},{7,8},{9,10},{11,12},{14,15},{16,17},{19,20},{21... | collective-permute-start | bytes 73736 | tf_op jit(solution)/shard_map/diag/ppermute | solution.py:270
  37.6 0.9 collective-permute-done.6
  38.4 0.1 broadcast_in_dim.4
  38.5 1.0 pad_maximum_fusion
  39.5 7.6 %all-to-all-start.1 = ((f32[32,8,896]{2,1,0:T(8,128)}), f32[32,8,896]{2,1,0:T(8,128)S(1)}, u32[]{:S(2)}, u32[]{:S(2)}) async-start(f32[32,8,896]{2,1,0:T(8,128)} %pad_maximum_fusion), calls=%async_computation.1 | async-start | bytes 1835008 | tf_op jit(solution)/shard_map/diag/all_to_all | solution.py:299
  47.1 0.0 copy-done
  47.1 0.7 collective-permute-start.8
  47.8 1.5 %collective-permute-start.7 = (f32[256,512]{1,0:T(8,128)S(1)}, f32[256,512]{1,0:T(8,128)}, u32[]{:S(2)}, u32[]{:S(2)}) collective-permute-start(f32[256,512]{1,0:T(8,128)S(1)} %copy-done), channel_id=1, source_target_pairs={{0,11},{16,27},{32,43},{48,59},{64,75},{80,91},{96,107},{112,123},... | collective-permute-start | bytes 1572872 | tf_op jit(solution)/shard_map/rowpanel/ppermute | solution.py:270
  49.3 12.7 %all-to-all-done.1 = f32[32,8,896]{2,1,0:T(8,128)S(1)} async-done(((f32[32,8,896]{2,1,0:T(8,128)}), f32[32,8,896]{2,1,0:T(8,128)S(1)}, u32[]{:S(2)}, u32[]{:S(2)}) %all-to-all-start.1) | async-done | bytes 917536 | tf_op jit(solution)/shard_map/diag/all_to_all | solution.py:299
  62.0 0.1 concatenate.11
  62.1 1.1 broadcast_in_dim.5
  63.2 5.0 %all-to-all-start.2 = ((f32[32,8,1152]{2,1,0:T(8,128)}), f32[32,8,1152]{2,1,0:T(8,128)S(1)}, u32[]{:S(2)}, u32[]{:S(2)}) async-start(f32[32,8,1152]{2,1,0:T(8,128)} %broadcast_in_dim.5), calls=%async_computation.2 | async-start | bytes 2359296 | tf_op jit(solution)/shard_map/columns/all_to_all | solution.py:299
  68.2 0.0 collective-permute-done.8
  68.2 0.0 collective-permute-done.7
  68.2 1.0 select_select_fusion
  69.2 1.3 %collective-permute-start.9 = (f32[256,512]{1,0:T(8,128)}, f32[256,512]{1,0:T(8,128)}, u32[]{:S(2)}, u32[]{:S(2)}) collective-permute-start(f32[256,512]{1,0:T(8,128)} %select_select_fusion), channel_id=1, source_target_pairs={{0,14},{5,3},{11,9},{16,30},{21,19},{27,25},{32,46},{37,35},{43,41... | collective-permute-start | bytes 1572872 | tf_op jit(solution)/shard_map/rowpanel/ppermute | solution.py:270
  70.4 1.5 %collective-permute-start.10 = (f32[256,512]{1,0:T(8,128)}, f32[256,512]{1,0:T(8,128)}, u32[]{:S(2)}, u32[]{:S(2)}) collective-permute-start(f32[256,512]{1,0:T(8,128)} %select_select_fusion), channel_id=1, source_target_pairs={{0,2},{5,7},{11,13},{16,18},{21,23},{27,29},{32,34},{37,39},{43,45... | collective-permute-start | bytes 1572872 | tf_op jit(solution)/shard_map/rowpanel/ppermute | solution.py:270
  71.9 9.8 %factor_first.1 = (f32[256,512]{1,0:T(8,128)S(1)}, f32[2,128]{1,0:T(2,128)S(1)}) custom-call(f32[256,896]{1,0:T(8,128)S(1)} %bitcast.18), custom_call_target="tpu_custom_call" | custom-call | flops 67108864 | bytes 41943040 | tf_op jit(solution)/shard_map/factor_first/pallas_call | solution.py:256
  81.7 0.0 copy-start.1
  81.7 0.8 copy-done.1
  82.5 4.1 %collective-permute-done.9 = f32[256,512]{1,0:T(8,128)} collective-permute-done((f32[256,512]{1,0:T(8,128)}, f32[256,512]{1,0:T(8,128)}, u32[]{:S(2)}, u32[]{:S(2)}) %collective-permute-start.9) | collective-permute-done | bytes 524320 | tf_op jit(solution)/shard_map/rowpanel/ppermute | solution.py:270
  86.6 1.1 broadcast_select_fusion.panel_ref
  87.7 0.0 all-to-all-done.2
  87.8 1.5 %collective-permute-start.12 = (f32[256,512]{1,0:T(8,128)S(1)}, f32[256,512]{1,0:T(8,128)}, u32[]{:S(2)}, u32[]{:S(2)}) collective-permute-start(f32[256,512]{1,0:T(8,128)S(1)} %broadcast_select_fusion.panel_ref), channel_id=1, source_target_pairs={{9,8},{25,24},{41,40},{57,56},{73,72},{89,88},{105,104},{121,120},... | collective-permute-start | bytes 1572872 | tf_op jit(solution)/shard_map/rowpanel/ppermute | solution.py:270
  89.2 4.0 %collective-permute-start.11 = (f32[256,512]{1,0:T(8,128)S(1)}, f32[256,512]{1,0:T(8,128)}, u32[]{:S(2)}, u32[]{:S(2)}) collective-permute-start(f32[256,512]{1,0:T(8,128)S(1)} %broadcast_select_fusion.panel_ref), channel_id=1, source_target_pairs={{0,1},{3,4},{5,6},{9,10},{11,12},{14,15},{16,17},{19,20},{21,22},{... | collective-permute-start | bytes 1572872 | tf_op jit(solution)/shard_map/rowpanel/ppermute | solution.py:270
  93.2 0.1 pad_add_fusion.ids_ref
  93.3 1.0 copy-done.2
  94.3 11.9 %factor_second.1 = (f32[256,512]{1,0:T(8,128)S(1)}, f32[256,512]{1,0:T(8,128)S(1)}, f32[2,128]{1,0:T(2,128)S(1)}) custom-call(f32[256,896]{1,0:T(8,128)S(1)} %bitcast.19, f32[256,512]{1,0:T(8,128)S(1)} %copy-done.2), custom_call_target="tpu_custom_call" | custom-call | flops 67108864 | bytes 41943040 | tf_op jit(solution)/shard_map/factor_second/pallas_call | solution.py:256
  106.3 0.0 collective-permute-done.10.ahead_ref
  106.3 0.0 collective-permute-done.12.rest_ref
  106.3 0.0 collective-permute-done.11.next_ref
  106.3 7.3 %finish.1 = (f32[256,512]{1,0:T(8,128)}, f32[64,256]{1,0:T(8,128)}, f32[1,64]{1,0:T(1,128)}) custom-call(s32[3]{0:T(128)S(1)} %pad_add_fusion.ids_ref, f32[256,512]{1,0:T(8,128)S(1)} %broadcast_select_fusion.panel_ref, f32[256,512]{1,0:T(8,128)} %collective-permute-done.10.ahead_ref, f32[256,512]{1,0:T(8,128)} %collective-permute-done.11.next_ref, ...), custom_call_target="tpu_custom_call" | custom-call | flops 67108864 | bytes 41943040 | tf_op jit(solution)/shard_map/finish/pallas_call | solution.py:256
  (11 shorter events, 0.1 us)
Async XLA Ops:
  0.6 23.5 %copy-start.3 = (f32[64,256]{1,0:T(8,128)S(1)}, f32[64,256]{1,0:T(8,128)}, u32[]{:S(2)}) copy-start(f32[64,256]{1,0:T(8,128)} %obs_ref.1) | copy-start | bytes 196612
  19.4 0.7 collective-permute-start
  20.1 2.6 %collective-permute-start.1 = (f32[8,768]{1,0:T(8,128)S(1)}, f32[8,768]{1,0:T(8,128)S(1)}, u32[]{:S(2)}, u32[]{:S(2)}) collective-permute-start(f32[8,768]{1,0:T(8,128)S(1)} %pad_maximum_fusion.1), channel_id=1, source_target_pairs={{0,11},{16,27},{32,43},{48,59},{64,75},{80,91},{96,107},{112,123},... | collective-permute-start | bytes 73736 | tf_op jit(solution)/shard_map/diag/ppermute | solution.py:270
  20.8 15.4 %collective-permute-start.5 = (f32[8,768]{1,0:T(8,128)S(1)}, f32[8,768]{1,0:T(8,128)S(1)}, u32[]{:S(2)}, u32[]{:S(2)}) collective-permute-start(f32[8,768]{1,0:T(8,128)S(1)} %broadcast_select_fusion.1), channel_id=1, source_target_pairs={{0,14},{5,3},{16,30},{21,19},{32,46},{37,35},{48,62},{53,51},{64,7... | collective-permute-start | bytes 73736 | tf_op jit(solution)/shard_map/diag/ppermute | solution.py:270
  22.1 14.1 %collective-permute-start.4 = (f32[8,768]{1,0:T(8,128)S(1)}, f32[8,768]{1,0:T(8,128)S(1)}, u32[]{:S(2)}, u32[]{:S(2)}) collective-permute-start(f32[8,768]{1,0:T(8,128)S(1)} %broadcast_select_fusion.1), channel_id=1, source_target_pairs={{0,2},{5,7},{16,18},{21,23},{32,34},{37,39},{48,50},{53,55},{64,66... | collective-permute-start | bytes 73736 | tf_op jit(solution)/shard_map/diag/ppermute | solution.py:270
  22.8 13.4 %collective-permute-start.3 = (f32[8,768]{1,0:T(8,128)S(1)}, f32[8,768]{1,0:T(8,128)S(1)}, u32[]{:S(2)}, u32[]{:S(2)}) collective-permute-start(f32[8,768]{1,0:T(8,128)S(1)} %broadcast_select_fusion.2), channel_id=1, source_target_pairs={{11,9},{27,25},{43,41},{59,57},{75,73},{91,89},{107,105},{123,121}... | collective-permute-start | bytes 73736 | tf_op jit(solution)/shard_map/diag/ppermute | solution.py:270
  23.5 12.7 %collective-permute-start.2 = (f32[8,768]{1,0:T(8,128)S(1)}, f32[8,768]{1,0:T(8,128)S(1)}, u32[]{:S(2)}, u32[]{:S(2)}) collective-permute-start(f32[8,768]{1,0:T(8,128)S(1)} %broadcast_select_fusion.2), channel_id=1, source_target_pairs={{11,13},{27,29},{43,45},{59,61},{75,77},{91,93},{107,109},{123,125... | collective-permute-start | bytes 73736 | tf_op jit(solution)/shard_map/diag/ppermute | solution.py:270
  36.2 2.2 %collective-permute-start.6 = (f32[8,768]{1,0:T(8,128)S(1)}, f32[8,768]{1,0:T(8,128)S(1)}, u32[]{:S(2)}, u32[]{:S(2)}) collective-permute-start(f32[8,768]{1,0:T(8,128)S(1)} %select_select_fusion.1), channel_id=1, source_target_pairs={{0,1},{3,4},{5,6},{7,8},{9,10},{11,12},{14,15},{16,17},{19,20},{21... | collective-permute-start | bytes 73736 | tf_op jit(solution)/shard_map/diag/ppermute | solution.py:270
  39.5 7.6 %copy-start = (f32[256,512]{1,0:T(8,128)S(1)}, f32[256,512]{1,0:T(8,128)}, u32[]{:S(2)}) copy-start(f32[256,512]{1,0:T(8,128)} %cov_ref.1) | copy-start | bytes 1572868
  39.5 22.5 %all-to-all-start.1 = ((f32[32,8,896]{2,1,0:T(8,128)}), f32[32,8,896]{2,1,0:T(8,128)S(1)}, u32[]{:S(2)}, u32[]{:S(2)}) async-start(f32[32,8,896]{2,1,0:T(8,128)} %pad_maximum_fusion), calls=%async_computation.1 | async-start | bytes 1835008 | tf_op jit(solution)/shard_map/diag/all_to_all | solution.py:299
  47.1 21.1 %collective-permute-start.8 = (f32[256,512]{1,0:T(8,128)S(1)}, f32[256,512]{1,0:T(8,128)S(1)}, u32[]{:S(2)}, u32[]{:S(2)}) collective-permute-start(f32[256,512]{1,0:T(8,128)S(1)} %copy-done), channel_id=1, source_target_pairs={{0,5},{16,21},{32,37},{48,53},{64,69},{80,85},{96,101},{112,117},{... | collective-permute-start | bytes 1572872 | tf_op jit(solution)/shard_map/rowpanel/ppermute | solution.py:270
  47.8 20.4 %collective-permute-start.7 = (f32[256,512]{1,0:T(8,128)S(1)}, f32[256,512]{1,0:T(8,128)}, u32[]{:S(2)}, u32[]{:S(2)}) collective-permute-start(f32[256,512]{1,0:T(8,128)S(1)} %copy-done), channel_id=1, source_target_pairs={{0,11},{16,27},{32,43},{48,59},{64,75},{80,91},{96,107},{112,123},... | collective-permute-start | bytes 1572872 | tf_op jit(solution)/shard_map/rowpanel/ppermute | solution.py:270
  63.2 24.5 %all-to-all-start.2 = ((f32[32,8,1152]{2,1,0:T(8,128)}), f32[32,8,1152]{2,1,0:T(8,128)S(1)}, u32[]{:S(2)}, u32[]{:S(2)}) async-start(f32[32,8,1152]{2,1,0:T(8,128)} %broadcast_in_dim.5), calls=%async_computation.2 | async-start | bytes 2359296 | tf_op jit(solution)/shard_map/columns/all_to_all | solution.py:299
  69.2 17.5 %collective-permute-start.9 = (f32[256,512]{1,0:T(8,128)}, f32[256,512]{1,0:T(8,128)}, u32[]{:S(2)}, u32[]{:S(2)}) collective-permute-start(f32[256,512]{1,0:T(8,128)} %select_select_fusion), channel_id=1, source_target_pairs={{0,14},{5,3},{11,9},{16,30},{21,19},{27,25},{32,46},{37,35},{43,41... | collective-permute-start | bytes 1572872 | tf_op jit(solution)/shard_map/rowpanel/ppermute | solution.py:270
  70.4 35.8 %collective-permute-start.10 = (f32[256,512]{1,0:T(8,128)}, f32[256,512]{1,0:T(8,128)}, u32[]{:S(2)}, u32[]{:S(2)}) collective-permute-start(f32[256,512]{1,0:T(8,128)} %select_select_fusion), channel_id=1, source_target_pairs={{0,2},{5,7},{11,13},{16,18},{21,23},{27,29},{32,34},{37,39},{43,45... | collective-permute-start | bytes 1572872 | tf_op jit(solution)/shard_map/rowpanel/ppermute | solution.py:270
  81.7 0.8 copy-start.1
  87.8 18.5 %collective-permute-start.12 = (f32[256,512]{1,0:T(8,128)S(1)}, f32[256,512]{1,0:T(8,128)}, u32[]{:S(2)}, u32[]{:S(2)}) collective-permute-start(f32[256,512]{1,0:T(8,128)S(1)} %broadcast_select_fusion.panel_ref), channel_id=1, source_target_pairs={{9,8},{25,24},{41,40},{57,56},{73,72},{89,88},{105,104},{121,120},... | collective-permute-start | bytes 1572872 | tf_op jit(solution)/shard_map/rowpanel/ppermute | solution.py:270
  89.2 17.1 %collective-permute-start.11 = (f32[256,512]{1,0:T(8,128)S(1)}, f32[256,512]{1,0:T(8,128)}, u32[]{:S(2)}, u32[]{:S(2)}) collective-permute-start(f32[256,512]{1,0:T(8,128)S(1)} %broadcast_select_fusion.panel_ref), channel_id=1, source_target_pairs={{0,1},{3,4},{5,6},{9,10},{11,12},{14,15},{16,17},{19,20},{21,22},{... | collective-permute-start | bytes 1572872 | tf_op jit(solution)/shard_map/rowpanel/ppermute | solution.py:270
  93.3 1.0 copy-start.2
